TPU v7x, 32 devices: a whole 2x2x4 slice. The times are simulated.
32 devices in a mesh: seq: 2 (over x), span: 16 (over z, y, core).
Axes of the slice: x: 2, y: 2, z: 4, core: 2. Of those that a mesh axis runs over, the one named last changes fastest.
Arguments:
- tokens: bfloat16 [4, 1024, 2048], P('seq', 'span'), may hold values from -6 to 6
- doc_lengths: int32 [4, 4], P('seq'), may hold values from 0 to 1024, as said below
- ln1_gain: bfloat16 [2048], P(('seq', 'span')), may hold values from 0.5 to 1.5
- ln1_shift: bfloat16 [2048], P(('seq', 'span')), may hold values from -1.25 to 1.25
- q_weight: bfloat16 [2048, 2048], P(('seq', 'span')), may hold values from -0.125 to 0.125
- q_bias: bfloat16 [2048], P(('seq', 'span')), may hold values from -3 to 3
- kv_weight: bfloat16 [2048, 256], P(('seq', 'span')), may hold values from -0.125 to 0.125
- v_bias: bfloat16 [128], P(('seq', 'span')), may hold values from -0.3125 to 0.3125
- o_weight: bfloat16 [2048, 2048], P(('seq', 'span')), may hold values from -2 to 2
- o_bias: bfloat16 [2048], P(('seq', 'span')), may hold values from -3 to 3
- ln2_gain: bfloat16 [2048], P(('seq', 'span')), may hold values from 0.5 to 1.5
- ln2_shift: bfloat16 [2048], P(('seq', 'span')), may hold values from -1.25 to 1.25
- fc_weight: bfloat16 [2048, 8192], P(('seq', 'span')), may hold values from -0.125 to 0.125
- fc_bias: bfloat16 [8192], P(('seq', 'span')), may hold values from -3 to 3
- proj_weight: bfloat16 [8192, 2048], P(('seq', 'span')), may hold values from -0.0625 to 0.0625
- proj_bias: bfloat16 [2048], P(('seq', 'span')), may hold values from -3 to 3
- cotangent: bfloat16 [4, 1024, 2048], P('seq', 'span'), may hold values from -6 to 6
Outputs:
- output: bfloat16 [4, 1024, 2048], P('seq', 'span')
- input_grad: float32 [4, 1024, 2048], P('seq', 'span')
- ln1_gain_grad: float32 [2048], P(('seq', 'span'))
- ln1_shift_grad: float32 [2048], P(('seq', 'span'))
- q_weight_grad: float32 [2048, 2048], P(('seq', 'span'))
- q_bias_grad: float32 [2048], P(('seq', 'span'))
- kv_weight_grad: float32 [2048, 256], P(('seq', 'span'))
- v_bias_grad: float32 [128], P(('seq', 'span'))
- o_weight_grad: float32 [2048, 2048], P(('seq', 'span'))
- o_bias_grad: float32 [2048], P(('seq', 'span'))
- ln2_gain_grad: float32 [2048], P(('seq', 'span'))
- ln2_shift_grad: float32 [2048], P(('seq', 'span'))
- fc_weight_grad: float32 [2048, 8192], P(('seq', 'span'))
- fc_bias_grad: float32 [8192], P(('seq', 'span'))
- proj_weight_grad: float32 [8192, 2048], P(('seq', 'span'))
- proj_bias_grad: float32 [2048], P(('seq', 'span'))
Inputs may be any that keep to these rules, and one draw needn't show every extreme that they name: `doc_lengths`: each row sums to 1024. In each group of 2 consecutive rows one row, drawn from the seed, is a single document: 1024 followed by zeros. Other rows may hold empty documents.
All inputs are finite; a program needn't handle non-finite values.
Results may differ from a plain program's by a relative error of at most 0.013.
Values may be sent and summed in bfloat16 or wider, within the bound.
No kernel may reach another device: no remote copies, remote signals or barrier semaphores. Data moves between devices by JAX's collectives and lax.ppermute only.
A program may use at most 448 MiB of HBM per device.

v0:
```python
import math

import jax
import jax.numpy as jnp
from jax import lax
from jax.sharding import PartitionSpec as P

HEADS = 16
HD = 128


EPS = 1e-05
GELU_C = 0.7978845608028654
MASKED = -1e30
FLOOR_MAX = -1e29


def layer_norm(values, gain, shift):
    center = values - jnp.mean(values, axis=-1, keepdims=True)
    spread = jnp.mean(center * center, axis=-1, keepdims=True)
    return center * lax.rsqrt(spread + EPS) * gain + shift


def gelu_tanh(values):
    return 0.5 * values * (1.0 + jnp.tanh(GELU_C * (values + 0.044715 * values * values * values)))


def doc_number(doc_ends, positions):
    return jnp.sum((positions[None, :, None] >= doc_ends[:, None, :]).astype(jnp.int32), axis=-1)


def masked_scores(queries, key_rows, query_pos, query_doc, doc_ends, key_start):
    count = key_rows.shape[1]
    scores = jnp.einsum(
        "sche,sre->schr", queries, key_rows, preferred_element_type=jnp.float32
    ) * HD ** (-0.5)
    key_pos = key_start + jnp.arange(count, dtype=jnp.int32)
    key_doc = doc_number(doc_ends, key_pos)
    visible = (key_pos[None, None, :] <= query_pos[None, :, None]) & (
        key_doc[:, None, :] == query_doc[:, :, None]
    )
    return jnp.where(visible[:, :, None, :], scores, MASKED)


def local_fold(step, initial, buffer):
    length = buffer.shape[1]
    block_rows = math.gcd(length, 512)

    def turn(index, carried):
        block_start = index * block_rows
        piece = lax.dynamic_slice_in_dim(buffer, block_start, block_rows, 1)
        return step(carried, piece, block_start)

    return lax.fori_loop(0, length // block_rows, turn, initial)


def local(
    tokens,
    doc_lengths,
    ln1_gain,
    ln1_shift,
    q_weight,
    q_bias,
    kv_weight,
    v_bias,
    o_weight,
    o_bias,
    ln2_gain,
    ln2_shift,
    fc_weight,
    fc_bias,
    proj_weight,
    proj_bias,
    cotangent,
):
    seqs_here, span_rows, width = tokens.shape
    row_count = seqs_here * span_rows
    gain_one, shift_one, query_w, query_b, pair_w, value_b, out_w, out_b = (
        lax.all_gather(ln1_gain, ("seq", "span"), axis=0, tiled=True),
        lax.all_gather(ln1_shift, ("seq", "span"), axis=0, tiled=True),
        lax.all_gather(q_weight, ("seq", "span"), axis=0, tiled=True),
        lax.all_gather(q_bias, ("seq", "span"), axis=0, tiled=True),
        lax.all_gather(kv_weight, ("seq", "span"), axis=0, tiled=True),
        lax.all_gather(v_bias, ("seq", "span"), axis=0, tiled=True),
        lax.all_gather(o_weight, ("seq", "span"), axis=0, tiled=True),
        lax.all_gather(o_bias, ("seq", "span"), axis=0, tiled=True),
    )
    gain_two, shift_two, up_w, up_b, down_w, down_b = (
        lax.all_gather(ln2_gain, ("seq", "span"), axis=0, tiled=True),
        lax.all_gather(ln2_shift, ("seq", "span"), axis=0, tiled=True),
        lax.all_gather(fc_weight, ("seq", "span"), axis=0, tiled=True),
        lax.all_gather(fc_bias, ("seq", "span"), axis=0, tiled=True),
        lax.all_gather(proj_weight, ("seq", "span"), axis=0, tiled=True),
        lax.all_gather(proj_bias, ("seq", "span"), axis=0, tiled=True),
    )
    span_index = lax.axis_index("span")
    query_pos = span_index * span_rows + jnp.arange(span_rows, dtype=jnp.int32)
    last_query = span_index * span_rows + span_rows - 1
    doc_ends = jnp.cumsum(doc_lengths, axis=1)
    query_doc = doc_number(doc_ends, query_pos)
    inputs_float = tokens.reshape(row_count, width).astype(jnp.float32)
    normed_one_f, norm_pull_one = jax.vjp(
        layer_norm, inputs_float, gain_one.astype(jnp.float32), shift_one.astype(jnp.float32)
    )
    normed_one = normed_one_f.astype(jnp.bfloat16)
    queries_flat = (
        jnp.dot(normed_one, query_w, preferred_element_type=jnp.float32)
        + query_b.astype(jnp.float32)
    ).astype(jnp.bfloat16)
    queries = queries_flat.reshape(seqs_here, span_rows, HEADS, HD)
    pair_shift = jnp.concatenate([jnp.zeros((HD,), jnp.float32), value_b.astype(jnp.float32)])
    pairs = (jnp.dot(normed_one, pair_w, preferred_element_type=jnp.float32) + pair_shift).astype(
        jnp.bfloat16
    )
    pairs_local = pairs.reshape(seqs_here, span_rows, 2 * HD)

    def lse_step(carried, piece, piece_start):

        def lse_compute(state_in):
            running, total = state_in
            scores = masked_scores(
                queries, piece[:, :, :HD], query_pos, query_doc, doc_ends, piece_start
            )
            fresh = jnp.maximum(running, jnp.max(scores, axis=-1))
            total = total * jnp.exp(running - fresh) + jnp.sum(
                jnp.exp(scores - fresh[..., None]), axis=-1
            )
            return (fresh, total)

        return lax.cond(piece_start <= last_query, lse_compute, lambda state_in: state_in, carried)

    def out_step(carried, piece, piece_start):

        def out_compute(summed):
            scores = masked_scores(
                queries, piece[:, :, :HD], query_pos, query_doc, doc_ends, piece_start
            )
            probs = jnp.exp(scores - log_total[..., None]).astype(jnp.bfloat16)
            return summed + jnp.einsum(
                "schr,sre->sche", probs, piece[:, :, HD:], preferred_element_type=jnp.float32
            )

        return lax.cond(piece_start <= last_query, out_compute, lambda summed: summed, carried)

    stat_shape = (seqs_here, span_rows, HEADS)
    lse_init = (jnp.full(stat_shape, FLOOR_MAX, jnp.float32), jnp.zeros(stat_shape, jnp.float32))
    out_init = jnp.zeros((seqs_here, span_rows, HEADS, HD), jnp.float32)
    kv_whole = lax.all_gather(pairs_local, "span", axis=1, tiled=True)
    running, total = local_fold(lse_step, lse_init, kv_whole)
    log_total = running + jnp.log(total)
    attn_float = local_fold(out_step, out_init, kv_whole)
    attn_low = attn_float.reshape(row_count, width).astype(jnp.bfloat16)
    resid = (
        inputs_float
        + jnp.dot(attn_low, out_w, preferred_element_type=jnp.float32)
        + out_b.astype(jnp.float32)
    )
    normed_two_f, norm_pull_two = jax.vjp(
        layer_norm, resid, gain_two.astype(jnp.float32), shift_two.astype(jnp.float32)
    )
    normed_two = normed_two_f.astype(jnp.bfloat16)
    pre_act = jnp.dot(normed_two, up_w, preferred_element_type=jnp.float32) + up_b.astype(
        jnp.float32
    )
    active_f, gelu_pull = jax.vjp(gelu_tanh, pre_act)
    activation = active_f.astype(jnp.bfloat16)
    output = (
        resid
        + jnp.dot(activation, down_w, preferred_element_type=jnp.float32)
        + down_b.astype(jnp.float32)
    ).astype(jnp.bfloat16)
    grad_out = cotangent.reshape(row_count, width)
    grad_down_w = jnp.einsum("tf,td->fd", activation, grad_out, preferred_element_type=jnp.float32)
    grad_down_b = jnp.sum(grad_out.astype(jnp.float32), axis=0)
    grad_active = jnp.einsum("td,fd->tf", grad_out, down_w, preferred_element_type=jnp.float32)
    grad_pre = gelu_pull(grad_active)[0].astype(jnp.bfloat16)
    grad_up_w = jnp.einsum("td,tf->df", normed_two, grad_pre, preferred_element_type=jnp.float32)
    grad_up_b = jnp.sum(grad_pre.astype(jnp.float32), axis=0)
    grad_normed_two = jnp.einsum("tf,df->td", grad_pre, up_w, preferred_element_type=jnp.float32)
    grad_resid_part, grad_gain_two, grad_shift_two = norm_pull_two(grad_normed_two)
    mlp_terms = (grad_gain_two, grad_shift_two, grad_up_w, grad_up_b, grad_down_w, grad_down_b)
    mlp_parts = (
        lax.psum_scatter(mlp_terms[0], ("seq", "span"), scatter_dimension=0, tiled=True),
        lax.psum_scatter(mlp_terms[1], ("seq", "span"), scatter_dimension=0, tiled=True),
        lax.psum_scatter(mlp_terms[2], ("seq", "span"), scatter_dimension=0, tiled=True),
        lax.psum_scatter(mlp_terms[3], ("seq", "span"), scatter_dimension=0, tiled=True),
        lax.psum_scatter(mlp_terms[4], ("seq", "span"), scatter_dimension=0, tiled=True),
        lax.psum_scatter(mlp_terms[5], ("seq", "span"), scatter_dimension=0, tiled=True),
    )
    grad_resid = grad_out.astype(jnp.float32) + grad_resid_part
    grad_proj = grad_resid.astype(jnp.bfloat16)
    grad_out_w = jnp.einsum("td,te->de", attn_low, grad_proj, preferred_element_type=jnp.float32)
    grad_out_b = jnp.sum(grad_proj.astype(jnp.float32), axis=0)
    grad_heads = jnp.einsum(
        "te,de->td", grad_proj, out_w, preferred_element_type=jnp.float32
    ).astype(jnp.bfloat16)
    grad_heads = grad_heads.reshape(seqs_here, span_rows, HEADS, HD)
    delta = jnp.sum(grad_heads.astype(jnp.float32) * attn_float, axis=-1)

    def back_step(carried, piece, piece_start):

        def back_compute(state_in):
            grad_query, grad_pairs = state_in
            key_rows = piece[:, :, :HD]
            value_rows = piece[:, :, HD:]
            scores = masked_scores(queries, key_rows, query_pos, query_doc, doc_ends, piece_start)
            probs = jnp.exp(scores - log_total[..., None])
            grad_values = jnp.einsum(
                "schr,sche->sre",
                probs.astype(jnp.bfloat16),
                grad_heads,
                preferred_element_type=jnp.float32,
            )
            grad_probs = jnp.einsum(
                "sche,sre->schr", grad_heads, value_rows, preferred_element_type=jnp.float32
            )
            grad_scores = (probs * (grad_probs - delta[..., None])).astype(jnp.bfloat16)
            grad_query = grad_query + jnp.einsum(
                "schr,sre->sche", grad_scores, key_rows, preferred_element_type=jnp.float32
            ) * HD ** (-0.5)
            grad_keys = jnp.einsum(
                "schr,sche->sre", grad_scores, queries, preferred_element_type=jnp.float32
            ) * HD ** (-0.5)
            update = jnp.concatenate([grad_keys, grad_values], axis=-1)
            current = lax.dynamic_slice_in_dim(grad_pairs, piece_start, piece.shape[1], 1)
            grad_pairs = lax.dynamic_update_slice_in_dim(
                grad_pairs, current + update, piece_start, 1
            )
            return (grad_query, grad_pairs)

        return lax.cond(piece_start <= last_query, back_compute, lambda state_in: state_in, carried)

    seq_length = span_rows * lax.axis_size("span")
    back_init = (
        jnp.zeros((seqs_here, span_rows, HEADS, HD), jnp.float32),
        jnp.zeros((seqs_here, seq_length, 2 * HD), jnp.float32),
    )
    grad_query, grad_pairs = local_fold(back_step, back_init, kv_whole)
    own_pairs = (
        lax.psum_scatter(grad_pairs, "span", scatter_dimension=1, tiled=True)
        .astype(jnp.bfloat16)
        .reshape(row_count, 2 * HD)
    )
    query_grad_low = grad_query.reshape(row_count, width).astype(jnp.bfloat16)
    grad_query_w = jnp.einsum(
        "td,te->de", normed_one, query_grad_low, preferred_element_type=jnp.float32
    )
    grad_query_b = jnp.sum(query_grad_low.astype(jnp.float32), axis=0)
    grad_pair_w = jnp.einsum("td,te->de", normed_one, own_pairs, preferred_element_type=jnp.float32)
    grad_value_b = jnp.sum(own_pairs[:, HD:].astype(jnp.float32), axis=0)
    grad_normed_one = jnp.einsum(
        "te,de->td", query_grad_low, query_w, preferred_element_type=jnp.float32
    ) + jnp.einsum("te,de->td", own_pairs, pair_w, preferred_element_type=jnp.float32)
    grad_input_part, grad_gain_one, grad_shift_one = norm_pull_one(grad_normed_one)
    input_grad = grad_resid + grad_input_part
    attn_terms = (
        grad_gain_one,
        grad_shift_one,
        grad_query_w,
        grad_query_b,
        grad_pair_w,
        grad_value_b,
        grad_out_w,
        grad_out_b,
    )
    attn_parts = (
        lax.psum_scatter(attn_terms[0], ("seq", "span"), scatter_dimension=0, tiled=True),
        lax.psum_scatter(attn_terms[1], ("seq", "span"), scatter_dimension=0, tiled=True),
        lax.psum_scatter(attn_terms[2], ("seq", "span"), scatter_dimension=0, tiled=True),
        lax.psum_scatter(attn_terms[3], ("seq", "span"), scatter_dimension=0, tiled=True),
        lax.psum_scatter(attn_terms[4], ("seq", "span"), scatter_dimension=0, tiled=True),
        lax.psum_scatter(attn_terms[5], ("seq", "span"), scatter_dimension=0, tiled=True),
        lax.psum_scatter(attn_terms[6], ("seq", "span"), scatter_dimension=0, tiled=True),
        lax.psum_scatter(attn_terms[7], ("seq", "span"), scatter_dimension=0, tiled=True),
    )
    return (
        output.reshape(seqs_here, span_rows, width),
        input_grad.reshape(seqs_here, span_rows, width),
        attn_parts[0],
        attn_parts[1],
        attn_parts[2],
        attn_parts[3],
        attn_parts[4],
        attn_parts[5],
        attn_parts[6],
        attn_parts[7],
        mlp_parts[0],
        mlp_parts[1],
        mlp_parts[2],
        mlp_parts[3],
        mlp_parts[4],
        mlp_parts[5],
    )


def solution(mesh):
    return jax.shard_map(
        local,
        mesh=mesh,
        in_specs=(
            P("seq", "span", None),
            P("seq", None),
            P(("seq", "span")),
            P(("seq", "span")),
            P(("seq", "span"), None),
            P(("seq", "span")),
            P(("seq", "span"), None),
            P(("seq", "span")),
            P(("seq", "span"), None),
            P(("seq", "span")),
            P(("seq", "span")),
            P(("seq", "span")),
            P(("seq", "span"), None),
            P(("seq", "span")),
            P(("seq", "span"), None),
            P(("seq", "span")),
            P("seq", "span", None),
        ),
        out_specs=(
            P("seq", "span", None),
            P("seq", "span", None),
            P(("seq", "span")),
            P(("seq", "span")),
            P(("seq", "span"), None),
            P(("seq", "span")),
            P(("seq", "span"), None),
            P(("seq", "span")),
            P(("seq", "span"), None),
            P(("seq", "span")),
            P(("seq", "span")),
            P(("seq", "span")),
            P(("seq", "span"), None),
            P(("seq", "span")),
            P(("seq", "span"), None),
            P(("seq", "span")),
        ),
        check_vma=False,
    )
```

profile of v0, /device:TPU:0, one launch (start us, length us, event | category | flops | bytes accessed | tf_op | source)
XLA Modules:
  0.0 2868.5 jit_solution(1356572202680756086)
XLA Ops:
  15.5 42.7 %all-reduce.19 = (bf16[2048]{0:T(1024)(128)(2,1)S(1)}, bf16[2048]{0:T(1024)(128)(2,1)S(1)}, bf16[2048]{0:T(1024)(128)(2,1)S(1)}, bf16[128]{0:T(256)(128)(2,1)S(1...) all-reduce(bf16[2048]{0:T(1024)(128)(2,1)S(1)} %dynamic-update-slic, ...), channel_id=1, replica_groups=mesh['seq'=2,'span'=16] {'seq','span'}, use_global_device_ids=true, to_apply=%add.5 | all-reduce | flops 14464 | bytes 57856
  58.3 1.2 convert_reduce_fusion.7
  59.6 1.3 multiply_reduce_fusion.6
  61.0 1.4 add_convert_fusion.2
  62.5 5.0 all-gather.8.cloned.1.call-done
  67.5 2.2 fusion.56
  71.7 39.9 %all-gather = bf16[32,1,256]{2,1,0:T(2,128)(2,1)S(1)} all-gather(bf16[1,1,256]{2,1,0:T(2,128)(2,1)S(1)} %reshape.356), channel_id=1, replica_groups=mesh['seq'=2,'span'=16] {'seq','span'}, dimensions={0}, use_global_device_ids=true | all-gather | bytes 16896 | tf_op jit(solution)/shard_map/all_gather | solution.py:92
  111.8 35.3 %all-gather.12.cloned.1.call-done = bf16[2048,2048]{1,0:T(8,128)(2,1)} async-done(((bf16[64,2048]{1,0:T(8,128)(2,1)}), bf16[2048,2048]{1,0:T(8,128)(2,1)}) %all-gather.12.cloned.1.call-update) | async-done | bytes 8388624 | tf_op jit(solution)/shard_map/all_gather | solution.py:81
  147.0 4.7 fusion.54
  152.0 34.4 %all-gather.10.cloned.1.call-done = bf16[2,1024,256]{2,1,0:T(8,128)(2,1)} async-done(((bf16[2,64,256]{2,1,0:T(8,128)(2,1)}), bf16[2,1024,256]{2,1,0:T(8,128)(2,1)}) %all-gather.10.cloned.1.call-update) | async-done | bytes 1048592 | tf_op jit(solution)/shard_map/all_gather | solution.py:148
  186.4 4.1 while.49
  186.9 3.6 conditional.9
  187.2 1.8 fusion.6
  189.0 1.4 exponential_reduce_fusion
  190.7 3.1 while.50
  190.7 3.0 conditional.10
  191.1 2.7 fusion.13
  194.7 71.0 %all-gather.14.cloned.1.call-done = bf16[2048,2048]{1,0:T(8,128)(2,1)} async-done(((bf16[64,2048]{1,0:T(8,128)(2,1)}), bf16[2048,2048]{1,0:T(8,128)(2,1)}) %all-gather.14.cloned.1.call-update) | async-done | bytes 8388624 | tf_op jit(solution)/shard_map/all_gather | solution.py:85
  265.6 5.0 fusion.78
  270.9 190.9 %all-gather.16.cloned.1.call-done = bf16[2048,8192]{1,0:T(8,128)(2,1)} async-done(((bf16[64,8192]{1,0:T(8,128)(2,1)}), bf16[2048,8192]{1,0:T(8,128)(2,1)}) %all-gather.16.cloned.1.call-update) | async-done | bytes 33554448 | tf_op jit(solution)/shard_map/all_gather | solution.py:91
  461.8 17.9 convolution_add_fusion
  479.7 177.8 %all-gather.18.cloned.1.call-done = bf16[8192,2048]{1,0:T(8,128)(2,1)} async-done(((bf16[256,2048]{1,0:T(8,128)(2,1)}), bf16[8192,2048]{1,0:T(8,128)(2,1)}) %all-gather.18.cloned.1.call-update) | async-done | bytes 33554448 | tf_op jit(solution)/shard_map/all_gather | solution.py:93
  657.5 20.8 convert_reduce_fusion.3
  678.3 19.6 multiply_reduce_fusion
  697.9 1.6 fusion.77
  700.5 1.9 convert_reduce_fusion.5
  702.4 6.5 fusion.55
  710.5 1.6 broadcast_in_dim.109
  712.1 13.9 while.51
  712.3 13.7 conditional.11
  712.3 3.6 fusion.38
  716.2 3.8 fusion.18
  720.0 2.5 fusion.30
  722.5 1.3 fusion.33
  724.7 1.3 copy-done.2
  726.0 3.0 copy.58
  729.8 1.1 add_convert_fusion
  732.4 7.2 fusion.60
  739.7 62.9 %reduce-scatter.7.cloned.1.call-done = f32[2,64,256]{2,1,0:T(8,128)} async-done(((f32[2,1024,256]{2,1,0:T(8,128)}), f32[2,64,256]{2,1,0:T(8,128)}) %reduce-scatter.7.cloned.1.call-update) | async-done | bytes 131088 | tf_op jit(solution)/shard_map/reduce_scatter | solution.py:240
  804.0 2.7 fusion.74
  806.7 1.1 multiply_reduce_fusion.1
  807.9 1.8 convolution_bitcast_fusion.1
  809.8 9.1 fusion.58
  819.9 9.1 fusion.62
  829.1 24.9 fusion.72
  854.1 1.0 copy-done.7
  855.1 25.5 fusion.73
  881.2 17.7 fusion.53
  899.0 1.5 add_add_fusion.2
  900.5 34.4 %all-reduce.22.cloned.1.call-done = (f32[2048]{0:T(1024)}, f32[2048]{0:T(1024)}, f32[2048]{0:T(1024)}, f32[128]{0:T(128)}, f32[2048]{0:T(1024)}, /*index=5*/f32[...) async-done(((f32[2048]{0:T(1024)}, f32[2048]{0:T(1024)}, f32[2048]{0:T(1024)}, f32[128]{0:T(128)}, f32[2048]{0:T(1024)}, /*index=5*/f32[2048]{0:T(1024)}, ...) | async-done | bytes 90640
  935.0 1.3 dynamic-slice
  936.2 1.3 dynamic-slice.1
  937.5 1.3 dynamic-slice.2
  938.7 1.3 dynamic-slice.4
  940.0 1.3 dynamic-slice.5
  941.3 1.3 dynamic-slice.6
  942.5 1.3 dynamic-slice.8
  943.8 1.2 dynamic-slice.3
  945.0 1.3 dynamic-slice.7
  946.3 129.3 %reduce-scatter.11.cloned.1.call-done = f32[64,256]{1,0:T(8,128)} async-done(((f32[2048,256]{1,0:T(8,128)}), f32[64,256]{1,0:T(8,128)}) %reduce-scatter.11.cloned.1.call-update) | async-done | bytes 65552 | tf_op jit(solution)/shard_map/reduce_scatter | solution.py:271
  1075.6 183.0 %reduce-scatter.9.cloned.1.call-done = f32[64,2048]{1,0:T(8,128)} async-done(((f32[2048,2048]{1,0:T(8,128)}), f32[64,2048]{1,0:T(8,128)}) %reduce-scatter.9.cloned.1.call-update) | async-done | bytes 524304 | tf_op jit(solution)/shard_map/reduce_scatter | solution.py:269
  1258.6 187.6 %reduce-scatter.13.cloned.1.call-done = f32[64,2048]{1,0:T(8,128)} async-done(((f32[2048,2048]{1,0:T(8,128)}), f32[64,2048]{1,0:T(8,128)}) %reduce-scatter.13.cloned.1.call-update) | async-done | bytes 524304 | tf_op jit(solution)/shard_map/reduce_scatter | solution.py:273
  1446.2 706.3 %reduce-scatter.15.cloned.1.call-done = f32[64,8192]{1,0:T(8,128)} async-done(((f32[2048,8192]{1,0:T(8,128)}), f32[64,8192]{1,0:T(8,128)}) %reduce-scatter.15.cloned.1.call-update) | async-done | bytes 2097168 | tf_op jit(solution)/shard_map/reduce_scatter | solution.py:185
  2152.6 708.9 %reduce-scatter.17.cloned.1.call-done = f32[256,2048]{1,0:T(8,128)} async-done(((f32[8192,2048]{1,0:T(8,128)}), f32[256,2048]{1,0:T(8,128)}) %reduce-scatter.17.cloned.1.call-update) | async-done | bytes 2097168 | tf_op jit(solution)/shard_map/reduce_scatter | solution.py:187
  (147 shorter events, 22.0 us)
Async XLA Ops:
  7.2 64.3 %copy-start.16 = (s32[2,4]{1,0:T(2,128)S(1)}, s32[2,4]{1,0:T(2,128)}, u32[]{:S(2)}) copy-start(s32[2,4]{1,0:T(2,128)} %param.30) | copy-start | bytes 100
  7.2 64.5 %copy-start.17 = (bf16[256]{0:T(256)(128)(2,1)S(1)}, bf16[256]{0:T(256)(128)(2,1)}, u32[]{:S(2)}) copy-start(bf16[256]{0:T(256)(128)(2,1)} %param.42) | copy-start | bytes 1540
  7.2 60.3 %all-gather.8.cloned.1.call-start = ((), (), s32[]{:S(2)}) async-start(), calls=%async_computation.6 | async-start | bytes 1081344 | tf_op jit(solution)/shard_map/all_gather | solution.py:83
  7.9 139.1 %all-gather.12.cloned.1.call-start = ((), (), s32[]{:S(2)}) async-start(), calls=%async_computation.8 | async-start | bytes 8650752 | tf_op jit(solution)/shard_map/all_gather | solution.py:81
  8.7 177.7 %all-gather.10.cloned.1.call-start = ((), (), s32[]{:S(2)}) async-start(), calls=%async_computation.7 | async-start | bytes 1114112 | tf_op jit(solution)/shard_map/all_gather | solution.py:148
  69.7 196.0 %all-gather.14.cloned.1.call-start = ((), (), s32[]{:S(2)}) async-start(), calls=%async_computation.9 | async-start | bytes 8650752 | tf_op jit(solution)/shard_map/all_gather | solution.py:85
  70.3 391.5 %all-gather.16.cloned.1.call-start = ((), (), s32[]{:S(2)}) async-start(), calls=%async_computation.10 | async-start | bytes 34603008 | tf_op jit(solution)/shard_map/all_gather | solution.py:91
  70.9 586.7 %all-gather.18.cloned.1.call-start = ((), (), s32[]{:S(2)}) async-start(), calls=%async_computation.11 | async-start | bytes 34603008 | tf_op jit(solution)/shard_map/all_gather | solution.py:93
  71.4 731.1 %reduce-scatter.7.cloned.1.call-start = ((), (), s32[]{:S(2)}) async-start(), calls=%async_computation.12 | async-start | bytes 2228224 | tf_op jit(solution)/shard_map/reduce_scatter | solution.py:240
  190.7 75.0 %copy-start.3 = (bf16[2,64,2048]{2,1,0:T(8,128)(2,1)S(1)}, bf16[2,64,2048]{2,1,0:T(8,128)(2,1)}, u32[]{:S(2)}) copy-start(bf16[2,64,2048]{2,1,0:T(8,128)(2,1)} %param.29) | copy-start | bytes 1572868
  699.6 1.0 copy-start.4
  699.6 9.3 copy-start.14
  702.4 6.5 copy-start.10
  716.2 6.3 copy-start.12
  720.0 2.5 copy-start
  722.5 1.9 copy-start.1
  724.7 1.3 copy-start.2
  726.0 3.1 copy-start.6
  729.0 205.9 %all-reduce.22.cloned.1.call-start = ((), (), s32[]{:S(2)}) async-start(), calls=%async_computation.18 | async-start | bytes 181248
  731.7 0.8 copy-start.11
  739.7 68.2 %copy-start.9 = (bf16[2,64,2048]{2,1,0:T(8,128)(2,1)S(1)}, bf16[2,64,2048]{2,1,0:T(8,128)(2,1)}, u32[]{:S(2)}) copy-start(bf16[2,64,2048]{2,1,0:T(8,128)(2,1)} %add_convert_fusion) | copy-start | bytes 1572868
  807.8 267.8 %reduce-scatter.11.cloned.1.call-start = ((), (), s32[]{:S(2)}) async-start(), calls=%async_computation.14 | async-start | bytes 2162688 | tf_op jit(solution)/shard_map/reduce_scatter | solution.py:271
  809.7 448.9 %reduce-scatter.9.cloned.1.call-start = ((), (), s32[]{:S(2)}) async-start(), calls=%async_computation.13 | async-start | bytes 17301504 | tf_op jit(solution)/shard_map/reduce_scatter | solution.py:269
  818.9 1.0 copy-start.8
  818.9 627.3 %reduce-scatter.13.cloned.1.call-start = ((), (), s32[]{:S(2)}) async-start(), calls=%async_computation.15 | async-start | bytes 17301504 | tf_op jit(solution)/shard_map/reduce_scatter | solution.py:273
  829.1 1323.5 %reduce-scatter.15.cloned.1.call-start = ((), (), s32[]{:S(2)}) async-start(), calls=%async_computation.16 | async-start | bytes 69206016 | tf_op jit(solution)/shard_map/reduce_scatter | solution.py:185
  854.1 1.0 copy-start.7
  854.1 2007.4 %reduce-scatter.17.cloned.1.call-start = ((), (), s32[]{:S(2)}) async-start(), calls=%async_computation.17 | async-start | bytes 69206016 | tf_op jit(solution)/shard_map/reduce_scatter | solution.py:187
  880.6 0.7 copy-start.13
  881.2 17.8 copy-start.5
  881.2 17.8 copy-start.15
Sparse Core Ops, SparseCore 0:
  10.9 56.5 all-gather.7
  70.4 76.6 all-gather.11
  149.8 36.5 all-gather.9
  189.1 76.4 all-gather.13
  268.4 193.3 all-gather.15
  464.5 192.9 all-gather.17
  729.1 73.3 reduce-scatter.6
  810.7 124.2 all-reduce.21
  937.8 137.7 reduce-scatter.10
  1078.5 180.1 reduce-scatter.8
  1261.6 184.5 reduce-scatter.12
  1449.1 703.3 reduce-scatter.14
  2155.6 705.8 reduce-scatter.16
where the time goes:
time: 2880 us; the launch traced here: 2870 us
  waiting for transfers between devices  2530 us (88%)
  matrix products  191 us (7%)
  blocking collectives  82.6 us (3%)
  local copies, waits for them, and re-layouts  29.9 us (1%)
    reduce_scatter x1, waiting for transfers between devices, local(): lax.psum_scatter(mlp_terms[4], ('seq', 'span'), scatter_dimension=0, tile...  709 us
    reduce_scatter x1, waiting for transfers between devices, local(): lax.psum_scatter(mlp_terms[2], ('seq', 'span'), scatter_dimension=0, tile...  706 us
    all_gather x1, waiting for transfers between devices, local(): lax.all_gather(fc_weight, ('seq', 'span'), axis=0, tiled=True)  191 us
    reduce_scatter x1, waiting for transfers between devices, local(): lax.psum_scatter(attn_terms[6], ('seq', 'span'), scatter_dimension=0, til...  188 us
    reduce_scatter x1, waiting for transfers between devices, local(): lax.psum_scatter(attn_terms[2], ('seq', 'span'), scatter_dimension=0, til...  183 us
    all_gather x1, waiting for transfers between devices, local(): lax.all_gather(proj_weight, ('seq', 'span'), axis=0, tiled=True)  178 us
    reduce_scatter x1, waiting for transfers between devices, local(): lax.psum_scatter(attn_terms[4], ('seq', 'span'), scatter_dimension=0, til...  129 us
    all_gather x1, waiting for transfers between devices, local(): lax.all_gather(o_weight, ('seq', 'span'), axis=0, tiled=True)  71 us
  transfers between devices with their start and end apart: 13, of which 13 were waited for; matrix products, arithmetic and copies ran while one was open for 6% of the time, Pallas kernels for 0%

commit v1 on v0

v1 whole, which is shorter than its diff:
```python
import math

import jax
import jax.numpy as jnp
from jax import lax
from jax.sharding import Mesh
from jax.sharding import PartitionSpec as P

HEADS = 16
HD = 128

EPS = 1e-05
GELU_C = 0.7978845608028654
MASKED = -1e30
FLOOR_MAX = -1e29
LOW = jnp.bfloat16
F32 = jnp.float32
SWAP = [(0, 1), (1, 0)]


def layer_norm(values, gain, shift):
    center = values - jnp.mean(values, axis=-1, keepdims=True)
    spread = jnp.mean(center * center, axis=-1, keepdims=True)
    return center * lax.rsqrt(spread + EPS) * gain + shift


def gelu_tanh(values):
    return 0.5 * values * (1.0 + jnp.tanh(GELU_C * (values + 0.044715 * values * values * values)))


def doc_number(doc_ends, positions):
    return jnp.sum((positions[None, :, None] >= doc_ends[:, None, :]).astype(jnp.int32), axis=-1)


def dot(left, right, dims=((1,), (0,))):
    return lax.dot_general(left, right, (dims, ((), ())), preferred_element_type=F32)


def swap(value, axis):
    return lax.ppermute(value, axis, SWAP)


def add_low(own, got):
    return (own.astype(F32) + got.astype(F32)).astype(LOW)


def in_order(own, got, axis, at=0):
    first = lax.axis_index(axis) == 0
    return jnp.stack([jnp.where(first, own, got), jnp.where(first, got, own)], axis=at)


def own_other(value, axis, at):
    index = lax.axis_index(axis)
    own = lax.dynamic_index_in_dim(value, index, at, keepdims=False)
    other = lax.dynamic_index_in_dim(value, 1 - index, at, keepdims=False)
    return own, other


def gather_two(value, axis, at=0):
    return in_order(value, swap(value, axis), axis, at)


def shift_z(value, by):
    count = lax.axis_size("z")
    return lax.ppermute(value, "z", [(i, (i + by) % count) for i in range(count)])


def gather_z(value, direct):
    count = lax.axis_size("z")
    me = lax.axis_index("z")
    held = [value]
    for step in range(1, count):
        held.append(shift_z(value, step) if direct else shift_z(held[-1], 1))
    held = jnp.stack(held)
    return jnp.stack(
        [lax.dynamic_index_in_dim(held, (me - a) % count, 0, keepdims=False) for a in range(count)]
    )


def scatter_z(value, low=True):
    count = lax.axis_size("z")
    me = lax.axis_index("z")

    def mine(step):
        return lax.dynamic_index_in_dim(value, (me - step) % count, 0, keepdims=False)

    running = mine(1)
    for step in range(2, count + 1):
        got = shift_z(running, 1)
        running = mine(step).astype(F32) + got.astype(F32)
        if step < count and low:
            running = running.astype(LOW)
    return running


def gather_chips(value):
    half = value.shape[1] // 2
    left = gather_z(value[:, :half], False)
    right = gather_z(value[:, half:], False)
    left = gather_two(gather_two(left, "x", 0), "y", 2)
    right = gather_two(gather_two(right, "y", 1), "x", 0)
    return jnp.concatenate([left, right], axis=-1)


def gather_rows(value):
    chips = gather_chips(value)
    whole = gather_two(chips, "c", 3)
    return whole.reshape(-1, value.shape[1])


def gather_rows_small(value):
    whole = gather_z(value, True)
    whole = gather_two(whole, "y", 1)
    whole = gather_two(whole, "x", 0)
    whole = gather_two(whole, "c", 3)
    return whole


def scatter_rows(value):
    count = lax.axis_size("z")
    width = value.shape[1]
    value = value.reshape(2, count, 2, 2, -1, width)
    own, other = own_other(value, "c", 3)
    value = add_low(own, swap(other, "c"))
    left, right = value[..., : width // 2], value[..., width // 2 :]
    own, other = own_other(left, "x", 0)
    left = add_low(own, swap(other, "x"))
    own, other = own_other(right, "y", 2)
    right = add_low(own, swap(other, "y"))
    own, other = own_other(left, "y", 1)
    left = add_low(own, swap(other, "y"))
    own, other = own_other(right, "x", 0)
    right = add_low(own, swap(other, "x"))
    return jnp.concatenate([scatter_z(left), scatter_z(right)], axis=-1)


def scatter_small(value):
    count = lax.axis_size("z")
    value = value.reshape(2, count, 2, 2, -1)
    for axis, at in (("c", 3), ("y", 2), ("x", 0)):
        own, other = own_other(value, axis, at)
        value = own + swap(other, axis)
    return scatter_z(value, False)


def spread_columns(value):
    own, other = own_other(value, "c", 3)
    value = gather_in(own, other, "c")
    own, other = own_other(value, "y", 3)
    value = gather_in(own, other, "y")
    own, other = own_other(value, "x", 3)
    return gather_in(own, other, "x")


def gather_in(own, other, axis):
    return in_order(own, swap(other, axis), axis)


def collect_columns(value):
    own, other = own_other(value, "x", 0)
    value = in_order(own, swap(other, "x"), "x", 3)
    own, other = own_other(value, "y", 0)
    value = in_order(own, swap(other, "y"), "y", 3)
    own, other = own_other(value, "c", 0)
    return in_order(own, swap(other, "c"), "c", 3)


def gather_plane(value):
    half = value.shape[0] // 2
    left, right = value[:half], value[half:]
    left_x, right_y = swap(left, "x"), swap(right, "y")
    left_two = jnp.concatenate([left, left_x])
    right_two = jnp.concatenate([right, right_y])
    four = jnp.concatenate([left_two, swap(left_two, "y"), right_two, swap(right_two, "x")])
    return jnp.concatenate([four, swap(four, "c")])


def scatter_plane(value):
    rows = value.shape[0] // 2
    four = add_low(value[:rows], swap(value[rows:], "c"))
    part = rows // 4
    left_own, left_far = four[:part], four[part : 2 * part]
    right_own, right_far = four[2 * part : 3 * part], four[3 * part :]
    left = add_low(left_own, swap(left_far, "y"))
    right = add_low(right_own, swap(right_far, "x"))
    half = part // 2
    left = left[:half].astype(F32) + swap(left[half:], "x").astype(F32)
    right = right[:half].astype(F32) + swap(right[half:], "y").astype(F32)
    return jnp.concatenate([left, right])


def masked_scores(queries, key_rows, query_pos, query_doc, doc_ends, key_start):
    count = key_rows.shape[1]
    scores = jnp.einsum(
        "sche,sre->schr", queries, key_rows, preferred_element_type=F32
    ) * HD ** (-0.5)
    key_pos = key_start + jnp.arange(count, dtype=jnp.int32)
    key_doc = doc_number(doc_ends, key_pos)
    visible = (key_pos[None, None, :] <= query_pos[None, :, None]) & (
        key_doc[:, None, :] == query_doc[:, :, None]
    )
    return jnp.where(visible[:, :, None, :], scores, MASKED)


def local_fold(step, initial, buffer):
    length = buffer.shape[1]
    block_rows = math.gcd(length, 512)

    def turn(index, carried):
        block_start = index * block_rows
        piece = lax.dynamic_slice_in_dim(buffer, block_start, block_rows, 1)
        return step(carried, piece, block_start)

    return lax.fori_loop(0, length // block_rows, turn, initial)


def local(
    tokens,
    doc_lengths,
    ln1_gain,
    ln1_shift,
    q_weight,
    q_bias,
    kv_weight,
    v_bias,
    o_weight,
    o_bias,
    ln2_gain,
    ln2_shift,
    fc_weight,
    fc_bias,
    proj_weight,
    proj_bias,
    cotangent,
):
    seqs_here, span_rows, width = tokens.shape
    row_count = seqs_here * span_rows
    planes = lax.axis_size("z")
    devices = 8 * planes
    rows = q_weight.shape[0]
    hidden = proj_weight.shape[0]
    span_size = 4 * planes
    at_x, at_z, at_y, at_c = (lax.axis_index(name) for name in ("x", "z", "y", "c"))
    span_index = at_z * 4 + at_y * 2 + at_c

    small = (ln1_gain, ln1_shift, q_bias, o_bias, ln2_gain, ln2_shift, proj_bias, fc_bias, v_bias)
    flat = jnp.concatenate(small)
    lanes = kv_weight.shape[1]
    flat = jnp.pad(flat, (0, -flat.shape[0] % (16 * lanes))).reshape(-1, lanes)
    packed = gather_rows_small(jnp.concatenate([kv_weight, flat]))
    pair_w = packed[..., :rows, :].reshape(width, lanes)
    flat = packed[..., rows:, :].reshape(devices, -1)
    parts, start = [], 0
    for piece in small:
        parts.append(flat[:, start : start + piece.shape[0]].reshape(-1).astype(F32))
        start += piece.shape[0]
    gain_one, shift_one, query_b, out_b, gain_two, shift_two, down_b, up_b, value_b = parts
    up_b = up_b.reshape(2, planes, 2, 2, hidden)
    up_b = lax.dynamic_slice(
        up_b, (at_x, 0, at_y, at_c, 0), (1, planes, 1, 1, hidden)
    ).reshape(-1)

    query_w = gather_rows(q_weight)
    out_w = gather_rows(o_weight)

    up_own = fc_weight.reshape(rows, 2, planes, 2, 2, hidden).transpose(0, 1, 3, 4, 2, 5)
    up_own = spread_columns(up_own.reshape(rows, 2, 2, 2, planes * hidden))
    up_own = up_own.reshape(2, 4 * rows, planes * hidden)
    up_w = lax.all_gather(up_own, "z", axis=1, tiled=True).reshape(width, planes * hidden)
    down_w = lax.all_gather(proj_weight, "z", axis=0, tiled=True)

    grad_out = cotangent.reshape(row_count, width)
    grad_out_plane = gather_plane(grad_out)

    query_pos = span_index * span_rows + jnp.arange(span_rows, dtype=jnp.int32)
    last_query = span_index * span_rows + span_rows - 1
    doc_ends = jnp.stack(
        [jnp.sum(doc_lengths[:, : j + 1], axis=1) for j in range(doc_lengths.shape[1])], axis=1
    )
    query_doc = doc_number(doc_ends, query_pos)
    inputs_float = tokens.reshape(row_count, width).astype(F32)
    normed_one_f, norm_pull_one = jax.vjp(layer_norm, inputs_float, gain_one, shift_one)
    normed_one = normed_one_f.astype(LOW)
    pair_shift = jnp.concatenate([jnp.zeros((HD,), F32), value_b])
    pairs = (dot(normed_one, pair_w) + pair_shift).astype(LOW)
    kv_whole = gather_z(pairs.reshape(seqs_here, span_rows, 2 * HD), True)
    kv_whole = gather_two(gather_two(kv_whole, "y", 1), "c", 2)
    kv_whole = jnp.moveaxis(kv_whole, 3, 0).reshape(seqs_here, span_size * span_rows, 2 * HD)
    queries = (dot(normed_one, query_w) + query_b).astype(LOW)
    queries = queries.reshape(seqs_here, span_rows, HEADS, HD)

    def lse_step(carried, piece, piece_start):

        def lse_compute(state_in):
            running, total = state_in
            scores = masked_scores(
                queries, piece[:, :, :HD], query_pos, query_doc, doc_ends, piece_start
            )
            fresh = jnp.maximum(running, jnp.max(scores, axis=-1))
            total = total * jnp.exp(running - fresh) + jnp.sum(
                jnp.exp(scores - fresh[..., None]), axis=-1
            )
            return (fresh, total)

        return lax.cond(piece_start <= last_query, lse_compute, lambda state_in: state_in, carried)

    def out_step(carried, piece, piece_start):

        def out_compute(summed):
            scores = masked_scores(
                queries, piece[:, :, :HD], query_pos, query_doc, doc_ends, piece_start
            )
            probs = jnp.exp(scores - log_total[..., None]).astype(LOW)
            return summed + jnp.einsum(
                "schr,sre->sche", probs, piece[:, :, HD:], preferred_element_type=F32
            )

        return lax.cond(piece_start <= last_query, out_compute, lambda summed: summed, carried)

    stat_shape = (seqs_here, span_rows, HEADS)
    lse_init = (jnp.full(stat_shape, FLOOR_MAX, F32), jnp.zeros(stat_shape, F32))
    out_init = jnp.zeros((seqs_here, span_rows, HEADS, HD), F32)
    running, total = local_fold(lse_step, lse_init, kv_whole)
    log_total = running + jnp.log(total)
    attn_float = local_fold(out_step, out_init, kv_whole)
    attn_low = attn_float.reshape(row_count, width).astype(LOW)
    resid = inputs_float + dot(attn_low, out_w) + out_b

    normed_two_f, norm_pull_two = jax.vjp(layer_norm, resid, gain_two, shift_two)
    normed_plane = gather_plane(normed_two_f.astype(LOW))
    pre_act = dot(normed_plane, up_w) + up_b
    active_f, gelu_pull = jax.vjp(gelu_tanh, pre_act)
    activation = active_f.astype(LOW)
    grad_down_w = dot(activation, grad_out_plane, ((0,), (0,))).astype(LOW)
    grad_down_w = lax.psum_scatter(grad_down_w, "z", scatter_dimension=0, tiled=True).astype(F32)
    grad_active = dot(grad_out_plane, down_w, ((1,), (1,)))
    grad_pre = gelu_pull(grad_active)[0].astype(LOW)
    grad_normed_two = scatter_plane(dot(grad_pre, up_w, ((1,), (1,))).astype(LOW))
    grad_up_w = dot(normed_plane, grad_pre, ((0,), (0,))).astype(LOW)
    grad_up_w = lax.psum_scatter(
        grad_up_w.reshape(2, planes * 4 * rows, planes * hidden),
        "z",
        scatter_dimension=1,
        tiled=True,
    )
    grad_up_w = collect_columns(grad_up_w.reshape(2, 2, 2, rows, planes * hidden))
    grad_up_w = (
        grad_up_w.reshape(rows, 2, 2, 2, planes, hidden)
        .transpose(0, 1, 4, 2, 3, 5)
        .reshape(rows, -1)
        .astype(F32)
    )
    grad_up_b = jnp.sum(grad_pre.astype(F32), axis=0)
    output = (resid + scatter_plane(dot(activation, down_w).astype(LOW)) + down_b).astype(LOW)
    grad_down_b = jnp.sum(grad_out.astype(F32), axis=0)

    grad_resid_part, grad_gain_two, grad_shift_two = norm_pull_two(grad_normed_two)
    grad_resid = grad_out.astype(F32) + grad_resid_part
    grad_proj = grad_resid.astype(LOW)

    grad_out_w = scatter_rows(dot(attn_low, grad_proj, ((0,), (0,))).astype(LOW))
    grad_out_b = jnp.sum(grad_proj.astype(F32), axis=0)
    grad_heads = dot(grad_proj, out_w, ((1,), (1,))).astype(LOW)
    grad_heads = grad_heads.reshape(seqs_here, span_rows, HEADS, HD)
    delta = jnp.sum(grad_heads.astype(F32) * attn_float, axis=-1)

    def back_step(carried, piece, piece_start):

        def back_compute(state_in):
            grad_query, grad_pairs = state_in
            key_rows = piece[:, :, :HD]
            value_rows = piece[:, :, HD:]
            scores = masked_scores(queries, key_rows, query_pos, query_doc, doc_ends, piece_start)
            probs = jnp.exp(scores - log_total[..., None])
            grad_values = jnp.einsum(
                "schr,sche->sre", probs.astype(LOW), grad_heads, preferred_element_type=F32
            )
            grad_probs = jnp.einsum(
                "sche,sre->schr", grad_heads, value_rows, preferred_element_type=F32
            )
            grad_scores = (probs * (grad_probs - delta[..., None])).astype(LOW)
            grad_query = grad_query + jnp.einsum(
                "schr,sre->sche", grad_scores, key_rows, preferred_element_type=F32
            ) * HD ** (-0.5)
            grad_keys = jnp.einsum(
                "schr,sche->sre", grad_scores, queries, preferred_element_type=F32
            ) * HD ** (-0.5)
            update = jnp.concatenate([grad_keys, grad_values], axis=-1)
            current = lax.dynamic_slice_in_dim(grad_pairs, piece_start, piece.shape[1], 1)
            grad_pairs = lax.dynamic_update_slice_in_dim(
                grad_pairs, current + update, piece_start, 1
            )
            return (grad_query, grad_pairs)

        return lax.cond(piece_start <= last_query, back_compute, lambda state_in: state_in, carried)

    back_init = (
        jnp.zeros((seqs_here, span_rows, HEADS, HD), F32),
        jnp.zeros((seqs_here, span_size * span_rows, 2 * HD), F32),
    )
    grad_query, grad_pairs = local_fold(back_step, back_init, kv_whole)
    grad_pairs = grad_pairs.reshape(seqs_here, planes, 2, 2, span_rows, 2 * HD)
    own, other = own_other(grad_pairs, "c", 3)
    grad_pairs = own + swap(other.astype(LOW), "c").astype(F32)
    own, other = own_other(grad_pairs, "y", 2)
    grad_pairs = own + swap(other.astype(LOW), "y").astype(F32)
    own_pairs = scatter_z(jnp.moveaxis(grad_pairs, 1, 0).astype(LOW))
    own_pairs = own_pairs.astype(LOW).reshape(row_count, 2 * HD)
    query_grad_low = grad_query.reshape(row_count, width).astype(LOW)
    grad_query_w = scatter_rows(dot(normed_one, query_grad_low, ((0,), (0,))).astype(LOW))
    grad_query_b = jnp.sum(query_grad_low.astype(F32), axis=0)
    grad_pair_w = scatter_rows(dot(normed_one, own_pairs, ((0,), (0,))).astype(LOW))
    grad_value_b = jnp.sum(own_pairs[:, HD:].astype(F32), axis=0)
    grad_normed_one = dot(query_grad_low, query_w, ((1,), (1,))) + dot(
        own_pairs, pair_w, ((1,), (1,))
    )
    grad_input_part, grad_gain_one, grad_shift_one = norm_pull_one(grad_normed_one)
    input_grad = grad_resid + grad_input_part

    grad_up_whole = lax.dynamic_update_slice(
        jnp.zeros((2, planes, 2, 2, hidden), F32),
        grad_up_b.reshape(1, planes, 1, 1, hidden),
        (at_x, 0, at_y, at_c, 0),
    ).reshape(-1)
    vectors = (
        grad_gain_one,
        grad_shift_one,
        grad_query_b,
        grad_out_b,
        grad_gain_two,
        grad_shift_two,
        grad_down_b,
        grad_up_whole,
        grad_value_b,
    )
    flat = jnp.concatenate([vector.reshape(devices, -1) for vector in vectors], axis=1)
    size = flat.shape[1]
    flat = scatter_small(jnp.pad(flat, ((0, 0), (0, -size % 128))))
    sums, start = [], 0
    for piece in small:
        sums.append(flat[start : start + piece.shape[0]])
        start += piece.shape[0]
    return (
        output.reshape(seqs_here, span_rows, width),
        input_grad.reshape(seqs_here, span_rows, width),
        sums[0],
        sums[1],
        grad_query_w,
        sums[2],
        grad_pair_w,
        sums[8],
        grad_out_w,
        sums[3],
        sums[4],
        sums[5],
        grad_up_w,
        sums[7],
        grad_down_w,
        sums[6],
    )


def solution(mesh):
    span = mesh.shape["span"]
    fine = Mesh(mesh.devices.reshape(2, span // 4, 2, 2), ("x", "z", "y", "c"))
    every = ("x", "z", "y", "c")
    acts = P("x", ("z", "y", "c"), None)
    vector = P(every)
    matrix = P(every, None)
    return jax.shard_map(
        local,
        mesh=fine,
        in_specs=(
            acts,
            P("x", None),
            vector,
            vector,
            matrix,
            vector,
            matrix,
            vector,
            matrix,
            vector,
            vector,
            vector,
            matrix,
            vector,
            matrix,
            vector,
            acts,
        ),
        out_specs=(
            acts,
            acts,
            vector,
            vector,
            matrix,
            vector,
            matrix,
            vector,
            matrix,
            vector,
            vector,
            vector,
            matrix,
            vector,
            matrix,
            vector,
        ),
        check_vma=False,
    )
```

time: 2880 us -> 724 us (0.25)
  waiting for transfers between devices: 2530 us -> 254 us
  starting transfers between devices: 0.77 us -> 142 us
  matrix products: 191 us -> 97.2 us
  blocking collectives: 82.6 us -> 0 us
  other arithmetic: 18.5 us -> 101 us
  local copies, waits for them, and re-layouts: 29.9 us -> 104 us
    reduce_scatter x6 -> x2, waiting for transfers between devices: 1980 us -> 0.01 us  [the longest x1 0.01 us: local(): lax.psum_scatter(grad_up_w.reshape(2, planes * 4 * rows, planes * hidden)...]
    all_gather x6 -> x2, waiting for transfers between devices: 514 us -> 0.01 us  [the longest x1 0.01 us: local(): lax.all_gather(up_own, 'z', axis=1, tiled=True)]
    ppermute x0 -> x103, waiting for transfers between devices: none -> 254 us  [the longest x61 161 us: swap(): return lax.ppermute(value, axis, SWAP)]
    ppermute x0 -> x103, starting transfers between devices: none -> 142 us  [the longest x42 92.1 us: shift_z(): lax.ppermute(value, 'z', [(i, (i + by) % count) for i in range(count)])]
    dot_general x18, matrix products: 181 us -> 88.9 us  [the longest x15 84 us: dot(): lax.dot_general(left, right, (dims, ((), ())), preferred_element_type=F32)]
    another operation x1 -> x43, other arithmetic: 0.18 us -> 48.3 us  [the longest x30 46.8 us: in_order(): jnp.stack([jnp.where(first, own, got), jnp.where(first, got, own)], axis=at)]
    unnamed x1 -> x0, blocking collectives: 42.7 us -> none
    all_gather x1 -> x0, blocking collectives: 39.9 us -> none  [local(): lax.all_gather(fc_bias, ('seq', 'span'), axis=0, tiled=True)]
  transfers between devices with their start and end apart: 13 -> 107, of which waited for: 13 -> 55; matrix products, arithmetic and copies ran while one was open for 6% -> 37% of each run, Pallas kernels for 0% -> 0%
where the time goes in v1:
time: 724 us; the launch traced here: 716 us
  waiting for transfers between devices  254 us (35%)
  starting transfers between devices  142 us (20%)
  local copies, waits for them, and re-layouts  104 us (14%)
  other arithmetic  101 us (14%)
  matrix products  97.2 us (13%)
  between operations  16.6 us (2%)
    ppermute x61, waiting for transfers between devices, swap(): return lax.ppermute(value, axis, SWAP)  161 us
    ppermute x42, waiting for transfers between devices, shift_z(): lax.ppermute(value, 'z', [(i, (i + by) % count) for i in range(count)])  93.1 us
    ppermute x42, starting transfers between devices, shift_z(): lax.ppermute(value, 'z', [(i, (i + by) % count) for i in range(count)])  92.1 us
    dot_general x15, matrix products, dot(): lax.dot_general(left, right, (dims, ((), ())), preferred_element_type=F32)  84 us
    ppermute x61, starting transfers between devices, swap(): return lax.ppermute(value, axis, SWAP)  49.7 us
    another operation x30, other arithmetic, in_order(): jnp.stack([jnp.where(first, own, got), jnp.where(first, got, own)], axis=at)  46.8 us
    unnamed x205, local copies, waits for them, and re-layouts  25.7 us
    convert_element_type x19, other arithmetic, add_low(): return (own.astype(F32) + got.astype(F32)).astype(LOW)  22.4 us
  transfers between devices with their start and end apart: 107, of which 55 were waited for; matrix products, arithmetic and copies ran while one was open for 37% of the time, Pallas kernels for 0%

profile of v1, /device:TPU:0, one launch (start us, length us, event | category | flops | bytes accessed | tf_op | source)
XLA Modules:
  0.0 715.5 jit_solution(3628859813352203467)
XLA Ops:
  15.5 12.2 %collective-permute-done.39 = bf16[2,64,2,1024]{3,1,2,0:T(8,128)(2,1)S(1)} collective-permute-done((bf16[2,64,2,1024]{3,1,2,0:T(8,128)(2,1)S(1)}, bf16[2,64,2,1024]{3,1,2,0:T(8,128)(2,1)S(1)}, u32[]{:S(2)}, u32[]{:S(2)}) %collective-permute-start.39) | collective-permute-done | bytes 524320 | tf_op jit(solution)/shard_map/ppermute | solution.py:40
  29.8 11.7 %collective-permute-done.40 = bf16[2,2,64,1024]{3,2,1,0:T(8,128)(2,1)S(1)} collective-permute-done((bf16[2,2,64,1024]{3,2,1,0:T(8,128)(2,1)S(1)}, bf16[2,2,64,1024]{3,2,1,0:T(8,128)(2,1)S(1)}, u32[]{:S(2)}, u32[]{:S(2)}) %collective-permute-start.40) | collective-permute-done | bytes 524320 | tf_op jit(solution)/shard_map/ppermute | solution.py:40
  53.0 3.4 collective-permute-start.27
  61.8 5.6 collective-permute-done.22
  67.4 5.6 collective-permute-done.27
  75.2 3.4 collective-permute-done.12
  78.6 5.0 collective-permute-start.13
  84.2 5.2 collective-permute-start.18
  90.5 7.2 %collective-permute-start.24 = (bf16[64,1024]{1,0:T(8,128)(2,1)S(1)}, bf16[64,1024]{1,0:T(8,128)(2,1)S(1)}, u32[]{:S(2)}, u32[]{:S(2)}) collective-permute-start(bf16[64,1024]{1,0:T(8,128)(2,1)S(1)} %collective-permute-done.23), channel_id=1, source_target_pairs={{0,4},{4,8},{8,12},{12,0},{1,5},{5,9},{9,13},{13,1},{2,6},{6,10},{... | collective-permute-start | bytes 393224 | tf_op jit(solution)/shard_map/ppermute | solution.py:65
  97.7 8.4 %collective-permute-start.29 = (bf16[64,1024]{1,0:T(8,128)(2,1)S(1)}, bf16[64,1024]{1,0:T(8,128)(2,1)S(1)}, u32[]{:S(2)}, u32[]{:S(2)}) collective-permute-start(bf16[64,1024]{1,0:T(8,128)(2,1)S(1)} %collective-permute-done.28), channel_id=1, source_target_pairs={{0,4},{4,8},{8,12},{12,0},{1,5},{5,9},{9,13},{13,1},{2,6},{6,10},{... | collective-permute-start | bytes 393224 | tf_op jit(solution)/shard_map/ppermute | solution.py:65
  111.9 8.0 %collective-permute-done.29 = bf16[64,1024]{1,0:T(8,128)(2,1)S(1)} collective-permute-done((bf16[64,1024]{1,0:T(8,128)(2,1)S(1)}, bf16[64,1024]{1,0:T(8,128)(2,1)S(1)}, u32[]{:S(2)}, u32[]{:S(2)}) %collective-permute-start.29) | collective-permute-done | bytes 131104 | tf_op jit(solution)/shard_map/ppermute | solution.py:65
  137.7 19.0 %collective-permute-done.15 = bf16[2,4,64,1024]{3,2,1,0:T(8,128)(2,1)} collective-permute-done((bf16[2,4,64,1024]{3,2,1,0:T(8,128)(2,1)}, bf16[2,4,64,1024]{3,2,1,0:T(8,128)(2,1)}, u32[]{:S(2)}, u32[]{:S(2)}) %collective-permute-start.15) | collective-permute-done | bytes 1048608 | tf_op jit(solution)/shard_map/ppermute | solution.py:40
  163.9 23.9 %collective-permute-start.6 = (bf16[2,64,256]{2,1,0:T(8,128)(2,1)S(1)}, bf16[2,64,256]{2,1,0:T(8,128)(2,1)S(1)}, u32[]{:S(2)}, u32[]{:S(2)}) collective-permute-start(bf16[2,64,256]{2,1,0:T(8,128)(2,1)S(1)} %bitcast.631), channel_id=1, source_target_pairs={{0,4},{4,8},{8,12},{12,0},{1,5},{5,9},{9,13},{13,1},{2,6},{6,10},{... | collective-permute-start | bytes 196616 | tf_op jit(solution)/shard_map/ppermute | solution.py:65
  191.6 6.2 collective-permute-start.8
  198.8 5.4 collective-permute-done.8
  217.7 5.9 collective-permute-done.9
  227.3 7.2 %collective-permute-done.47 = bf16[128,2048]{1,0:T(8,128)(2,1)S(1)} collective-permute-done((bf16[128,2048]{1,0:T(8,128)(2,1)S(1)}, bf16[128,2048]{1,0:T(8,128)(2,1)S(1)}, u32[]{:S(2)}, u32[]{:S(2)}) %collective-permute-start.47) | collective-permute-done | bytes 524320 | tf_op jit(solution)/shard_map/ppermute | solution.py:40
  238.5 6.8 select_bitcast_fusion.3
  245.3 7.7 %pad_maximum_fusion = bf16[2,4,2,2,64,2048]{5,4,3,2,1,0:T(8,128)(2,1)} fusion(bf16[2,4,2,1,64,2048]{5,4,3,2,1,0:T(8,128)(2,1)} %get-tuple-element.1130, bf16[2,4,2,1,64,2048]{5,4,3,2,1,0:T(8,128)(2,1)} %get-tuple-element.1129), kind=kLoop, calls=%fused_computation.61 | loop fusion | flops 4194304 | bytes 16777216 | tf_op jit(solution)/shard_map/stack | solution.py:49
  252.9 4.7 fusion.59
  265.3 7.7 %select_bitcast_fusion.1 = (bf16[2,4,2,1,64,2048]{5,4,2,1,0,3:T(8,128)(2,1)}, bf16[2,4,2,1,64,2048]{5,4,2,1,0,3:T(8,128)(2,1)}) fusion(bf16[2,4,2,64,2048]{4,3,2,1,0:T(8,128)(2,1)} %collective-permute-done.32, pred[]{:T(512)S(6)} %eq.141, bf16[1,4,2,64,1024]{4,3,2,1,0:T(8,128)(2,1)} %copy-done.21, bf16[1,4,2,64,1024]{4,3,2,1,0:T(8,128)(2,1)} %copy-done.20, ...), kind=kLoop, calls=%fused_computation.90 | loop fusion | flops 20971520 | bytes 16777216 | tf_op jit(solution)/shard_map/stack | solution.py:49
  273.0 7.6 %pad_maximum_fusion.1 = bf16[2,4,2,2,64,2048]{5,4,2,1,0,3:T(8,128)(2,1)} fusion(bf16[2,4,2,1,64,2048]{5,4,2,1,0,3:T(8,128)(2,1)} %get-tuple-element.1132, bf16[2,4,2,1,64,2048]{5,4,2,1,0,3:T(8,128)(2,1)} %get-tuple-element.1131), kind=kLoop, calls=%fused_computation.62 | loop fusion | flops 4194304 | bytes 16777216 | tf_op jit(solution)/shard_map/stack | solution.py:49
  280.6 8.4 %copy.170 = bf16[2,4,2,2,64,2048]{5,4,3,2,1,0:T(8,128)(2,1)} copy(bf16[2,4,2,2,64,2048]{5,4,2,1,0,3:T(8,128)(2,1)} %pad_maximum_fusion.1) | data formatting | bytes 16777216 | tf_op jit(solution)/shard_map/stack | solution.py:49
  289.1 4.8 fusion.154
  296.2 7.1 collective-permute-done.33
  307.6 8.6 %collective-permute-done.34 = bf16[128,2048]{1,0:T(8,128)(2,1)S(1)} collective-permute-done((bf16[128,2048]{1,0:T(8,128)(2,1)S(1)}, bf16[128,2048]{1,0:T(8,128)(2,1)S(1)}, u32[]{:S(2)}, u32[]{:S(2)}) %collective-permute-start.34) | collective-permute-done | bytes 524320 | tf_op jit(solution)/shard_map/ppermute | solution.py:40
  320.2 4.1 collective-permute-done.35
  326.6 8.5 %collective-permute-done.36 = bf16[128,2048]{1,0:T(8,128)(2,1)S(1)} collective-permute-done((bf16[128,2048]{1,0:T(8,128)(2,1)S(1)}, bf16[128,2048]{1,0:T(8,128)(2,1)S(1)}, u32[]{:S(2)}, u32[]{:S(2)}) %collective-permute-start.36) | collective-permute-done | bytes 524320 | tf_op jit(solution)/shard_map/ppermute | solution.py:40
  337.1 3.2 constant_dynamic-update-slice_fusion.21
  340.7 3.2 constant_dynamic-update-slice_fusion.8
  343.9 10.0 %fusion.155 = f32[1024,1024]{1,0:T(8,128)} fusion(bf16[1024,2048]{1,0:T(8,128)(2,1)} %constant_dynamic-update-slice_fusion.8, bf16[2048,1024]{1,0:T(8,128)(2,1)} %bitcast.664), kind=kOutput, calls=%fused_computation.486 | convolution fusion | flops 4294967296 | bytes 12582912 | tf_op jit(solution)/shard_map/dot_general | solution.py:36
  353.9 11.5 %convert_reduce_fusion.3 = (f32[1024]{0:T(1024)S(1)}, bf16[1024,1024]{1,0:T(8,128)(2,1)S(1)}) fusion(f32[1024,1024]{1,0:T(8,128)} %fusion.155, f32[1024]{0:T(1024)S(1)} %bitcast.656, bf16[1024,2048]{1,0:T(8,128)(2,1)} %constant_dynamic-update-slice_fusion.21, bf16[1024,2048]{1,0:T(8,128)(2,1)} %all-gather.5.cloned.1.call-done), kind=kOutput, calls=%fused_computation.85 | convolution fusion | flops 4323277824 | bytes 14688256 | tf_op jit(solution)/shard_map/dot_general | solution.py:36
  365.4 5.0 convolution_convert_fusion.4
  374.8 5.2 convolution_convert_fusion.5
  381.7 8.8 %convolution_convert_fusion.3 = bf16[2048,1024]{1,0:T(8,128)(2,1)} fusion(bf16[1024,2048]{1,0:T(8,128)(2,1)} %constant_dynamic-update-slice_fusion.8, bf16[1024,1024]{1,0:T(8,128)(2,1)S(1)} %get-tuple-element.1116), kind=kOutput, calls=%fused_computation.94 | convolution fusion | flops 4297064448 | bytes 10485760 | tf_op jit(solution)/shard_map/dot_general | solution.py:36
  390.6 3.2 add_convert_fusion
  403.8 6.2 collective-permute-done.52
  415.3 5.9 collective-permute-done.42
  428.3 4.3 collective-permute-done.43
  443.3 11.2 %while.51 = (s32[]{:T(128)}, f32[2,64,16,128]{3,2,1,0:T(8,128)S(1)}, f32[2,1024,256]{1,2,0:T(8,128)}, s32[]{:T(128)}, s32[2,4]{1,0:T(2,128)S(1)}, /*index=5*/s32...) while((s32[]{:T(128)}, ...), condition=%wide.region_27.28_spmd.clone, body=%wide.region_23.27_spmd.clone.sunk | while | flops 1354018304 | bytes 64020480 | solution.py:214
  443.7 10.7 %conditional.11 = ((f32[2,64,16,128]{3,2,1,0:T(8,128)S(1)}, f32[2,1024,256]{1,2,0:T(8,128)})) conditional(s32[]{:T(128)} %convert_element_type.1241, (f32[2,64,16,128]{3,2,1,0:T(8,128)S(1)}, f32[2,1024,256]{1,2,0:T(8,128)}) %tuple.264, (s32[]{:T(128)}, s32[]{:T(128)}, s32[2,4]{1,0:T(2,128)S(1)}, s32[2,64]{1,0:T(2,128)S(1)}, ...), branch_computations={%region_24.24_spmd, %region_25.26_spmd} | conditional | flops 1354018304 | bytes 64019952 | solution.py:395
  446.9 3.8 fusion.18
  463.9 10.7 %convolution_convert_fusion.2 = bf16[1024,2048]{1,0:T(8,128)(2,1)} fusion(bf16[1024,2048]{1,0:T(8,128)(2,1)} %constant_dynamic-update-slice_fusion.21, f32[1024,1024]{1,0:T(8,128)} %fusion.155, f32[1024]{0:T(1024)S(1)} %bitcast.658), kind=kOutput, calls=%fused_computation.93 | convolution fusion | flops 4307550208 | bytes 12587008 | tf_op jit(solution)/shard_map/dot_general | solution.py:36
  475.9 3.3 collective-permute-start.58
  479.2 6.8 convolution_convert_fusion
  486.1 12.8 %collective-permute-done.58 = bf16[2,64,256]{2,1,0:T(8,128)(2,1)S(1)} collective-permute-done((bf16[2,64,256]{2,1,0:T(8,128)(2,1)S(1)}, bf16[2,64,256]{2,1,0:T(8,128)(2,1)S(1)}, u32[]{:S(2)}, u32[]{:S(2)}) %collective-permute-start.58) | collective-permute-done | bytes 65568 | tf_op jit(solution)/shard_map/ppermute | solution.py:65
  498.9 3.4 collective-permute-start.59
  503.0 4.7 collective-permute-done.59
  509.2 5.7 convolution_convert_fusion.1
  521.1 6.6 fusion.144
  528.9 8.8 %constant_dynamic-slice_fusion.1 = (bf16[2,4,2,1,64,2048]{5,4,3,2,1,0:T(8,128)(2,1)}, bf16[2,4,2,1,64,2048]{5,4,3,2,1,0:T(8,128)(2,1)}) fusion(bf16[2,4,2,2,64,2048]{5,4,3,2,1,0:T(8,128)(2,1)} %bitcast.597, s32[]{:T(128)S(6)} %select_n.608, s32[]{:T(128)S(6)} %select_n.609), kind=kLoop, calls=%fused_computation.380 | loop fusion | bytes 16777224 | tf_op jit(solution)/shard_map/jit(dynamic_index_in_dim)/dynamic_slice | solution.py:54
  537.7 4.9 copy.257
  544.8 4.2 constant_dynamic-slice_fusion.13
  549.0 4.8 copy.258
  560.3 3.2 collective-permute-done.64
  564.1 5.3 collective-permute-done.65
  571.0 3.9 collective-permute-done.66
  584.8 3.6 collective-permute-done.85
  590.4 3.7 collective-permute-done.86
  596.0 3.7 collective-permute-done.87
  601.5 3.8 collective-permute-done.88
  605.3 4.1 fusion.44
  618.1 18.2 %collective-permute-done.90 = bf16[4,2,64,1024]{3,2,0,1:T(8,128)(2,1)S(1)} collective-permute-done((bf16[4,2,64,1024]{3,2,0,1:T(8,128)(2,1)S(1)}, bf16[4,2,64,1024]{3,2,0,1:T(8,128)(2,1)S(1)}, u32[]{:S(2)}, u32[]{:S(2)}) %collective-permute-start.90) | collective-permute-done | bytes 1048608 | tf_op jit(solution)/shard_map/ppermute | solution.py:40
  639.7 19.0 %collective-permute-done.68 = bf16[4,2,64,1024]{3,2,0,1:T(8,128)(2,1)S(1)} collective-permute-done((bf16[4,2,64,1024]{3,2,0,1:T(8,128)(2,1)S(1)}, bf16[4,2,64,1024]{3,2,0,1:T(8,128)(2,1)S(1)}, u32[]{:S(2)}, u32[]{:S(2)}) %collective-permute-start.68) | collective-permute-done | bytes 1048608 | tf_op jit(solution)/shard_map/ppermute | solution.py:40
  (677 shorter events, 274.8 us)
Async XLA Ops:
  7.2 336.7 %all-gather.3.cloned.1.call-start = ((), (), s32[]{:S(2)}) async-start(), calls=%async_computation.2 | async-start | bytes 5242880 | tf_op jit(solution)/shard_map/all_gather | solution.py:269
  12.5 15.2 %collective-permute-start.39 = (bf16[2,64,2,1024]{3,1,2,0:T(8,128)(2,1)S(1)}, bf16[2,64,2,1024]{3,1,2,0:T(8,128)(2,1)S(1)}, u32[]{:S(2)}, u32[]{:S(2)}) collective-permute-start(bf16[2,64,2,1024]{3,1,2,0:T(8,128)(2,1)S(1)} %fusion.83), channel_id=1, source_target_pairs={{0,2},{2,0},{1,3},{3,1},{4,6},{6,4},{5,7},{7,5},{8,10},{10,8},{9,1... | collective-permute-start | bytes 1572872 | tf_op jit(solution)/shard_map/ppermute | solution.py:40
  28.0 13.5 %collective-permute-start.40 = (bf16[2,2,64,1024]{3,2,1,0:T(8,128)(2,1)S(1)}, bf16[2,2,64,1024]{3,2,1,0:T(8,128)(2,1)S(1)}, u32[]{:S(2)}, u32[]{:S(2)}) collective-permute-start(bf16[2,2,64,1024]{3,2,1,0:T(8,128)(2,1)S(1)} %fusion.79), channel_id=1, source_target_pairs={{0,16},{16,0},{1,17},{17,1},{2,18},{18,2},{3,19},{19,3},{4,20},{20... | collective-permute-start | bytes 1572872 | tf_op jit(solution)/shard_map/ppermute | solution.py:40
  42.7 311.2 %all-gather.5.cloned.1.call-start = ((), (), s32[]{:S(2)}) async-start(), calls=%async_computation.3 | async-start | bytes 5242880 | tf_op jit(solution)/shard_map/all_gather | solution.py:270
  49.2 12.5 %collective-permute-start.16 = (bf16[64,1024]{1,0:T(8,128)(2,1)S(1)}, bf16[64,1024]{1,0:T(8,128)(2,1)S(1)}, u32[]{:S(2)}, u32[]{:S(2)}) collective-permute-start(bf16[64,1024]{1,0:T(8,128)(2,1)S(1)} %get-tuple-element.1240), channel_id=1, source_target_pairs={{0,4},{4,8},{8,12},{12,0},{1,5},{5,9},{9,13},{13,1},{2,6},{6,10},{... | collective-permute-start | bytes 393224 | tf_op jit(solution)/shard_map/ppermute | solution.py:65
  49.6 613.6 %reduce-scatter.3.cloned.1.call-start = ((), (), s32[]{:S(2)}) async-start(), calls=%async_computation.4 | async-start | bytes 5242880 | tf_op jit(solution)/shard_map/reduce_scatter | solution.py:340
  52.4 14.9 %collective-permute-start.22 = (bf16[64,1024]{1,0:T(8,128)(2,1)S(1)}, bf16[64,1024]{1,0:T(8,128)(2,1)S(1)}, u32[]{:S(2)}, u32[]{:S(2)}) collective-permute-start(bf16[64,1024]{1,0:T(8,128)(2,1)S(1)} %get-tuple-element.1249), channel_id=1, source_target_pairs={{0,4},{4,8},{8,12},{12,0},{1,5},{5,9},{9,13},{13,1},{2,6},{6,10},{... | collective-permute-start | bytes 393224 | tf_op jit(solution)/shard_map/ppermute | solution.py:65
  53.0 19.9 %collective-permute-start.27 = (bf16[64,1024]{1,0:T(8,128)(2,1)S(1)}, bf16[64,1024]{1,0:T(8,128)(2,1)S(1)}, u32[]{:S(2)}, u32[]{:S(2)}) collective-permute-start(bf16[64,1024]{1,0:T(8,128)(2,1)S(1)} %get-tuple-element.1248), channel_id=1, source_target_pairs={{0,4},{4,8},{8,12},{12,0},{1,5},{5,9},{9,13},{13,1},{2,6},{6,10},{... | collective-permute-start | bytes 393224 | tf_op jit(solution)/shard_map/ppermute | solution.py:65
  56.5 27.2 %collective-permute-start.3 = (bf16[4,80,256]{2,1,0:T(8,128)(2,1)S(1)}, bf16[4,80,256]{2,1,0:T(8,128)(2,1)S(1)}, u32[]{:S(2)}, u32[]{:S(2)}) collective-permute-start(bf16[4,80,256]{2,1,0:T(8,128)(2,1)S(1)} %pad_maximum_fusion.31), channel_id=1, source_target_pairs={{0,2},{2,0},{1,3},{3,1},{4,6},{6,4},{5,7},{7,5},{8,10},{10,8},{9,1... | collective-permute-start | bytes 491528 | tf_op jit(solution)/shard_map/ppermute | solution.py:40
  58.1 20.5 %collective-permute-start.12 = (bf16[64,1024]{1,0:T(8,128)(2,1)S(1)}, bf16[64,1024]{1,0:T(8,128)(2,1)S(1)}, u32[]{:S(2)}, u32[]{:S(2)}) collective-permute-start(bf16[64,1024]{1,0:T(8,128)(2,1)S(1)} %collective-permute-done.11), channel_id=1, source_target_pairs={{0,4},{4,8},{8,12},{12,0},{1,5},{5,9},{9,13},{13,1},{2,6},{6,10},{... | collective-permute-start | bytes 393224 | tf_op jit(solution)/shard_map/ppermute | solution.py:65
  61.7 22.4 %collective-permute-start.17 = (bf16[64,1024]{1,0:T(8,128)(2,1)S(1)}, bf16[64,1024]{1,0:T(8,128)(2,1)S(1)}, u32[]{:S(2)}, u32[]{:S(2)}) collective-permute-start(bf16[64,1024]{1,0:T(8,128)(2,1)S(1)} %collective-permute-done.16), channel_id=1, source_target_pairs={{0,4},{4,8},{8,12},{12,0},{1,5},{5,9},{9,13},{13,1},{2,6},{6,10},{... | collective-permute-start | bytes 393224 | tf_op jit(solution)/shard_map/ppermute | solution.py:65
  67.4 23.1 %collective-permute-start.23 = (bf16[64,1024]{1,0:T(8,128)(2,1)S(1)}, bf16[64,1024]{1,0:T(8,128)(2,1)S(1)}, u32[]{:S(2)}, u32[]{:S(2)}) collective-permute-start(bf16[64,1024]{1,0:T(8,128)(2,1)S(1)} %collective-permute-done.22), channel_id=1, source_target_pairs={{0,4},{4,8},{8,12},{12,0},{1,5},{5,9},{9,13},{13,1},{2,6},{6,10},{... | collective-permute-start | bytes 393224 | tf_op jit(solution)/shard_map/ppermute | solution.py:65
  72.9 24.8 %collective-permute-start.28 = (bf16[64,1024]{1,0:T(8,128)(2,1)S(1)}, bf16[64,1024]{1,0:T(8,128)(2,1)S(1)}, u32[]{:S(2)}, u32[]{:S(2)}) collective-permute-start(bf16[64,1024]{1,0:T(8,128)(2,1)S(1)} %collective-permute-done.27), channel_id=1, source_target_pairs={{0,4},{4,8},{8,12},{12,0},{1,5},{5,9},{9,13},{13,1},{2,6},{6,10},{... | collective-permute-start | bytes 393224 | tf_op jit(solution)/shard_map/ppermute | solution.py:65
  78.6 27.5 %collective-permute-start.13 = (bf16[64,1024]{1,0:T(8,128)(2,1)S(1)}, bf16[64,1024]{1,0:T(8,128)(2,1)S(1)}, u32[]{:S(2)}, u32[]{:S(2)}) collective-permute-start(bf16[64,1024]{1,0:T(8,128)(2,1)S(1)} %collective-permute-done.12), channel_id=1, source_target_pairs={{0,4},{4,8},{8,12},{12,0},{1,5},{5,9},{9,13},{13,1},{2,6},{6,10},{... | collective-permute-start | bytes 393224 | tf_op jit(solution)/shard_map/ppermute | solution.py:65
  84.2 22.0 %collective-permute-start.18 = (bf16[64,1024]{1,0:T(8,128)(2,1)S(1)}, bf16[64,1024]{1,0:T(8,128)(2,1)S(1)}, u32[]{:S(2)}, u32[]{:S(2)}) collective-permute-start(bf16[64,1024]{1,0:T(8,128)(2,1)S(1)} %collective-permute-done.17), channel_id=1, source_target_pairs={{0,4},{4,8},{8,12},{12,0},{1,5},{5,9},{9,13},{13,1},{2,6},{6,10},{... | collective-permute-start | bytes 393224 | tf_op jit(solution)/shard_map/ppermute | solution.py:65
  89.4 34.0 %collective-permute-start.4 = (bf16[4,2,80,256]{3,2,1,0:T(8,128)(2,1)S(1)}, bf16[4,2,80,256]{3,2,1,0:T(8,128)(2,1)S(1)}, u32[]{:S(2)}, u32[]{:S(2)}) collective-permute-start(bf16[4,2,80,256]{3,2,1,0:T(8,128)(2,1)S(1)} %pad_maximum_fusion.26), channel_id=1, source_target_pairs={{0,16},{16,0},{1,17},{17,1},{2,18},{18,2},{3,19},{19,3},{4,20},{20... | collective-permute-start | bytes 983048 | tf_op jit(solution)/shard_map/ppermute | solution.py:40
  90.5 21.3 %collective-permute-start.24 = (bf16[64,1024]{1,0:T(8,128)(2,1)S(1)}, bf16[64,1024]{1,0:T(8,128)(2,1)S(1)}, u32[]{:S(2)}, u32[]{:S(2)}) collective-permute-start(bf16[64,1024]{1,0:T(8,128)(2,1)S(1)} %collective-permute-done.23), channel_id=1, source_target_pairs={{0,4},{4,8},{8,12},{12,0},{1,5},{5,9},{9,13},{13,1},{2,6},{6,10},{... | collective-permute-start | bytes 393224 | tf_op jit(solution)/shard_map/ppermute | solution.py:65
  97.7 22.2 %collective-permute-start.29 = (bf16[64,1024]{1,0:T(8,128)(2,1)S(1)}, bf16[64,1024]{1,0:T(8,128)(2,1)S(1)}, u32[]{:S(2)}, u32[]{:S(2)}) collective-permute-start(bf16[64,1024]{1,0:T(8,128)(2,1)S(1)} %collective-permute-done.28), channel_id=1, source_target_pairs={{0,4},{4,8},{8,12},{12,0},{1,5},{5,9},{9,13},{13,1},{2,6},{6,10},{... | collective-permute-start | bytes 393224 | tf_op jit(solution)/shard_map/ppermute | solution.py:65
  106.5 17.2 %collective-permute-start.14 = (bf16[4,64,1024]{2,1,0:T(8,128)(2,1)S(1)}, bf16[4,64,1024]{2,1,0:T(8,128)(2,1)S(1)}, u32[]{:S(2)}, u32[]{:S(2)}) collective-permute-start(bf16[4,64,1024]{2,1,0:T(8,128)(2,1)S(1)} %pad_maximum_fusion.13), channel_id=1, source_target_pairs={{0,16},{16,0},{1,17},{17,1},{2,18},{18,2},{3,19},{19,3},{4,20},{20... | collective-permute-start | bytes 1572872 | tf_op jit(solution)/shard_map/ppermute | solution.py:40
  107.9 17.4 %collective-permute-start.19 = (bf16[4,64,1024]{2,1,0:T(8,128)(2,1)S(1)}, bf16[4,64,1024]{2,1,0:T(8,128)(2,1)S(1)}, u32[]{:S(2)}, u32[]{:S(2)}) collective-permute-start(bf16[4,64,1024]{2,1,0:T(8,128)(2,1)S(1)} %pad_maximum_fusion.15), channel_id=1, source_target_pairs={{0,2},{2,0},{1,3},{3,1},{4,6},{6,4},{5,7},{7,5},{8,10},{10,8},{9,1... | collective-permute-start | bytes 1572872 | tf_op jit(solution)/shard_map/ppermute | solution.py:40
  121.8 12.4 %collective-permute-start.30 = (bf16[4,64,1024]{2,1,0:T(8,128)(2,1)S(1)}, bf16[4,64,1024]{2,1,0:T(8,128)(2,1)S(1)}, u32[]{:S(2)}, u32[]{:S(2)}) collective-permute-start(bf16[4,64,1024]{2,1,0:T(8,128)(2,1)S(1)} %pad_maximum_fusion.19), channel_id=1, source_target_pairs={{0,2},{2,0},{1,3},{3,1},{4,6},{6,4},{5,7},{7,5},{8,10},{10,8},{9,1... | collective-permute-start | bytes 1572872 | tf_op jit(solution)/shard_map/ppermute | solution.py:40
  123.6 12.3 %collective-permute-start.5 = (bf16[2,4,2,80,256]{4,3,2,1,0:T(8,128)(2,1)S(1)}, bf16[2,4,2,80,256]{4,3,2,1,0:T(8,128)(2,1)S(1)}, u32[]{:S(2)}, u32[]{:S(2)}) collective-permute-start(bf16[2,4,2,80,256]{4,3,2,1,0:T(8,128)(2,1)S(1)} %pad_maximum_fusion.10), channel_id=1, source_target_pairs={{0,1},{1,0},{2,3},{3,2},{4,5},{5,4},{6,7},{7,6},{8,9},{9,8},{10,11... | collective-permute-start | bytes 1966088 | tf_op jit(solution)/shard_map/ppermute | solution.py:40
  124.8 31.9 %collective-permute-start.15 = (bf16[2,4,64,1024]{3,2,1,0:T(8,128)(2,1)}, bf16[2,4,64,1024]{3,2,1,0:T(8,128)(2,1)}, u32[]{:S(2)}, u32[]{:S(2)}) collective-permute-start(bf16[2,4,64,1024]{3,2,1,0:T(8,128)(2,1)} %pad_maximum_fusion.4), channel_id=1, source_target_pairs={{0,2},{2,0},{1,3},{3,1},{4,6},{6,4},{5,7},{7,5},{8,10},{10,8},{9,1... | collective-permute-start | bytes 3145736 | tf_op jit(solution)/shard_map/ppermute | solution.py:40
  126.5 31.6 %collective-permute-start.20 = (bf16[4,2,64,1024]{3,2,1,0:T(8,128)(2,1)}, bf16[4,2,64,1024]{3,2,1,0:T(8,128)(2,1)}, u32[]{:S(2)}, u32[]{:S(2)}) collective-permute-start(bf16[4,2,64,1024]{3,2,1,0:T(8,128)(2,1)} %pad_maximum_fusion.5), channel_id=1, source_target_pairs={{0,16},{16,0},{1,17},{17,1},{2,18},{18,2},{3,19},{19,3},{4,20},{20... | collective-permute-start | bytes 3145736 | tf_op jit(solution)/shard_map/ppermute | solution.py:40
  130.7 77.2 %collective-permute-start.26 = (bf16[2,4,64,1024]{3,2,1,0:T(8,128)(2,1)}, bf16[2,4,64,1024]{3,2,1,0:T(8,128)(2,1)}, u32[]{:S(2)}, u32[]{:S(2)}) collective-permute-start(bf16[2,4,64,1024]{3,2,1,0:T(8,128)(2,1)} %pad_maximum_fusion.6), channel_id=1, source_target_pairs={{0,2},{2,0},{1,3},{3,1},{4,6},{6,4},{5,7},{7,5},{8,10},{10,8},{9,1... | collective-permute-start | bytes 3145736 | tf_op jit(solution)/shard_map/ppermute | solution.py:40
  135.5 74.1 %collective-permute-start.31 = (bf16[4,2,64,1024]{3,2,1,0:T(8,128)(2,1)}, bf16[4,2,64,1024]{3,2,1,0:T(8,128)(2,1)}, u32[]{:S(2)}, u32[]{:S(2)}) collective-permute-start(bf16[4,2,64,1024]{3,2,1,0:T(8,128)(2,1)} %pad_maximum_fusion.7), channel_id=1, source_target_pairs={{0,16},{16,0},{1,17},{17,1},{2,18},{18,2},{3,19},{19,3},{4,20},{20... | collective-permute-start | bytes 3145736 | tf_op jit(solution)/shard_map/ppermute | solution.py:40
  163.0 75.5 %collective-permute-start.21 = (bf16[2,4,2,64,2048]{4,3,2,1,0:T(8,128)(2,1)}, bf16[2,4,2,64,2048]{4,3,2,1,0:T(8,128)(2,1)}, u32[]{:S(2)}, u32[]{:S(2)}) collective-permute-start(bf16[2,4,2,64,2048]{4,3,2,1,0:T(8,128)(2,1)} %maximum_maximum_fusion), channel_id=1, source_target_pairs={{0,1},{1,0},{2,3},{3,2},{4,5},{5,4},{6,7},{7,6},{8,9},{9,8},{10,11... | collective-permute-start | bytes 12582920 | tf_op jit(solution)/shard_map/ppermute | solution.py:40
  163.9 27.7 %collective-permute-start.6 = (bf16[2,64,256]{2,1,0:T(8,128)(2,1)S(1)}, bf16[2,64,256]{2,1,0:T(8,128)(2,1)S(1)}, u32[]{:S(2)}, u32[]{:S(2)}) collective-permute-start(bf16[2,64,256]{2,1,0:T(8,128)(2,1)S(1)} %bitcast.631), channel_id=1, source_target_pairs={{0,4},{4,8},{8,12},{12,0},{1,5},{5,9},{9,13},{13,1},{2,6},{6,10},{... | collective-permute-start | bytes 196616 | tf_op jit(solution)/shard_map/ppermute | solution.py:65
  191.6 12.6 %collective-permute-start.8 = (bf16[2,64,256]{2,1,0:T(8,128)(2,1)S(1)}, bf16[2,64,256]{2,1,0:T(8,128)(2,1)S(1)}, u32[]{:S(2)}, u32[]{:S(2)}) collective-permute-start(bf16[2,64,256]{2,1,0:T(8,128)(2,1)S(1)} %bitcast.633), channel_id=1, source_target_pairs={{0,12},{4,0},{8,4},{12,8},{1,13},{5,1},{9,5},{13,9},{2,14},{6,2},{... | collective-permute-start | bytes 196616 | tf_op jit(solution)/shard_map/ppermute | solution.py:65
  197.9 16.7 %collective-permute-start.46 = (bf16[64,2048]{1,0:T(8,128)(2,1)}, bf16[64,2048]{1,0:T(8,128)(2,1)}, u32[]{:S(2)}, u32[]{:S(2)}) collective-permute-start(bf16[64,2048]{1,0:T(8,128)(2,1)} %get-tuple-element.1197), channel_id=1, source_target_pairs={{0,16},{16,0},{1,17},{17,1},{2,18},{18,2},{3,19},{19,3},{4,20},{20... | collective-permute-start | bytes 786440 | tf_op jit(solution)/shard_map/ppermute | solution.py:40
  204.2 20.2 %collective-permute-start.48 = (bf16[64,2048]{1,0:T(8,128)(2,1)}, bf16[64,2048]{1,0:T(8,128)(2,1)S(1)}, u32[]{:S(2)}, u32[]{:S(2)}) collective-permute-start(bf16[64,2048]{1,0:T(8,128)(2,1)} %get-tuple-element.1196), channel_id=1, source_target_pairs={{0,2},{2,0},{1,3},{3,1},{4,6},{6,4},{5,7},{7,5},{8,10},{10,8},{9,1... | collective-permute-start | bytes 786440 | tf_op jit(solution)/shard_map/ppermute | solution.py:40
  214.3 50.9 %collective-permute-start.32 = (bf16[2,4,2,64,2048]{4,3,2,1,0:T(8,128)(2,1)}, bf16[2,4,2,64,2048]{4,3,2,1,0:T(8,128)(2,1)}, u32[]{:S(2)}, u32[]{:S(2)}) collective-permute-start(bf16[2,4,2,64,2048]{4,3,2,1,0:T(8,128)(2,1)} %maximum_maximum_fusion.1), channel_id=1, source_target_pairs={{0,1},{1,0},{2,3},{3,2},{4,5},{5,4},{6,7},{7,6},{8,9},{9,8},{10,11... | collective-permute-start | bytes 12582920 | tf_op jit(solution)/shard_map/ppermute | solution.py:40
  215.6 18.8 %collective-permute-start.47 = (bf16[128,2048]{1,0:T(8,128)(2,1)S(1)}, bf16[128,2048]{1,0:T(8,128)(2,1)S(1)}, u32[]{:S(2)}, u32[]{:S(2)}) collective-permute-start(bf16[128,2048]{1,0:T(8,128)(2,1)S(1)} %pad_maximum_fusion.22), channel_id=1, source_target_pairs={{0,2},{2,0},{1,3},{3,1},{4,6},{6,4},{5,7},{7,5},{8,10},{10,8},{9,1... | collective-permute-start | bytes 1572872 | tf_op jit(solution)/shard_map/ppermute | solution.py:40
  224.5 12.7 %collective-permute-start.10 = (bf16[4,2,2,64,256]{4,3,2,0,1:T(8,128)(2,1)}, bf16[4,2,2,64,256]{4,3,2,0,1:T(8,128)(2,1)}, u32[]{:S(2)}, u32[]{:S(2)}) collective-permute-start(bf16[4,2,2,64,256]{4,3,2,0,1:T(8,128)(2,1)} %pad_maximum_fusion.11), channel_id=1, source_target_pairs={{0,1},{1,0},{2,3},{3,2},{4,5},{5,4},{6,7},{7,6},{8,9},{9,8},{10,11... | collective-permute-start | bytes 1572872 | tf_op jit(solution)/shard_map/ppermute | solution.py:40
  225.3 79.4 %collective-permute-start.49 = (bf16[128,2048]{1,0:T(8,128)(2,1)}, bf16[128,2048]{1,0:T(8,128)(2,1)}, u32[]{:S(2)}, u32[]{:S(2)}) collective-permute-start(bf16[128,2048]{1,0:T(8,128)(2,1)} %pad_maximum_fusion.23), channel_id=1, source_target_pairs={{0,16},{16,0},{1,17},{17,1},{2,18},{18,2},{3,19},{19,3},{4,20},{20... | collective-permute-start | bytes 1572872 | tf_op jit(solution)/shard_map/ppermute | solution.py:40
  303.3 12.8 %collective-permute-start.34 = (bf16[128,2048]{1,0:T(8,128)(2,1)S(1)}, bf16[128,2048]{1,0:T(8,128)(2,1)S(1)}, u32[]{:S(2)}, u32[]{:S(2)}) collective-permute-start(bf16[128,2048]{1,0:T(8,128)(2,1)S(1)} %pad_maximum_fusion.20), channel_id=1, source_target_pairs={{0,2},{2,0},{1,3},{3,1},{4,6},{6,4},{5,7},{7,5},{8,10},{10,8},{9,1... | collective-permute-start | bytes 1572872 | tf_op jit(solution)/shard_map/ppermute | solution.py:40
  306.9 30.2 %collective-permute-start.50 = (bf16[512,2048]{1,0:T(8,128)(2,1)}, bf16[512,2048]{1,0:T(8,128)(2,1)}, u32[]{:S(2)}, u32[]{:S(2)}) collective-permute-start(bf16[512,2048]{1,0:T(8,128)(2,1)} %get-tuple-element.1188), channel_id=1, source_target_pairs={{0,1},{1,0},{2,3},{3,2},{4,5},{5,4},{6,7},{7,6},{8,9},{9,8},{10,11... | collective-permute-start | bytes 6291464 | tf_op jit(solution)/shard_map/ppermute | solution.py:40
  324.3 10.8 %collective-permute-start.36 = (bf16[128,2048]{1,0:T(8,128)(2,1)S(1)}, bf16[128,2048]{1,0:T(8,128)(2,1)S(1)}, u32[]{:S(2)}, u32[]{:S(2)}) collective-permute-start(bf16[128,2048]{1,0:T(8,128)(2,1)S(1)} %pad_maximum_fusion.21), channel_id=1, source_target_pairs={{0,16},{16,0},{1,17},{17,1},{2,18},{18,2},{3,19},{19,3},{4,20},{20... | collective-permute-start | bytes 1572872 | tf_op jit(solution)/shard_map/ppermute | solution.py:40
  373.5 17.1 %collective-permute-start.51 = (bf16[512,2048]{1,0:T(8,128)(2,1)}, bf16[512,2048]{1,0:T(8,128)(2,1)}, u32[]{:S(2)}, u32[]{:S(2)}) collective-permute-start(bf16[512,2048]{1,0:T(8,128)(2,1)} %slice.287), channel_id=1, source_target_pairs={{0,1},{1,0},{2,3},{3,2},{4,5},{5,4},{6,7},{7,6},{8,9},{9,8},{10,11... | collective-permute-start | bytes 6291464 | tf_op jit(solution)/shard_map/ppermute | solution.py:40
  381.6 15.7 %collective-permute-start.41 = (bf16[512,2048]{1,0:T(8,128)(2,1)}, bf16[512,2048]{1,0:T(8,128)(2,1)}, u32[]{:S(2)}, u32[]{:S(2)}) collective-permute-start(bf16[512,2048]{1,0:T(8,128)(2,1)} %slice.276), channel_id=1, source_target_pairs={{0,1},{1,0},{2,3},{3,2},{4,5},{5,4},{6,7},{7,6},{8,9},{9,8},{10,11... | collective-permute-start | bytes 6291464 | tf_op jit(solution)/shard_map/ppermute | solution.py:40
  390.6 276.2 %reduce-scatter.5.cloned.1.call-start = ((), (), s32[]{:S(2)}) async-start(), calls=%async_computation.5 | async-start | bytes 5242880 | tf_op jit(solution)/shard_map/reduce_scatter | solution.py:335
  394.9 15.1 %collective-permute-start.52 = (bf16[128,2048]{1,0:T(8,128)(2,1)}, bf16[128,2048]{1,0:T(8,128)(2,1)}, u32[]{:S(2)}, u32[]{:S(2)}) collective-permute-start(bf16[128,2048]{1,0:T(8,128)(2,1)} %get-tuple-element.1139), channel_id=1, source_target_pairs={{0,2},{2,0},{1,3},{3,1},{4,6},{6,4},{5,7},{7,5},{8,10},{10,8},{9,1... | collective-permute-start | bytes 1572872 | tf_op jit(solution)/shard_map/ppermute | solution.py:40
  396.2 15.1 %collective-permute-start.54 = (bf16[128,2048]{1,0:T(8,128)(2,1)}, bf16[128,2048]{1,0:T(8,128)(2,1)}, u32[]{:S(2)}, u32[]{:S(2)}) collective-permute-start(bf16[128,2048]{1,0:T(8,128)(2,1)} %get-tuple-element.1140), channel_id=1, source_target_pairs={{0,16},{16,0},{1,17},{17,1},{2,18},{18,2},{3,19},{19,3},{4,20},{20... | collective-permute-start | bytes 1572872 | tf_op jit(solution)/shard_map/ppermute | solution.py:40
  402.0 19.2 %collective-permute-start.42 = (bf16[128,2048]{1,0:T(8,128)(2,1)}, bf16[128,2048]{1,0:T(8,128)(2,1)}, u32[]{:S(2)}, u32[]{:S(2)}) collective-permute-start(bf16[128,2048]{1,0:T(8,128)(2,1)} %get-tuple-element.1143), channel_id=1, source_target_pairs={{0,2},{2,0},{1,3},{3,1},{4,6},{6,4},{5,7},{7,5},{8,10},{10,8},{9,1... | collective-permute-start | bytes 1572872 | tf_op jit(solution)/shard_map/ppermute | solution.py:40
  402.8 19.8 %collective-permute-start.44 = (bf16[128,2048]{1,0:T(8,128)(2,1)}, bf16[128,2048]{1,0:T(8,128)(2,1)}, u32[]{:S(2)}, u32[]{:S(2)}) collective-permute-start(bf16[128,2048]{1,0:T(8,128)(2,1)} %get-tuple-element.1144), channel_id=1, source_target_pairs={{0,16},{16,0},{1,17},{17,1},{2,18},{18,2},{3,19},{19,3},{4,20},{20... | collective-permute-start | bytes 1572872 | tf_op jit(solution)/shard_map/ppermute | solution.py:40
  413.3 14.8 %collective-permute-start.53 = (bf16[64,2048]{1,0:T(8,128)(2,1)S(1)}, bf16[64,2048]{1,0:T(8,128)(2,1)S(1)}, u32[]{:S(2)}, u32[]{:S(2)}) collective-permute-start(bf16[64,2048]{1,0:T(8,128)(2,1)S(1)} %slice.291), channel_id=1, source_target_pairs={{0,16},{16,0},{1,17},{17,1},{2,18},{18,2},{3,19},{19,3},{4,20},{20... | collective-permute-start | bytes 786440 | tf_op jit(solution)/shard_map/ppermute | solution.py:40
  414.4 13.8 %collective-permute-start.55 = (bf16[64,2048]{1,0:T(8,128)(2,1)S(1)}, bf16[64,2048]{1,0:T(8,128)(2,1)S(1)}, u32[]{:S(2)}, u32[]{:S(2)}) collective-permute-start(bf16[64,2048]{1,0:T(8,128)(2,1)S(1)} %slice.295), channel_id=1, source_target_pairs={{0,2},{2,0},{1,3},{3,1},{4,6},{6,4},{5,7},{7,5},{8,10},{10,8},{9,1... | collective-permute-start | bytes 786440 | tf_op jit(solution)/shard_map/ppermute | solution.py:40
  463.2 11.6 %collective-permute-start.57 = (bf16[2,4,64,256]{3,2,1,0:T(8,128)(2,1)S(1)}, bf16[2,4,64,256]{3,2,1,0:T(8,128)(2,1)S(1)}, u32[]{:S(2)}, u32[]{:S(2)}) collective-permute-start(bf16[2,4,64,256]{3,2,1,0:T(8,128)(2,1)S(1)} %fusion.103), channel_id=1, source_target_pairs={{0,2},{2,0},{1,3},{3,1},{4,6},{6,4},{5,7},{7,5},{8,10},{10,8},{9,1... | collective-permute-start | bytes 786440 | tf_op jit(solution)/shard_map/ppermute | solution.py:40
  475.9 22.9 %collective-permute-start.58 = (bf16[2,64,256]{2,1,0:T(8,128)(2,1)S(1)}, bf16[2,64,256]{2,1,0:T(8,128)(2,1)S(1)}, u32[]{:S(2)}, u32[]{:S(2)}) collective-permute-start(bf16[2,64,256]{2,1,0:T(8,128)(2,1)S(1)} %dynamic-slice_bitcast_fusion.30), channel_id=1, source_target_pairs={{0,4},{4,8},{8,12},{12,0},{1,5},{5,9},{9,13},{13,1},{2,6},{6,10},{... | collective-permute-start | bytes 196616 | tf_op jit(solution)/shard_map/ppermute | solution.py:65
  507.7 11.9 %collective-permute-start.60 = (bf16[2,64,256]{2,1,0:T(8,128)(2,1)S(1)}, bf16[2,64,256]{2,1,0:T(8,128)(2,1)}, u32[]{:S(2)}, u32[]{:S(2)}) collective-permute-start(bf16[2,64,256]{2,1,0:T(8,128)(2,1)S(1)} %fusion.118), channel_id=1, source_target_pairs={{0,4},{4,8},{8,12},{12,0},{1,5},{5,9},{9,13},{13,1},{2,6},{6,10},{... | collective-permute-start | bytes 196616 | tf_op jit(solution)/shard_map/ppermute | solution.py:65
  528.8 14.2 %collective-permute-start.61 = (f32[2,4,2,768]{3,2,1,0:T(2,128)S(1)}, f32[2,4,2,768]{3,2,1,0:T(2,128)S(1)}, u32[]{:S(2)}, u32[]{:S(2)}) collective-permute-start(f32[2,4,2,768]{3,2,1,0:T(2,128)S(1)} %bitcast.651), channel_id=1, source_target_pairs={{0,1},{1,0},{2,3},{3,2},{4,5},{5,4},{6,7},{7,6},{8,9},{9,8},{10,11... | collective-permute-start | bytes 147464 | tf_op jit(solution)/shard_map/ppermute | solution.py:40
  542.5 62.8 %collective-permute-start.89 = (bf16[2,4,2,64,2048]{4,3,1,0,2:T(8,128)(2,1)}, bf16[2,4,2,64,2048]{4,3,1,0,2:T(8,128)(2,1)}, u32[]{:S(2)}, u32[]{:S(2)}) collective-permute-start(bf16[2,4,2,64,2048]{4,3,1,0,2:T(8,128)(2,1)} %bitcast.580), channel_id=1, source_target_pairs={{0,1},{1,0},{2,3},{3,2},{4,5},{5,4},{6,7},{7,6},{8,9},{9,8},{10,11... | collective-permute-start | bytes 12582920 | tf_op jit(solution)/shard_map/ppermute | solution.py:40
  553.8 57.2 %collective-permute-start.67 = (bf16[2,4,2,64,2048]{4,3,1,0,2:T(8,128)(2,1)}, bf16[2,4,2,64,2048]{4,3,1,0,2:T(8,128)(2,1)S(1)}, u32[]{:S(2)}, u32[]{:S(2)}) collective-permute-start(bf16[2,4,2,64,2048]{4,3,1,0,2:T(8,128)(2,1)} %bitcast.581), channel_id=1, source_target_pairs={{0,1},{1,0},{2,3},{3,2},{4,5},{5,4},{6,7},{7,6},{8,9},{9,8},{10,11... | collective-permute-start | bytes 12582920 | tf_op jit(solution)/shard_map/ppermute | solution.py:40
  560.2 14.7 %collective-permute-start.78 = (bf16[2,4,2,64,256]{4,3,1,0,2:T(8,128)(2,1)S(1)}, bf16[2,4,2,64,256]{4,3,1,0,2:T(8,128)(2,1)S(1)}, u32[]{:S(2)}, u32[]{:S(2)}) collective-permute-start(bf16[2,4,2,64,256]{4,3,1,0,2:T(8,128)(2,1)S(1)} %bitcast.627), channel_id=1, source_target_pairs={{0,1},{1,0},{2,3},{3,2},{4,5},{5,4},{6,7},{7,6},{8,9},{9,8},{10,11... | collective-permute-start | bytes 1572872 | tf_op jit(solution)/shard_map/ppermute | solution.py:40
  610.1 26.2 %collective-permute-start.90 = (bf16[4,2,64,1024]{3,2,0,1:T(8,128)(2,1)S(1)}, bf16[4,2,64,1024]{3,2,0,1:T(8,128)(2,1)S(1)}, u32[]{:S(2)}, u32[]{:S(2)}) collective-permute-start(bf16[4,2,64,1024]{3,2,0,1:T(8,128)(2,1)S(1)} %dynamic-slice_bitcast_fusion.13), channel_id=1, source_target_pairs={{0,16},{16,0},{1,17},{17,1},{2,18},{18,2},{3,19},{19,3},{4,20},{20... | collective-permute-start | bytes 3145736 | tf_op jit(solution)/shard_map/ppermute | solution.py:40
  610.4 27.7 %collective-permute-start.95 = (bf16[2,4,64,1024]{3,2,1,0:T(8,128)(2,1)S(1)}, bf16[2,4,64,1024]{3,2,1,0:T(8,128)(2,1)S(1)}, u32[]{:S(2)}, u32[]{:S(2)}) collective-permute-start(bf16[2,4,64,1024]{3,2,1,0:T(8,128)(2,1)S(1)} %dynamic-slice_bitcast_fusion.12), channel_id=1, source_target_pairs={{0,2},{2,0},{1,3},{3,1},{4,6},{6,4},{5,7},{7,5},{8,10},{10,8},{9,1... | collective-permute-start | bytes 3145736 | tf_op jit(solution)/shard_map/ppermute | solution.py:40
  615.1 43.7 %collective-permute-start.68 = (bf16[4,2,64,1024]{3,2,0,1:T(8,128)(2,1)S(1)}, bf16[4,2,64,1024]{3,2,0,1:T(8,128)(2,1)S(1)}, u32[]{:S(2)}, u32[]{:S(2)}) collective-permute-start(bf16[4,2,64,1024]{3,2,0,1:T(8,128)(2,1)S(1)} %dynamic-slice_bitcast_fusion.15), channel_id=1, source_target_pairs={{0,16},{16,0},{1,17},{17,1},{2,18},{18,2},{3,19},{19,3},{4,20},{20... | collective-permute-start | bytes 3145736 | tf_op jit(solution)/shard_map/ppermute | solution.py:40
  616.6 44.0 %collective-permute-start.73 = (bf16[2,4,64,1024]{3,2,1,0:T(8,128)(2,1)S(1)}, bf16[2,4,64,1024]{3,2,1,0:T(8,128)(2,1)S(1)}, u32[]{:S(2)}, u32[]{:S(2)}) collective-permute-start(bf16[2,4,64,1024]{3,2,1,0:T(8,128)(2,1)S(1)} %dynamic-slice_bitcast_fusion.14), channel_id=1, source_target_pairs={{0,2},{2,0},{1,3},{3,1},{4,6},{6,4},{5,7},{7,5},{8,10},{10,8},{9,1... | collective-permute-start | bytes 3145736 | tf_op jit(solution)/shard_map/ppermute | solution.py:40
  637.5 32.1 %collective-permute-start.91 = (bf16[4,64,1024]{2,1,0:T(8,128)(2,1)}, bf16[4,64,1024]{2,1,0:T(8,128)(2,1)}, u32[]{:S(2)}, u32[]{:S(2)}) collective-permute-start(bf16[4,64,1024]{2,1,0:T(8,128)(2,1)} %dynamic-slice_bitcast_fusion.18), channel_id=1, source_target_pairs={{0,2},{2,0},{1,3},{3,1},{4,6},{6,4},{5,7},{7,5},{8,10},{10,8},{9,1... | collective-permute-start | bytes 1572872 | tf_op jit(solution)/shard_map/ppermute | solution.py:40
  639.4 31.7 %collective-permute-start.96 = (bf16[4,64,1024]{2,1,0:T(8,128)(2,1)}, bf16[4,64,1024]{2,1,0:T(8,128)(2,1)}, u32[]{:S(2)}, u32[]{:S(2)}) collective-permute-start(bf16[4,64,1024]{2,1,0:T(8,128)(2,1)} %dynamic-slice_bitcast_fusion.17), channel_id=1, source_target_pairs={{0,16},{16,0},{1,17},{17,1},{2,18},{18,2},{3,19},{19,3},{4,20},{20... | collective-permute-start | bytes 1572872 | tf_op jit(solution)/shard_map/ppermute | solution.py:40
  660.0 12.4 %collective-permute-start.69 = (bf16[4,64,1024]{2,1,0:T(8,128)(2,1)}, bf16[4,64,1024]{2,1,0:T(8,128)(2,1)}, u32[]{:S(2)}, u32[]{:S(2)}) collective-permute-start(bf16[4,64,1024]{2,1,0:T(8,128)(2,1)} %dynamic-slice_bitcast_fusion.20), channel_id=1, source_target_pairs={{0,2},{2,0},{1,3},{3,1},{4,6},{6,4},{5,7},{7,5},{8,10},{10,8},{9,1... | collective-permute-start | bytes 1572872 | tf_op jit(solution)/shard_map/ppermute | solution.py:40
  662.9 14.3 %collective-permute-start.74 = (bf16[4,64,1024]{2,1,0:T(8,128)(2,1)}, bf16[4,64,1024]{2,1,0:T(8,128)(2,1)}, u32[]{:S(2)}, u32[]{:S(2)}) collective-permute-start(bf16[4,64,1024]{2,1,0:T(8,128)(2,1)} %dynamic-slice_bitcast_fusion.19), channel_id=1, source_target_pairs={{0,16},{16,0},{1,17},{17,1},{2,18},{18,2},{3,19},{19,3},{4,20},{20... | collective-permute-start | bytes 1572872 | tf_op jit(solution)/shard_map/ppermute | solution.py:40
  665.0 22.1 %collective-permute-start.100 = (bf16[2,2,64,1024]{3,2,1,0:T(8,128)(2,1)}, bf16[2,2,64,1024]{3,2,1,0:T(8,128)(2,1)}, u32[]{:S(2)}, u32[]{:S(2)}) collective-permute-start(bf16[2,2,64,1024]{3,2,1,0:T(8,128)(2,1)} %dynamic-slice_bitcast_fusion.16), channel_id=1, source_target_pairs={{0,16},{16,0},{1,17},{17,1},{2,18},{18,2},{3,19},{19,3},{4,20},{20... | collective-permute-start | bytes 1572872 | tf_op jit(solution)/shard_map/ppermute | solution.py:40
  688.3 10.9 %collective-permute-start.101 = (bf16[2,64,2,1024]{3,1,2,0:T(8,128)(2,1)S(1)}, bf16[2,64,2,1024]{3,1,2,0:T(8,128)(2,1)S(1)}, u32[]{:S(2)}, u32[]{:S(2)}) collective-permute-start(bf16[2,64,2,1024]{3,1,2,0:T(8,128)(2,1)S(1)} %fusion.75), channel_id=1, source_target_pairs={{0,2},{2,0},{1,3},{3,1},{4,6},{6,4},{5,7},{7,5},{8,10},{10,8},{9,1... | collective-permute-start | bytes 1572872 | tf_op jit(solution)/shard_map/ppermute | solution.py:40
  (137 other events, 1537.5 us)
Sparse Core Ops, SparseCore 0:
  42.8 109.9 all-gather.2
  154.4 84.8 all-gather.4
  390.7 83.8 reduce-scatter.2
  476.8 95.5 reduce-scatter.4

commit v2 on v1

v2 whole, which is shorter than its diff:
```python
import itertools

import jax
import jax.numpy as jnp
from jax import lax
from jax.experimental import pallas as pl
from jax.experimental.pallas import tpu as pltpu
from jax.sharding import Mesh
from jax.sharding import PartitionSpec as P

HEADS = 16
HD = 128

EPS = 1e-05
GELU_C = 0.7978845608028654
MASKED = -1e30
LOG2E = 1.4426950408889634
LOW = jnp.bfloat16
F32 = jnp.float32
SWAP = [(0, 1), (1, 0)]


def layer_norm(values, gain, shift):
    center = values - jnp.mean(values, axis=-1, keepdims=True)
    spread = jnp.mean(center * center, axis=-1, keepdims=True)
    return center * lax.rsqrt(spread + EPS) * gain + shift


def gelu_tanh(values):
    return 0.5 * values * (1.0 + jnp.tanh(GELU_C * (values + 0.044715 * values * values * values)))


def dot(left, right, dims=((1,), (0,))):
    return lax.dot_general(left, right, (dims, ((), ())), preferred_element_type=F32)


def swap(value, axis):
    return lax.ppermute(value, axis, SWAP)


def add_low(own, got):
    return (own.astype(F32) + got.astype(F32)).astype(LOW)


CHIPS = ("x", "y")
LINE = ("z", "c")
PLANE = ("x", "y", "c")
EVERY = ("x", "z", "y", "c")


def exchange(value, axes):
    return lax.all_to_all(value, axes, 0, 0, tiled=True)


def spread(value, axes):
    return exchange(jnp.broadcast_to(value, (lax.axis_size(axes), *value.shape)), axes)


def after(value, *events):
    return lax.optimization_barrier((value, *events))[0]


def hop(value, mask):
    return lax.ppermute(value, CHIPS, [(i, i ^ mask) for i in range(4)])


def pick_blocks(value, order):
    size = value.shape[1] // len(order)
    if size % HD:
        return jnp.concatenate([value[:, i * size : (i + 1) * size] for i in order], axis=1)

    def kernel(in_ref, out_ref):
        for to, i in enumerate(order):
            out_ref[:, to * size : (to + 1) * size] = in_ref[:, i * size : (i + 1) * size]

    shape = jax.ShapeDtypeStruct(value.shape, value.dtype)
    return pl.pallas_call(kernel, out_shape=shape, name="pick_blocks")(value)


def spread_heads(value, planes):
    rows = value.shape[0]

    def kernel(in_ref, out_ref):
        for x, y, c, two in itertools.product((0, 1), repeat=4):
            start = (((x * 2 + c) * 2 + two) * 2 + y) * HD
            piece = in_ref[:, start : start + HD]
            for z in range(planes):
                target = ((x * planes + z) * 2 + y) * 2 + c
                out_ref[target, :, two * HD : (two + 1) * HD] = piece

    shape = jax.ShapeDtypeStruct((8 * planes, rows, 2 * HD), value.dtype)
    return pl.pallas_call(kernel, out_shape=shape, name="spread_heads")(value)


def collect_heads(value, planes):
    rows = value.shape[1]

    def kernel(in_ref, out_ref):
        for x, y, c, two in itertools.product((0, 1), repeat=4):
            start = (((x * 2 + c) * 2 + two) * 2 + y) * HD
            piece = in_ref[(x * 2 + y) * 2 + c, :, two * HD : (two + 1) * HD]
            out_ref[:, start : start + HD] = piece.astype(F32)

    shape = jax.ShapeDtypeStruct((rows, HEADS * HD), F32)
    return pl.pallas_call(kernel, out_shape=shape, name="collect_heads")(value)


def spread_units(value, planes):
    rows, count = value.shape
    hidden = count // (8 * planes)
    if hidden % HD:
        value = value.reshape(rows, 2, planes, 2, 2, hidden).transpose(2, 4, 0, 1, 3, 5)
        return value.reshape(2 * planes, rows, 4 * hidden)

    def kernel(in_ref, out_ref):
        for x, z, y, c in itertools.product((0, 1), range(planes), (0, 1), (0, 1)):
            start = (((x * planes + z) * 2 + y) * 2 + c) * hidden
            to = (x * 2 + y) * hidden
            out_ref[z * 2 + c, :, to : to + hidden] = in_ref[:, start : start + hidden]

    shape = jax.ShapeDtypeStruct((2 * planes, rows, 4 * hidden), value.dtype)
    return pl.pallas_call(kernel, out_shape=shape, name="spread_units")(value)


def collect_units(value, planes):
    _, rows, count = value.shape
    hidden = count // 4
    if hidden % HD:
        value = value.reshape(planes, 2, rows, 2, 2, hidden).transpose(2, 3, 0, 4, 1, 5)
        return value.reshape(rows, -1).astype(F32)

    def kernel(in_ref, out_ref):
        for x, z, y, c in itertools.product((0, 1), range(planes), (0, 1), (0, 1)):
            start = (((x * planes + z) * 2 + y) * 2 + c) * hidden
            at = (x * 2 + y) * hidden
            piece = in_ref[z * 2 + c, :, at : at + hidden]
            out_ref[:, start : start + hidden] = piece.astype(F32)

    shape = jax.ShapeDtypeStruct((rows, 8 * planes * hidden), F32)
    return pl.pallas_call(kernel, out_shape=shape, name="collect_units")(value)


def scatter_sum(value, axes):
    return lax.psum_scatter(value, axes, scatter_dimension=0, tiled=True)


def own_other(value, at):
    core = lax.axis_index("c")
    own = lax.dynamic_index_in_dim(value, core, at, keepdims=False)
    return own, lax.dynamic_index_in_dim(value, 1 - core, at, keepdims=False)


def in_order(own, got, at=0):
    first = lax.axis_index("c") == 0
    return jnp.stack([jnp.where(first, own, got), jnp.where(first, got, own)], axis=at)


def shift_z(value, by):
    count = lax.axis_size("z")
    return lax.ppermute(value, "z", [(i, (i + by) % count) for i in range(count)])


def line(value, pairs):
    return lax.ppermute(value, "z", pairs)


NEAR = [(0, 1), (1, 0), (2, 3), (3, 2)]
FAR = [(0, 2), (2, 0), (1, 3), (3, 1)]
MIDDLE = [(1, 2), (2, 1)]
ACROSS = [(0, 3), (3, 0), (1, 2), (2, 1)]
INWARD = [(0, 1), (3, 2)]
OUTWARD = [(1, 0), (2, 3)]


def gather_line(value):
    count = lax.axis_size("z")
    if count == 4:
        near, far = line(value, NEAR), line(value, FAR)
        middle = line(after(value, far), MIDDLE)
        pieces = [value, near, far, middle + line(far, OUTWARD)]
    else:
        pieces = [value] + [shift_z(value, step) for step in range(1, count)]
    return jnp.concatenate(pieces)


def add_cores(value):
    half = value.shape[0] // 2
    return add_low(value[:half], swap(value[half:], "c"))


def scatter_line_parts(whole):
    count = lax.axis_size("z")
    pieces = jnp.split(whole, count)
    if count == 4:
        inward = line(pieces[3], INWARD)
        middle = line(pieces[3], MIDDLE)
        outer = add_low(pieces[2], inward)

        def final():
            return [pieces[0], line(after(pieces[1], inward), NEAR), middle, line(outer, FAR)]

        return [outer, middle], final
    return [], lambda: [pieces[0]] + [shift_z(pieces[k], -k) for k in range(1, count)]


def scatter_line(value):
    count = lax.axis_size("z")
    pieces = jnp.split(value, count)
    if count == 4:
        got = [line(piece, pairs) for piece, pairs in zip(pieces[1:], (NEAR, FAR, ACROSS))]
    else:
        got = [shift_z(pieces[step], -step) for step in range(1, count)]
    total = pieces[0].astype(F32)
    for piece in got:
        total = total + piece.astype(F32)
    return total


def gather_z_direct(value):
    count = lax.axis_size("z")
    me = lax.axis_index("z")
    held = jnp.stack([value] + [shift_z(value, step) for step in range(1, count)])
    return jnp.stack(
        [lax.dynamic_index_in_dim(held, (me - a) % count, 0, keepdims=False) for a in range(count)]
    )


def gather_chips(value):
    me = lax.axis_index("x") * 2 + lax.axis_index("y")
    held = jnp.stack([value] + [hop(value, mask) for mask in (1, 2, 3)])
    return jnp.stack(
        [lax.dynamic_index_in_dim(held, me ^ a, 0, keepdims=False) for a in range(4)]
    )


def scatter_chips(value):
    pieces = jnp.split(value, 4)
    total = pieces[0].astype(F32)
    for mask in (1, 2, 3):
        total = total + hop(pieces[mask], mask).astype(F32)
    return total


def scatter_plane(value):
    return scatter_chips(add_cores(value))


def visible_keys(key_pos_ref, query_pos_ref, start_ref):
    key_pos = key_pos_ref[...]
    return (key_pos <= query_pos_ref[...]) & (key_pos >= start_ref[0])


def attention_kernel(q_ref, kv_ref, key_pos_ref, query_pos_ref, start_ref, out_ref, lse_ref):
    count = key_pos_ref.shape[0]
    queries = q_ref[...].reshape(-1, q_ref.shape[-1])
    pairs = kv_ref[...].reshape(count, 2 * HD)
    keys = pairs[:, :HD]
    values_t = pairs[:, HD:].T
    seen = visible_keys(key_pos_ref, query_pos_ref, start_ref)
    outs = []
    for head in range(queries.shape[1] // HD):
        scores = dot(keys, queries[:, head * HD : (head + 1) * HD], ((1,), (1,)))
        scores = jnp.where(seen, scores * (HD**-0.5 * LOG2E), MASKED)
        top = jnp.max(scores, axis=0, keepdims=True)
        weights = jnp.exp2(scores - top)
        total = jnp.sum(weights, axis=0, keepdims=True)
        probs = (weights * (1.0 / total)).astype(LOW)
        outs.append(dot(values_t, probs).T)
        lse_ref[0, head] = top + jnp.log2(total)
    out_ref[...] = jnp.concatenate(outs, axis=1).astype(LOW).reshape(out_ref.shape)


def attention_grad_kernel(
    q_ref, grad_ref, kv_ref, lse_ref, key_pos_ref, query_pos_ref, start_ref, dq_ref, dkv_ref
):
    count = key_pos_ref.shape[0]
    queries = q_ref[...].reshape(-1, q_ref.shape[-1])
    grads = grad_ref[...].reshape(-1, q_ref.shape[-1])
    pairs = kv_ref[...].reshape(count, 2 * HD)
    keys, values = pairs[:, :HD], pairs[:, HD:]
    keys_t = keys.T
    seen = visible_keys(key_pos_ref, query_pos_ref, start_ref)
    outs, grad_keys, grad_values = [], None, None
    for head in range(queries.shape[1] // HD):
        query = queries[:, head * HD : (head + 1) * HD]
        grad = grads[:, head * HD : (head + 1) * HD]
        scores = dot(keys, query, ((1,), (1,))) * (HD**-0.5 * LOG2E)
        probs = jnp.where(seen, jnp.exp2(scores - lse_ref[0, head]), 0.0)
        grad_probs = dot(values, grad, ((1,), (1,)))
        weighted = probs * grad_probs
        delta = jnp.sum(weighted, axis=0, keepdims=True)
        grad_scores = (weighted - probs * delta).astype(LOW)
        outs.append(dot(keys_t, grad_scores).T * HD**-0.5)
        keys_part = dot(grad_scores, query) * HD**-0.5
        values_part = dot(probs.astype(LOW), grad)
        grad_keys = keys_part if head == 0 else grad_keys + keys_part
        grad_values = values_part if head == 0 else grad_values + values_part
    dq_ref[...] = jnp.concatenate(outs, axis=1).astype(LOW).reshape(dq_ref.shape)
    dkv = jnp.concatenate([grad_keys, grad_values], axis=1)
    dkv_ref[...] = dkv.astype(LOW).reshape(dkv_ref.shape)


def normed_rows(near, far, gain, shift):
    count, width = near.shape
    block = count // 4

    def kernel(near_ref, far_ref, gain_ref, shift_ref, out_ref):
        def norm(ref):
            values = ref[...].astype(F32)
            out_ref[...] = layer_norm(values, gain_ref[...], shift_ref[...]).astype(LOW)

        first = pl.program_id(0) < 4
        pl.when(first)(lambda: norm(near_ref))
        pl.when(jnp.logical_not(first))(lambda: norm(far_ref))

    return pl.pallas_call(
        kernel,
        grid=(8,),
        in_specs=[
            pl.BlockSpec((block, width), lambda i: (jnp.minimum(i, 3), 0)),
            pl.BlockSpec((block, width), lambda i: (jnp.maximum(i - 4, 0), 0)),
            pl.BlockSpec((1, width), lambda i: (0, 0)),
            pl.BlockSpec((1, width), lambda i: (0, 0)),
        ],
        out_specs=pl.BlockSpec((block, width), lambda i: (i, 0)),
        out_shape=jax.ShapeDtypeStruct((2 * count, width), LOW),
        name="normed_rows",
    )(near, far, gain[None], shift[None])


def hidden_units(near, far, grad_near, grad_far, up_w, bias, down_w):
    count, width = near.shape
    units = up_w.shape[1]
    lanes = min(units, 256)

    def kernel(
        near_ref, far_ref, grad_near_ref, grad_far_ref, up_ref, bias_ref, down_ref,
        act_ref, pre_ref, sum_ref
    ):
        sums = jnp.zeros((1, lanes), F32)
        for side, (rows_ref, grads_ref) in enumerate(
            ((near_ref, grad_near_ref), (far_ref, grad_far_ref))
        ):
            at = slice(side * count, (side + 1) * count)
            value = dot(rows_ref[...], up_ref[...]) + bias_ref[...]
            grad = dot(grads_ref[...], down_ref[...], ((1,), (1,)))
            square = value * value
            bend = jnp.tanh(GELU_C * value * (1.0 + 0.044715 * square))
            upper = 0.5 * (1.0 + bend)
            act_ref[at, :] = (value * upper).astype(LOW)
            inner = GELU_C * (1.0 + 3 * 0.044715 * square)
            slope = upper + 0.5 * value * (1.0 - bend * bend) * inner
            low = (grad * slope).astype(LOW)
            pre_ref[at, :] = low
            sums = sums + jnp.sum(low.astype(F32), axis=0, keepdims=True)
        sum_ref[...] = sums

    once = pl.Buffered(1)
    tall = pl.BlockSpec((count, width), lambda j: (0, 0), pipeline_mode=once)
    out = pl.BlockSpec((2 * count, lanes), lambda j: (0, j))
    thin = pl.BlockSpec((1, lanes), lambda j: (0, j))
    return pl.pallas_call(
        kernel,
        grid=(units // lanes,),
        in_specs=[tall, tall, tall, tall]
        + [
            pl.BlockSpec((width, lanes), lambda j: (0, j)),
            thin,
            pl.BlockSpec((lanes, width), lambda j: (j, 0)),
        ],
        out_specs=[out, out, thin],
        out_shape=[
            jax.ShapeDtypeStruct((2 * count, units), LOW),
            jax.ShapeDtypeStruct((2 * count, units), LOW),
            jax.ShapeDtypeStruct((1, units), F32),
        ],
        compiler_params=pltpu.CompilerParams(**PARAMS),
        cost_estimate=pl.CostEstimate(
            flops=8 * count * width * units,
            bytes_accessed=8 * count * width + 4 * width * units + 8 * count * units,
            transcendentals=2 * count * units,
        ),
        name="hidden_units",
    )(near, far, grad_near, grad_far, up_w, bias[None], down_w)


def attention_specs(rows, planes, width):
    query = pl.BlockSpec((2, 1, 2, 1, rows, width), lambda i, j: (0, i, 0, j, 0, 0))
    pairs = pl.BlockSpec(
        (2, 1, 2, planes, 1, rows, 2 * HD), lambda i, j: (0, i, 0, 0, j, 0, 0)
    )
    key_pos = pl.BlockSpec((4 * planes * rows, 1), lambda i, j: (0, 0))
    query_pos = pl.BlockSpec((1, 4 * rows), lambda i, j: (0, 0))
    start = pl.BlockSpec((1, 1, 4 * rows), lambda i, j: (2 * i + j, 0, 0))
    lse = pl.BlockSpec((1, width // HD, 1, 4 * rows), lambda i, j: (2 * i + j, 0, 0, 0))
    return query, pairs, key_pos, query_pos, start, lse


PARAMS = dict(vmem_limit_bytes=60 * 2**20)


def attention(queries, pairs, key_pos, query_pos, starts):
    rows, width = queries.shape[-2:]
    planes = pairs.shape[3]
    query, pair, kpos, qpos, start, lse = attention_specs(rows, planes, width)
    area = 4 * 4 * rows * 4 * planes * rows * (width // HD)
    return pl.pallas_call(
        attention_kernel,
        grid=(2, 2),
        in_specs=[query, pair, kpos, qpos, start],
        out_specs=[query, lse],
        out_shape=[
            jax.ShapeDtypeStruct(queries.shape, LOW),
            jax.ShapeDtypeStruct((4, width // HD, 1, 4 * rows), F32),
        ],
        compiler_params=pltpu.CompilerParams(**PARAMS),
        cost_estimate=pl.CostEstimate(
            flops=4 * area * HD, bytes_accessed=pairs.size * 2 + queries.size * 4, transcendentals=area
        ),
        name="attention",
    )(queries, pairs, key_pos, query_pos, starts)


def attention_grad(queries, grads, pairs, lses, key_pos, query_pos, starts):
    rows, width = queries.shape[-2:]
    planes = pairs.shape[3]
    query, pair, kpos, qpos, start, lse = attention_specs(rows, planes, width)
    area = 4 * 4 * rows * 4 * planes * rows * (width // HD)
    return pl.pallas_call(
        attention_grad_kernel,
        grid=(2, 2),
        in_specs=[query, query, pair, lse, kpos, qpos, start],
        out_specs=[query, pair],
        out_shape=[
            jax.ShapeDtypeStruct(queries.shape, LOW),
            jax.ShapeDtypeStruct(pairs.shape, LOW),
        ],
        compiler_params=pltpu.CompilerParams(**PARAMS),
        cost_estimate=pl.CostEstimate(
            flops=area, bytes_accessed=queries.size, transcendentals=0
        ),
        name="attention_grad",
    )(queries, grads, pairs, lses, key_pos, query_pos, starts)


def local(
    tokens,
    doc_lengths,
    ln1_gain,
    ln1_shift,
    q_weight,
    q_bias,
    kv_weight,
    v_bias,
    o_weight,
    o_bias,
    ln2_gain,
    ln2_shift,
    fc_weight,
    fc_bias,
    proj_weight,
    proj_bias,
    cotangent,
):
    seqs_here, span_rows, width = tokens.shape
    row_count = seqs_here * span_rows
    planes = lax.axis_size("z")
    devices = 8 * planes
    rows = q_weight.shape[0]
    hidden = proj_weight.shape[0]
    at_x, at_z, at_y, at_c = (lax.axis_index(name) for name in ("x", "z", "y", "c"))

    small = (ln1_gain, ln1_shift, q_bias, o_bias, ln2_gain, ln2_shift, proj_bias)
    lengths = doc_lengths.reshape(-1)
    lanes = kv_weight.shape[1]
    tail = jnp.concatenate([v_bias, (lengths // 256).astype(LOW), (lengths % 256).astype(LOW)])
    lines = [jnp.pad(jnp.stack(small), ((0, 0), (0, lanes - rows)))]
    for piece in (fc_bias, tail):
        lines.append(jnp.pad(piece, (0, lanes - piece.shape[0]))[None])
    lines.append(jnp.zeros((16 - len(small) - 2, lanes), LOW))
    flat = jnp.concatenate(lines)
    packed = gather_z_direct(jnp.concatenate([kv_weight, flat]))
    packed = gather_chips(packed)
    packed = in_order(packed, swap(packed, "c"), 2)
    packed = packed.reshape(2, 2, *packed.shape[1:]).transpose(0, 2, 1, 3, 4, 5)
    pair_w = packed[..., :rows, :].reshape(width, lanes)
    flat = packed[..., rows:, :].reshape(devices, 16, lanes)
    parts = flat[:, : len(small), :rows].transpose(1, 0, 2).reshape(len(small), width).astype(F32)
    gain_one, shift_one, query_b, out_b, gain_two, shift_two, down_b = parts
    up_b = flat[:, len(small), :hidden].reshape(2, planes, 2, 2, hidden).astype(F32)
    up_b = lax.dynamic_slice(
        up_b, (0, at_z, 0, at_c, 0), (2, 1, 2, 1, hidden)
    ).reshape(-1)
    flat = flat[:, len(small) + 1]
    ends = v_bias.shape[0]
    value_b = flat[:, :ends].reshape(-1).astype(F32)
    lengths = flat[:: devices // 2, ends:].astype(jnp.int32)
    count = doc_lengths.size
    lengths = (lengths[:, :count] * 256 + lengths[:, count : 2 * count]).reshape(-1, doc_lengths.shape[1])

    up_own = exchange(spread_units(fc_weight, planes), LINE)
    own_q = after(spread_heads(q_weight, planes), up_own)
    query_w = exchange(own_q, EVERY).reshape(width, 2 * HD)
    query_b = lax.dynamic_slice(
        query_b.reshape(2, 2, 2, 2, HD), (at_x, at_c, 0, at_y, 0), (1, 1, 2, 1, HD)
    ).reshape(-1)
    whole_heads = planes == 4 and 2 * rows == HD
    if whole_heads:
        out_w = lax.all_gather(o_weight, "z", axis=0, tiled=True)
        own, other = own_other(out_w.reshape(2, 2, rows, width), 0)
        out_w = in_order(own, swap(other, "c"), 1).reshape(2 * HD, width)
    else:
        out_w = lax.all_gather(o_weight, EVERY, axis=0, tiled=True)
        out_w = lax.dynamic_slice(
            out_w.reshape(2, 2, 2, 2, HD, width),
            (at_x, at_c, 0, at_y, 0, 0),
            (1, 1, 2, 1, HD, width),
        ).reshape(2 * HD, width)

    up_w = lax.all_gather(up_own.reshape(-1, 4 * hidden), CHIPS, axis=0, tiled=True)
    down_w = lax.all_gather(proj_weight, CHIPS, axis=0, tiled=True)

    def features_out(value):
        order = [(x * planes + z) * 2 + y for x in (0, 1) for y in (0, 1) for z in range(planes)]
        return pick_blocks(value, order)

    def features_back(value):
        order = [(x * 2 + y) * planes + z for x in (0, 1) for z in range(planes) for y in (0, 1)]
        return pick_blocks(value, order)

    tokens_own = tokens.reshape(row_count, width)
    inputs_float = tokens_own.astype(F32)
    steps = jnp.arange(2, dtype=jnp.int32)
    within = jnp.arange(span_rows, dtype=jnp.int32)
    depth = (at_z - jnp.arange(planes, dtype=jnp.int32)) % planes
    core_part = (steps ^ at_c) * span_rows
    row_part = (steps ^ at_y) * (2 * span_rows)
    key_pos = (
        core_part[:, None, None, None]
        + row_part[None, :, None, None]
        + depth[None, None, :, None] * (4 * span_rows)
        + within
    ).reshape(-1, 1)
    query_pos = (
        core_part[:, None, None] + row_part[None, :, None] + at_z * (4 * span_rows) + within
    ).reshape(1, -1)
    starts = jnp.zeros((2 * seqs_here, query_pos.shape[1]), jnp.int32)
    for j in range(lengths.shape[1]):
        doc_end = jnp.sum(lengths[:, : j + 1], axis=1, keepdims=True)
        starts = jnp.where(query_pos >= doc_end, jnp.maximum(starts, doc_end), starts)
    starts = jnp.where(at_x == 0, starts, jnp.roll(starts, seqs_here, axis=0))[:, None, :]

    grad_out = cotangent.reshape(row_count, width)
    tokens_near = jnp.concatenate([tokens_own] + [hop(tokens_own, mask) for mask in (1, 2, 3)])
    normed_one_plane = normed_rows(tokens_near, swap(tokens_near, "c"), gain_one, shift_one)
    normed_one_f, norm_pull_one = jax.vjp(layer_norm, inputs_float, gain_one, shift_one)
    normed_one = normed_one_f.astype(LOW)
    pair_shift = jnp.concatenate([jnp.zeros((HD,), F32), value_b])
    pairs = (dot(normed_one, pair_w) + pair_shift).astype(LOW)
    pairs = pairs.reshape(seqs_here, span_rows, 2 * HD)
    pairs = jnp.stack([pairs] + [shift_z(pairs, step) for step in range(1, planes)])
    pairs, normed_one_plane = lax.optimization_barrier((pairs, normed_one_plane))
    pairs = jnp.stack([pairs] + [hop(pairs, mask) for mask in (1, 2, 3)])
    pairs = jnp.stack([pairs, swap(pairs, "c")])
    pairs = pairs.reshape(2, 2, 2, *pairs.shape[2:])

    plane_shape = (2, 2, 2, 2, span_rows, 2 * HD)
    queries = (dot(normed_one_plane, query_w) + query_b).astype(LOW).reshape(plane_shape)
    attn_low, lses = attention(queries, pairs, key_pos, query_pos, starts)
    attn_low = attn_low.reshape(-1, 2 * HD)
    resid = inputs_float + scatter_plane(dot(attn_low, out_w).astype(LOW)) + out_b

    grad_near = gather_line(after(grad_out, attn_low))
    grad_far = swap(grad_near, "c")
    normed_two_f, norm_pull_two = jax.vjp(layer_norm, resid, gain_two, shift_two)
    near = gather_line(features_out(normed_two_f.astype(LOW)))
    far = swap(near, "c")
    activation, grad_pre, grad_up_b = hidden_units(
        near, far, grad_near, grad_far, up_w, up_b, down_w
    )
    grad_normed_two = dot(grad_pre, up_w, ((1,), (1,))).astype(LOW)
    grad_normed_two = add_cores(grad_normed_two)
    grad_pre = after(grad_pre, grad_normed_two)
    grad_up_part = dot(jnp.concatenate([near, far]), grad_pre, ((0,), (0,))).astype(LOW)
    grad_up_w = scatter_sum(grad_up_part, CHIPS).reshape(2 * planes, rows, 4 * hidden)
    activation = after(activation, grad_up_part, grad_normed_two)
    grad_out_line = jnp.concatenate([grad_near, grad_far])
    grad_down_part = dot(activation, grad_out_line, ((0,), (0,))).astype(LOW)
    result = add_cores(dot(activation, down_w).astype(LOW))
    grad_normed_two = after(scatter_line(grad_normed_two), grad_down_part, result)
    grad_normed_two = features_back(grad_normed_two)
    grad_down_b = jnp.sum(grad_out.astype(F32), axis=0)

    grad_resid_part, grad_gain_two, grad_shift_two = norm_pull_two(grad_normed_two)
    grad_resid = grad_out.astype(F32) + grad_resid_part
    grad_proj = grad_resid.astype(LOW)

    inner, final = scatter_line_parts(after(result, grad_proj))
    grad_proj_plane = jnp.concatenate([grad_proj] + [hop(grad_proj, mask) for mask in (1, 2, 3)])
    grad_proj_plane = after(grad_proj_plane, *inner)
    grad_proj_plane = jnp.concatenate([grad_proj_plane, swap(grad_proj_plane, "c")])
    grad_down_w = scatter_sum(after(grad_down_part, grad_up_w), CHIPS).astype(F32)
    result = final()
    grad_heads = dot(grad_proj_plane, out_w, ((1,), (1,))).astype(LOW).reshape(plane_shape)
    grad_out_b = jnp.sum(grad_proj.astype(F32), axis=0)
    query_grad, grad_pairs = attention_grad(
        queries, grad_heads, pairs, lses, key_pos, query_pos, starts
    )
    query_grad = query_grad.reshape(-1, 2 * HD)
    grad_normed_one = dot(query_grad, query_w, ((1,), (1,))).astype(LOW)
    grad_pairs = add_low(grad_pairs[0], swap(grad_pairs[1], "c"))
    grad_pairs = after(grad_pairs, grad_down_w)
    grad_pairs, grad_normed_one = lax.optimization_barrier((grad_pairs, grad_normed_one))
    grad_total = grad_pairs[0, 0].astype(F32)
    for mask in (1, 2, 3):
        grad_total = grad_total + hop(grad_pairs[mask >> 1, mask & 1], mask).astype(F32)
    grad_up_w = exchange(grad_up_w, LINE)
    grad_total = after(grad_total, grad_up_w)
    output = (resid + sum(part.astype(F32) for part in result) + down_b).astype(LOW)
    grad_normed_one = add_cores(grad_normed_one)
    grad_normed_one = scatter_chips(grad_normed_one)
    grad_query_w = dot(normed_one_plane, after(query_grad, grad_total), ((0,), (0,))).astype(LOW)
    grad_query_w = lax.psum_scatter(
        grad_query_w.reshape(2, planes * 4 * rows, 2 * HD), "z", scatter_dimension=1, tiled=True
    )
    grad_pairs = after(grad_total.astype(LOW), grad_normed_one, *result)
    own_pairs = grad_pairs[0].astype(F32)
    for step in range(1, planes):
        own_pairs = own_pairs + shift_z(grad_pairs[step], -step).astype(F32)
    own_pairs = own_pairs.astype(LOW).reshape(row_count, 2 * HD)
    grad_query_b = jnp.sum(query_grad.astype(F32), axis=0)
    grad_out_w = dot(attn_low, after(grad_proj_plane, grad_normed_one), ((0,), (0,))).astype(LOW)
    if whole_heads:
        own, other = own_other(grad_out_w.reshape(2, 2, rows, width), 1)
        grad_out_w = in_order(own, swap(other, "c"), 0).reshape(planes * rows, width)
        grad_out_w = lax.psum_scatter(grad_out_w, "z", scatter_dimension=0, tiled=True).astype(F32)
    else:
        placed = lax.dynamic_update_slice(
            jnp.zeros((2, 2, 2, 2, HD, width), LOW),
            grad_out_w.reshape(1, 1, 2, 1, HD, width),
            (at_x, at_c, 0, at_y, 0, 0),
        ).reshape(width, width)
        grad_out_w = lax.psum_scatter(
            placed, EVERY, scatter_dimension=0, tiled=True
        ).astype(F32)
    grad_pair_w = dot(normed_one, own_pairs, ((0,), (0,))).astype(LOW)
    grad_value_b = jnp.sum(own_pairs[:, HD:].astype(F32), axis=0)
    grad_normed_one = grad_normed_one + dot(own_pairs, pair_w, ((1,), (1,)))
    grad_input_part, grad_gain_one, grad_shift_one = norm_pull_one(grad_normed_one)
    input_grad = grad_resid + grad_input_part

    grad_query_whole = lax.dynamic_update_slice(
        jnp.zeros((2, 2, 2, 2, HD), F32),
        grad_query_b.reshape(1, 1, 2, 1, HD),
        (at_x, at_c, 0, at_y, 0),
    ).reshape(-1)
    grad_up_whole = lax.dynamic_update_slice(
        jnp.zeros((2, planes, 2, 2, hidden), F32),
        grad_up_b.reshape(2, 1, 2, 1, hidden),
        (0, at_z, 0, at_c, 0),
    ).reshape(-1)
    vectors = (
        grad_gain_one,
        grad_shift_one,
        grad_query_whole,
        grad_out_b,
        grad_gain_two,
        grad_shift_two,
        grad_down_b,
        grad_up_whole,
        grad_value_b,
    )
    shares = [vector.reshape(devices, -1) for vector in vectors]
    lines = [jnp.pad(share, ((0, 0), (0, lanes - share.shape[1]))) for share in shares]
    flat = jnp.pad(jnp.stack(lines, axis=1), ((0, 0), (0, 16 - len(lines)), (0, 0))).astype(LOW)
    flat = jnp.concatenate([grad_pair_w.reshape(devices, rows, 2 * HD), flat], axis=1)
    flat = exchange(flat, EVERY)
    grad_query_w = exchange(after(grad_query_w.reshape(8, rows, 2 * HD), flat), PLANE)
    grad_query_w = collect_heads(grad_query_w, planes)
    flat = jnp.sum(flat.astype(F32), axis=0)
    grad_up_w = collect_units(grad_up_w, planes)
    grad_pair_w = flat[:rows]
    sums = [flat[rows + i, : share.shape[1]] for i, share in enumerate(shares)]
    return (
        output.reshape(seqs_here, span_rows, width),
        input_grad.reshape(seqs_here, span_rows, width),
        sums[0],
        sums[1],
        grad_query_w,
        sums[2],
        grad_pair_w,
        sums[8],
        grad_out_w,
        sums[3],
        sums[4],
        sums[5],
        grad_up_w,
        sums[7],
        grad_down_w,
        sums[6],
    )


def solution(mesh):
    span = mesh.shape["span"]
    fine = Mesh(mesh.devices.reshape(2, span // 4, 2, 2), ("x", "z", "y", "c"))
    every = ("x", "z", "y", "c")
    acts = P("x", ("z", "y", "c"), None)
    vector = P(every)
    matrix = P(every, None)
    return jax.shard_map(
        local,
        mesh=fine,
        in_specs=(
            acts,
            P("x", None),
            vector,
            vector,
            matrix,
            vector,
            matrix,
            vector,
            matrix,
            vector,
            vector,
            vector,
            matrix,
            vector,
            matrix,
            vector,
            acts,
        ),
        out_specs=(
            acts,
            acts,
            vector,
            vector,
            matrix,
            vector,
            matrix,
            vector,
            matrix,
            vector,
            vector,
            vector,
            matrix,
            vector,
            matrix,
            vector,
        ),
        check_vma=False,
    )
```

time: 724 us -> 578 us (0.80)
  Pallas kernels: 0 us -> 58.8 us
  local copies, waits for them, and re-layouts: 104 us -> 49.3 us
  starting transfers between devices: 142 us -> 92.6 us
  matrix products: 97.2 us -> 52.2 us
  other arithmetic: 101 us -> 66 us
  waiting for transfers between devices: 254 us -> 233 us
    ppermute x61 -> x13, waiting for transfers between devices: 161 us -> 8.24 us  [swap(): return lax.ppermute(value, axis, SWAP)]
    ppermute x0 -> x36, waiting for transfers between devices: none -> 129 us  [the longest x21 80.5 us: hop(): return lax.ppermute(value, CHIPS, [(i, i ^ mask) for i in range(4)])]
    ppermute x42 -> x9, waiting for transfers between devices: 93.1 us -> 12.5 us  [shift_z(): lax.ppermute(value, 'z', [(i, (i + by) % count) for i in range(count)])]
    ppermute x42 -> x9, starting transfers between devices: 92.1 us -> 14.5 us  [shift_z(): lax.ppermute(value, 'z', [(i, (i + by) % count) for i in range(count)])]
    pallas_call x0 -> x10, Pallas kernels: none -> 58.8 us  [the longest x1 16.8 us: hidden_units(): pl.pallas_call(kernel, grid=(units // lanes,), in_specs=[tall, tall, tall...]
    ppermute x0 -> x36, starting transfers between devices: none -> 56.8 us  [the longest x15 32.4 us: line(): return lax.ppermute(value, 'z', pairs)]
    all_to_all x0 -> x5, waiting for transfers between devices: none -> 53.7 us  [exchange(): return lax.all_to_all(value, axes, 0, 0, tiled=True)]
    ppermute x61 -> x13, starting transfers between devices: 49.7 us -> 1.76 us  [swap(): return lax.ppermute(value, axis, SWAP)]
  transfers between devices with their start and end apart: 107 -> 70, of which waited for: 55 -> 30; matrix products, arithmetic and copies ran while one was open for 37% -> 24% of each run, Pallas kernels for 0% -> 7%
where the time goes in v2:
time: 578 us; the launch traced here: 568 us
  waiting for transfers between devices  233 us (40%)
  starting transfers between devices  92.6 us (16%)
  other arithmetic  66 us (11%)
  Pallas kernels  58.8 us (10%)
  matrix products  52.2 us (9%)
  local copies, waits for them, and re-layouts  49.3 us (9%)
  between operations  15.8 us (3%)
    ppermute x21, waiting for transfers between devices, hop(): return lax.ppermute(value, CHIPS, [(i, i ^ mask) for i in range(4)])  80.5 us
    all_to_all x5, waiting for transfers between devices, exchange(): return lax.all_to_all(value, axes, 0, 0, tiled=True)  53.7 us
    dot_general x13, matrix products, dot(): lax.dot_general(left, right, (dims, ((), ())), preferred_element_type=F32)  52.2 us
    ppermute x15, waiting for transfers between devices, line(): return lax.ppermute(value, 'z', pairs)  48.8 us
    ppermute x15, starting transfers between devices, line(): return lax.ppermute(value, 'z', pairs)  32.4 us
    reduce_scatter x2, waiting for transfers between devices, scatter_sum(): return lax.psum_scatter(value, axes, scatter_dimension=0, tiled=True)  27.7 us
    ppermute x21, starting transfers between devices, hop(): return lax.ppermute(value, CHIPS, [(i, i ^ mask) for i in range(4)])  24.4 us
    all_to_all x5, starting transfers between devices, exchange(): return lax.all_to_all(value, axes, 0, 0, tiled=True)  18.6 us
  transfers between devices with their start and end apart: 70, of which 30 were waited for; matrix products, arithmetic and copies ran while one was open for 24% of the time, Pallas kernels for 7%

profile of v2, /device:TPU:0, one launch (start us, length us, event | category | flops | bytes accessed | tf_op | source)
XLA Modules:
  0.0 567.6 jit_solution(18082118990533631809)
XLA Ops:
  11.7 4.1 collective-permute-start.1
  20.8 2.3 spread_units.1
  23.1 4.4 all-to-all-start
  29.8 2.4 collective-permute-start.5
  32.5 2.9 collective-permute-done.3
  36.8 4.0 collective-permute-done.5
  46.6 4.8 collective-permute-done.12
  51.4 2.7 pad_maximum_fusion.near_ref
  59.0 2.4 collective-permute-start.8
  63.3 2.7 all-to-all-done
  66.0 2.7 all-to-all-start.1
  77.7 8.1 %normed_rows.1 = bf16[1024,2048]{1,0:T(8,128)(2,1)} custom-call(bf16[512,2048]{1,0:T(8,128)(2,1)} %pad_maximum_fusion.near_ref, bf16[512,2048]{1,0:T(8,128)(2,1)} %collective-permute-done.13.far_ref, f32[1,2048]{1,0:T(1,128)} %unstack.27.gain_ref, f32[1,2048]{1,0:T(1,128)} %unstack.28.shift_ref), custom_call_target="tpu_custom_call" | custom-call | tf_op jit(solution)/shard_map/normed_rows/pallas_call | solution.py:316
  90.1 7.5 %collective-permute-done.14 = bf16[4,2,64,256]{3,2,1,0:T(8,128)(2,1)S(1)} collective-permute-done((bf16[4,2,64,256]{3,2,1,0:T(8,128)(2,1)S(1)}, bf16[4,2,64,256]{3,2,1,0:T(8,128)(2,1)S(1)}, u32[]{:S(2)}, u32[]{:S(2)}) %collective-permute-start.14) | collective-permute-done | bytes 262176 | tf_op jit(solution)/shard_map/ppermute | solution.py:64
  97.6 2.8 collective-permute-done.15
  100.4 10.6 %collective-permute-done.16 = bf16[4,2,64,256]{3,2,1,0:T(8,128)(2,1)S(1)} collective-permute-done((bf16[4,2,64,256]{3,2,1,0:T(8,128)(2,1)S(1)}, bf16[4,2,64,256]{3,2,1,0:T(8,128)(2,1)S(1)}, u32[]{:S(2)}, u32[]{:S(2)}) %collective-permute-start.16) | collective-permute-done | bytes 262176 | tf_op jit(solution)/shard_map/ppermute | solution.py:64
  114.4 4.6 fusion.7
  119.0 3.1 pad_maximum_fusion.1.kv_ref
  122.1 9.8 %attention.1 = (bf16[2,2,2,2,64,256]{5,4,3,2,1,0:T(8,128)(2,1)}, f32[4,2,1,256]{3,2,1,0:T(1,128)}) custom-call(bf16[2,2,2,2,64,256]{5,4,3,2,1,0:T(8,128)(2,1)} %bitcast.229, bf16[2,2,2,4,2,64,256]{6,5,4,3,2,1,0:T(8,128)(2,1)} %pad_maximum_fusion.1.kv_ref, s32[1024,1]{1,0:T(8,128)} %add.499.key_pos_ref, s32[1,256]{1,0:T(1,128)} %add.452.query_pos_ref, ...), custom_call_target="tpu_custom_call" | custom-call | flops 1073741824 | bytes 3145728 | tf_op jit(solution)/shard_map/attention/pallas_call | solution.py:407
  131.8 2.6 convolution_convert_fusion.1
  142.6 3.0 add_convert_fusion.3
  149.8 15.7 %collective-permute-done.29 = bf16[128,2048]{1,0:T(8,128)(2,1)} collective-permute-done((bf16[128,2048]{1,0:T(8,128)(2,1)S(1)}, bf16[128,2048]{1,0:T(8,128)(2,1)}, u32[]{:S(2)}, u32[]{:S(2)}) %collective-permute-start.29) | collective-permute-done | bytes 524320 | tf_op jit(solution)/shard_map/ppermute | solution.py:164
  172.4 11.9 %collective-permute-done.22 = bf16[128,2048]{1,0:T(8,128)(2,1)S(1)} collective-permute-done((bf16[128,2048]{1,0:T(8,128)(2,1)S(1)}, bf16[128,2048]{1,0:T(8,128)(2,1)S(1)}, u32[]{:S(2)}, u32[]{:S(2)}) %collective-permute-start.22) | collective-permute-done | bytes 524320 | tf_op jit(solution)/shard_map/ppermute | solution.py:64
  190.3 2.2 constant_dynamic-update-slice_fusion.6
  192.5 2.7 pad_maximum_fusion.3.grad_near_ref
  195.2 18.7 %collective-permute-done.24 = bf16[128,2048]{1,0:T(8,128)(2,1)S(1)} collective-permute-done((bf16[128,2048]{1,0:T(8,128)(2,1)}, bf16[128,2048]{1,0:T(8,128)(2,1)S(1)}, u32[]{:S(2)}, u32[]{:S(2)}) %collective-permute-start.24) | collective-permute-done | bytes 524320 | tf_op jit(solution)/shard_map/ppermute | solution.py:164
  216.1 14.2 %collective-permute-done.26 = bf16[128,2048]{1,0:T(8,128)(2,1)S(1)} collective-permute-done((bf16[128,2048]{1,0:T(8,128)(2,1)S(1)}, bf16[128,2048]{1,0:T(8,128)(2,1)S(1)}, u32[]{:S(2)}, u32[]{:S(2)}) %collective-permute-start.26) | collective-permute-done | bytes 524320 | tf_op jit(solution)/shard_map/ppermute | solution.py:164
  235.7 2.8 collective-permute-done.27.far_ref
  238.5 16.8 %hidden_units.1 = (bf16[1024,1024]{1,0:T(8,128)(2,1)}, bf16[1024,1024]{1,0:T(8,128)(2,1)}, f32[1,1024]{1,0:T(1,128)}) custom-call(bf16[512,2048]{1,0:T(8,128)(2,1)} %pad_maximum_fusion.2.near_ref, bf16[512,2048]{1,0:T(8,128)(2,1)} %collective-permute-done.27.far_ref, bf16[512,2048]{1,0:T(8,128)(2,1)} %pad_maximum_fusion.3.grad_near_ref, ...), custom_call_target="tpu_custom_call" | custom-call | flops 8589934592 | bytes 20971520 | tf_op jit(solution)/shard_map/hidden_units/pallas_call | solution.py:362
  255.3 7.3 %convolution_convert_fusion.5 = bf16[1024,2048]{1,0:T(8,128)(2,1)S(1)} fusion(bf16[1024,1024]{1,0:T(8,128)(2,1)} %get-tuple-element.53, bf16[2048,1024]{1,0:T(8,128)(2,1)} %all-gather.6.cloned.1.call-done.up_ref), kind=kOutput, calls=%fused_computation.9 | convolution fusion | flops 4297064448 | bytes 10485760 | tf_op jit(solution)/shard_map/dot_general | solution.py:34
  269.2 6.2 %convolution_convert_fusion.4 = bf16[2048,1024]{1,0:T(8,128)(2,1)} fusion(bf16[1024,2048]{1,0:T(8,128)(2,1)S(1)} %constant_dynamic-update-slice_fusion, bf16[1024,1024]{1,0:T(8,128)(2,1)S(1)} %copy-done.51), kind=kOutput, calls=%fused_computation.8 | convolution fusion | flops 4297064448 | bytes 10485760 | tf_op jit(solution)/shard_map/dot_general | solution.py:34
  275.6 7.5 %convolution_convert_fusion.3 = bf16[1024,2048]{1,0:T(8,128)(2,1)S(1)} fusion(bf16[1024,1024]{1,0:T(8,128)(2,1)} %get-tuple-element.54, bf16[1024,2048]{1,0:T(8,128)(2,1)} %all-gather.8.cloned.1.call-done.down_ref), kind=kOutput, calls=%fused_computation.7 | convolution fusion | flops 4297064448 | bytes 10485760 | tf_op jit(solution)/shard_map/dot_general | solution.py:34
  284.7 3.2 constant_dynamic-update-slice_fusion.5
  290.8 2.7 collective-permute-start.37
  293.5 6.3 %convolution_convert_fusion.2 = bf16[1024,2048]{1,0:T(8,128)(2,1)} fusion(bf16[1024,1024]{1,0:T(8,128)(2,1)S(1)} %copy-done.50, bf16[1024,2048]{1,0:T(8,128)(2,1)S(1)} %constant_dynamic-update-slice_fusion.5), kind=kOutput, calls=%fused_computation.6 | convolution fusion | flops 4297064448 | bytes 10485760 | tf_op jit(solution)/shard_map/dot_general | solution.py:34
  299.8 27.7 %reduce-scatter.5.cloned.1.call-done = bf16[512,1024]{1,0:T(8,128)(2,1)} async-done(((bf16[2048,1024]{1,0:T(8,128)(2,1)}), bf16[512,1024]{1,0:T(8,128)(2,1)}) %reduce-scatter.5.cloned.1.call-update) | async-done | bytes 1048592 | tf_op jit(solution)/shard_map/reduce_scatter | solution.py:144
  327.6 2.8 convert_add_fusion.3.in_ref
  330.4 4.4 add_convert_fusion.1
  334.9 2.3 pick_blocks.3
  346.3 13.6 %collective-permute-start.38 = (bf16[128,2048]{1,0:T(8,128)(2,1)S(1)}, bf16[128,2048]{1,0:T(8,128)(2,1)S(1)}, u32[]{:S(2)}, u32[]{:S(2)}) collective-permute-start(bf16[128,2048]{1,0:T(8,128)(2,1)S(1)} %get-tuple-element.100), channel_id=1, source_target_pairs={{0,4},{12,8},{1,5},{13,9},{2,6},{14,10},{3,7},{15,11},{16,20},{28,... | collective-permute-start | bytes 1572872 | tf_op jit(solution)/shard_map/ppermute | solution.py:164
  360.8 6.8 %collective-permute-done.42 = bf16[128,2048]{1,0:T(8,128)(2,1)S(1)} collective-permute-done((bf16[128,2048]{1,0:T(8,128)(2,1)S(1)}, bf16[128,2048]{1,0:T(8,128)(2,1)S(1)}, u32[]{:S(2)}, u32[]{:S(2)}) %collective-permute-start.42) | collective-permute-done | bytes 524320 | tf_op jit(solution)/shard_map/ppermute | solution.py:64
  369.4 15.5 %collective-permute-done.44 = bf16[128,2048]{1,0:T(8,128)(2,1)S(1)} collective-permute-done((bf16[128,2048]{1,0:T(8,128)(2,1)S(1)}, bf16[128,2048]{1,0:T(8,128)(2,1)S(1)}, u32[]{:S(2)}, u32[]{:S(2)}) %collective-permute-start.44) | collective-permute-done | bytes 524320 | tf_op jit(solution)/shard_map/ppermute | solution.py:64
  386.3 4.0 collective-permute-done.45
  390.6 2.2 convolution_convert_fusion.8
  392.8 10.9 %attention_grad.1 = (bf16[2,2,2,2,64,256]{5,4,3,2,1,0:T(8,128)(2,1)}, bf16[2,2,2,4,2,64,256]{6,5,4,3,2,1,0:T(8,128)(2,1)}) custom-call(bf16[2,2,2,2,64,256]{5,4,3,2,1,0:T(8,128)(2,1)} %bitcast.230, bf16[2,2,2,2,64,256]{5,4,3,2,1,0:T(8,128)(2,1)} %bitcast.232, bf16[2,2,2,4,2,64,256]{6,5,4,3,2,1,0:T(8,128)(2,1)} %pad_maximum_fusion.1.kv_ref, ...), custom_call_target="tpu_custom_call" | custom-call | flops 2097152 | bytes 262144 | tf_op jit(solution)/shard_map/attention_grad/pallas_call | solution.py:429
  405.2 4.8 convolution_convert_fusion
  411.3 2.8 convert_element_type.323
  414.1 3.3 slice.164
  417.7 4.6 all-to-all-start.2
  424.1 2.9 collective-permute-start.41
  432.1 2.3 collective-permute-start.53
  434.5 3.0 add_convert_fusion
  441.4 6.0 %collective-permute-done.53 = bf16[4,2,64,256]{3,2,1,0:T(8,128)(2,1)S(1)} collective-permute-done((bf16[4,2,64,256]{3,2,1,0:T(8,128)(2,1)S(1)}, bf16[4,2,64,256]{3,2,1,0:T(8,128)(2,1)S(1)}, u32[]{:S(2)}, u32[]{:S(2)}) %collective-permute-start.53) | collective-permute-done | bytes 262176 | tf_op jit(solution)/shard_map/ppermute | solution.py:64
  449.0 11.7 %all-to-all-done.2.in_ref = bf16[8,64,1024]{2,1,0:T(8,128)(2,1)} async-done(((bf16[8,64,1024]{2,1,0:T(8,128)(2,1)}), bf16[8,64,1024]{2,1,0:T(8,128)(2,1)}, u32[]{:S(2)}, u32[]{:S(2)}) %all-to-all-start.2) | async-done | bytes 1048608 | tf_op jit(solution)/shard_map/all_to_all | solution.py:52
  460.7 4.6 convolution_convert_fusion.7
  465.4 2.8 collective-permute-done.50
  470.1 3.6 convolution_convert_fusion.6
  477.5 4.0 collective-permute-done.54
  481.5 8.4 %collective-permute-done.55 = bf16[2,64,256]{2,1,0:T(8,128)(2,1)S(1)} collective-permute-done((bf16[2,64,256]{2,1,0:T(8,128)(2,1)S(1)}, bf16[2,64,256]{2,1,0:T(8,128)(2,1)S(1)}, u32[]{:S(2)}, u32[]{:S(2)}) %collective-permute-start.55) | collective-permute-done | bytes 65568 | tf_op jit(solution)/shard_map/ppermute | solution.py:160
  495.4 3.4 all-to-all-start.3
  501.3 2.8 add_convert_fusion.4
  504.1 2.7 collect_units.1
  506.8 2.7 add_add_fusion.2
  509.5 38.9 %all-to-all-done.3 = bf16[32,80,256]{2,1,0:T(8,128)(2,1)} async-done(((bf16[32,80,256]{2,1,0:T(8,128)(2,1)}), bf16[32,80,256]{2,1,0:T(8,128)(2,1)}, u32[]{:S(2)}, u32[]{:S(2)}) %all-to-all-start.3) | async-done | bytes 1310752 | tf_op jit(solution)/shard_map/all_to_all | solution.py:52
  548.4 3.4 all-to-all-start.4
  (376 shorter events, 137.1 us)
Async XLA Ops:
  7.2 66.7 %all-gather.4.cloned.1.call-start = ((), (), s32[]{:S(2)}) async-start(), calls=%async_computation.9 | async-start | bytes 1310720 | tf_op jit(solution)/shard_map/all_gather | solution.py:509
  11.7 16.9 %collective-permute-start.1 = (bf16[80,256]{1,0:T(8,128)(2,1)S(1)}, bf16[80,256]{1,0:T(8,128)(2,1)S(1)}, u32[]{:S(2)}, u32[]{:S(2)}) collective-permute-start(bf16[80,256]{1,0:T(8,128)(2,1)S(1)} %concatenate.55), channel_id=1, source_target_pairs={{0,8},{4,12},{8,0},{12,4},{1,9},{5,13},{9,1},{13,5},{2,10},{6,14},... | collective-permute-start | bytes 122888 | tf_op jit(solution)/shard_map/ppermute | solution.py:160
  15.8 12.8 %collective-permute-start.2 = (bf16[80,256]{1,0:T(8,128)(2,1)S(1)}, bf16[80,256]{1,0:T(8,128)(2,1)S(1)}, u32[]{:S(2)}, u32[]{:S(2)}) collective-permute-start(bf16[80,256]{1,0:T(8,128)(2,1)S(1)} %concatenate.55), channel_id=1, source_target_pairs={{0,12},{4,0},{8,4},{12,8},{1,13},{5,1},{9,5},{13,9},{2,14},{6,2},{... | collective-permute-start | bytes 122888 | tf_op jit(solution)/shard_map/ppermute | solution.py:160
  17.1 11.4 %collective-permute-start = (bf16[80,256]{1,0:T(8,128)(2,1)S(1)}, bf16[80,256]{1,0:T(8,128)(2,1)S(1)}, u32[]{:S(2)}, u32[]{:S(2)}) collective-permute-start(bf16[80,256]{1,0:T(8,128)(2,1)S(1)} %concatenate.55), channel_id=1, source_target_pairs={{0,4},{4,8},{8,12},{12,0},{1,5},{5,9},{9,13},{13,1},{2,6},{6,10},{... | collective-permute-start | bytes 122888 | tf_op jit(solution)/shard_map/ppermute | solution.py:160
  17.8 28.7 %collective-permute-start.10 = (bf16[128,2048]{1,0:T(8,128)(2,1)}, bf16[128,2048]{1,0:T(8,128)(2,1)S(1)}, u32[]{:S(2)}, u32[]{:S(2)}) collective-permute-start(bf16[128,2048]{1,0:T(8,128)(2,1)} %bitcast.192), channel_id=1, source_target_pairs={{0,2},{2,0},{16,18},{18,16},{1,3},{3,1},{17,19},{19,17},{4,6},{6,4... | collective-permute-start | bytes 1572872 | tf_op jit(solution)/shard_map/ppermute | solution.py:64
  19.3 27.2 %collective-permute-start.11 = (bf16[128,2048]{1,0:T(8,128)(2,1)}, bf16[128,2048]{1,0:T(8,128)(2,1)}, u32[]{:S(2)}, u32[]{:S(2)}) collective-permute-start(bf16[128,2048]{1,0:T(8,128)(2,1)} %bitcast.193), channel_id=1, source_target_pairs={{0,16},{2,18},{16,0},{18,2},{1,17},{3,19},{17,1},{19,3},{4,20},{6,... | collective-permute-start | bytes 1572872 | tf_op jit(solution)/shard_map/ppermute | solution.py:64
  23.1 42.9 %all-to-all-start = ((bf16[8,64,1024]{2,1,0:T(8,128)(2,1)}), bf16[8,64,1024]{2,1,0:T(8,128)(2,1)}, u32[]{:S(2)}, u32[]{:S(2)}) async-start(bf16[8,64,1024]{2,1,0:T(8,128)(2,1)} %spread_units.1), calls=%async_computation | async-start | bytes 2097152 | tf_op jit(solution)/shard_map/all_to_all | solution.py:52
  27.6 208.1 %all-gather.8.cloned.1.call-start = ((), (), s32[]{:S(2)}) async-start(), calls=%async_computation.11 | async-start | bytes 5242880 | tf_op jit(solution)/shard_map/all_gather | solution.py:521
  28.7 6.7 %collective-permute-start.3 = (bf16[4,80,256]{2,1,0:T(8,128)(2,1)S(1)}, bf16[4,80,256]{2,1,0:T(8,128)(2,1)S(1)}, u32[]{:S(2)}, u32[]{:S(2)}) collective-permute-start(bf16[4,80,256]{2,1,0:T(8,128)(2,1)S(1)} %get-tuple-element.124), channel_id=1, source_target_pairs={{0,2},{2,0},{16,18},{18,16},{1,3},{3,1},{17,19},{19,17},{4,6},{6,4... | collective-permute-start | bytes 491528 | tf_op jit(solution)/shard_map/ppermute | solution.py:64
  29.3 7.5 %collective-permute-start.4 = (bf16[4,80,256]{2,1,0:T(8,128)(2,1)S(1)}, bf16[4,80,256]{2,1,0:T(8,128)(2,1)S(1)}, u32[]{:S(2)}, u32[]{:S(2)}) collective-permute-start(bf16[4,80,256]{2,1,0:T(8,128)(2,1)S(1)} %get-tuple-element.124), channel_id=1, source_target_pairs={{0,16},{2,18},{16,0},{18,2},{1,17},{3,19},{17,1},{19,3},{4,20},{6,... | collective-permute-start | bytes 491528 | tf_op jit(solution)/shard_map/ppermute | solution.py:64
  29.8 10.9 %collective-permute-start.5 = (bf16[4,80,256]{2,1,0:T(8,128)(2,1)S(1)}, bf16[4,80,256]{2,1,0:T(8,128)(2,1)S(1)}, u32[]{:S(2)}, u32[]{:S(2)}) collective-permute-start(bf16[4,80,256]{2,1,0:T(8,128)(2,1)S(1)} %get-tuple-element.124), channel_id=1, source_target_pairs={{0,18},{2,16},{16,2},{18,0},{1,19},{3,17},{17,3},{19,1},{4,22},{6,... | collective-permute-start | bytes 491528 | tf_op jit(solution)/shard_map/ppermute | solution.py:64
  35.4 16.0 %collective-permute-start.12 = (bf16[128,2048]{1,0:T(8,128)(2,1)S(1)}, bf16[128,2048]{1,0:T(8,128)(2,1)}, u32[]{:S(2)}, u32[]{:S(2)}) collective-permute-start(bf16[128,2048]{1,0:T(8,128)(2,1)S(1)} %bitcast.194), channel_id=1, source_target_pairs={{0,18},{2,16},{16,2},{18,0},{1,19},{3,17},{17,3},{19,1},{4,22},{6,... | collective-permute-start | bytes 1572872 | tf_op jit(solution)/shard_map/ppermute | solution.py:64
  41.0 13.1 %collective-permute-start.6 = (bf16[4,4,80,256]{3,2,1,0:T(8,128)(2,1)S(1)}, bf16[4,4,80,256]{3,2,1,0:T(8,128)(2,1)S(1)}, u32[]{:S(2)}, u32[]{:S(2)}) collective-permute-start(bf16[4,4,80,256]{3,2,1,0:T(8,128)(2,1)S(1)} %pad_maximum_fusion.9), channel_id=1, source_target_pairs={{0,1},{1,0},{2,3},{3,2},{4,5},{5,4},{6,7},{7,6},{8,9},{9,8},{10,11... | collective-permute-start | bytes 1966088 | tf_op jit(solution)/shard_map/ppermute | solution.py:38
  54.1 23.6 %collective-permute-start.13 = (bf16[512,2048]{1,0:T(8,128)(2,1)}, bf16[512,2048]{1,0:T(8,128)(2,1)}, u32[]{:S(2)}, u32[]{:S(2)}) collective-permute-start(bf16[512,2048]{1,0:T(8,128)(2,1)} %pad_maximum_fusion.near_ref), channel_id=1, source_target_pairs={{0,1},{1,0},{2,3},{3,2},{4,5},{5,4},{6,7},{7,6},{8,9},{9,8},{10,11... | collective-permute-start | bytes 6291464 | tf_op jit(solution)/shard_map/ppermute | solution.py:38
  57.2 18.7 %collective-permute-start.7 = (bf16[2,64,256]{2,1,0:T(8,128)(2,1)S(1)}, bf16[2,64,256]{2,1,0:T(8,128)(2,1)S(1)}, u32[]{:S(2)}, u32[]{:S(2)}) collective-permute-start(bf16[2,64,256]{2,1,0:T(8,128)(2,1)S(1)} %bitcast.234), channel_id=1, source_target_pairs={{0,4},{4,8},{8,12},{12,0},{1,5},{5,9},{9,13},{13,1},{2,6},{6,10},{... | collective-permute-start | bytes 196616 | tf_op jit(solution)/shard_map/ppermute | solution.py:160
  59.0 17.0 %collective-permute-start.8 = (bf16[2,64,256]{2,1,0:T(8,128)(2,1)S(1)}, bf16[2,64,256]{2,1,0:T(8,128)(2,1)S(1)}, u32[]{:S(2)}, u32[]{:S(2)}) collective-permute-start(bf16[2,64,256]{2,1,0:T(8,128)(2,1)S(1)} %bitcast.235), channel_id=1, source_target_pairs={{0,8},{4,12},{8,0},{12,4},{1,9},{5,13},{9,1},{13,5},{2,10},{6,14},... | collective-permute-start | bytes 196616 | tf_op jit(solution)/shard_map/ppermute | solution.py:160
  61.3 14.7 %collective-permute-start.9 = (bf16[2,64,256]{2,1,0:T(8,128)(2,1)S(1)}, bf16[2,64,256]{2,1,0:T(8,128)(2,1)S(1)}, u32[]{:S(2)}, u32[]{:S(2)}) collective-permute-start(bf16[2,64,256]{2,1,0:T(8,128)(2,1)S(1)} %bitcast.236), channel_id=1, source_target_pairs={{0,12},{4,0},{8,4},{12,8},{1,13},{5,1},{9,5},{13,9},{2,14},{6,2},{... | collective-permute-start | bytes 196616 | tf_op jit(solution)/shard_map/ppermute | solution.py:160
  66.0 48.4 %all-to-all-start.1 = ((bf16[32,64,256]{2,1,0:T(8,128)(2,1)}), bf16[32,64,256]{2,1,0:T(8,128)(2,1)S(1)}, u32[]{:S(2)}, u32[]{:S(2)}) async-start(bf16[32,64,256]{2,1,0:T(8,128)(2,1)} %spread_heads.1), calls=%async_computation.1 | async-start | bytes 2097152 | tf_op jit(solution)/shard_map/all_to_all | solution.py:52
  68.7 166.9 %all-gather.6.cloned.1.call-start = ((), (), s32[]{:S(2)}) async-start(), calls=%async_computation.10 | async-start | bytes 5242880 | tf_op jit(solution)/shard_map/all_gather | solution.py:520
  75.7 36.3 %collective-permute-start.18 = (bf16[2,64,2048]{2,1,0:T(8,128)(2,1)}, bf16[2,64,2048]{2,1,0:T(8,128)(2,1)}, u32[]{:S(2)}, u32[]{:S(2)}) collective-permute-start(bf16[2,64,2048]{2,1,0:T(8,128)(2,1)} %dynamic-slice_bitcast_fusion.1), channel_id=1, source_target_pairs={{0,1},{1,0},{2,3},{3,2},{4,5},{5,4},{6,7},{7,6},{8,9},{9,8},{10,11... | collective-permute-start | bytes 1572872 | tf_op jit(solution)/shard_map/ppermute | solution.py:38
  85.8 11.8 %collective-permute-start.14 = (bf16[4,2,64,256]{3,2,1,0:T(8,128)(2,1)S(1)}, bf16[4,2,64,256]{3,2,1,0:T(8,128)(2,1)S(1)}, u32[]{:S(2)}, u32[]{:S(2)}) collective-permute-start(bf16[4,2,64,256]{3,2,1,0:T(8,128)(2,1)S(1)} %pad_maximum_fusion.10), channel_id=1, source_target_pairs={{0,2},{2,0},{16,18},{18,16},{1,3},{3,1},{17,19},{19,17},{4,6},{6,4... | collective-permute-start | bytes 786440 | tf_op jit(solution)/shard_map/ppermute | solution.py:64
  87.5 12.9 %collective-permute-start.15 = (bf16[4,2,64,256]{3,2,1,0:T(8,128)(2,1)S(1)}, bf16[4,2,64,256]{3,2,1,0:T(8,128)(2,1)S(1)}, u32[]{:S(2)}, u32[]{:S(2)}) collective-permute-start(bf16[4,2,64,256]{3,2,1,0:T(8,128)(2,1)S(1)} %pad_maximum_fusion.10), channel_id=1, source_target_pairs={{0,16},{2,18},{16,0},{18,2},{1,17},{3,19},{17,1},{19,3},{4,20},{6,... | collective-permute-start | bytes 786440 | tf_op jit(solution)/shard_map/ppermute | solution.py:64
  88.9 22.0 %collective-permute-start.16 = (bf16[4,2,64,256]{3,2,1,0:T(8,128)(2,1)S(1)}, bf16[4,2,64,256]{3,2,1,0:T(8,128)(2,1)S(1)}, u32[]{:S(2)}, u32[]{:S(2)}) collective-permute-start(bf16[4,2,64,256]{3,2,1,0:T(8,128)(2,1)S(1)} %pad_maximum_fusion.10), channel_id=1, source_target_pairs={{0,18},{2,16},{16,2},{18,0},{1,19},{3,17},{17,3},{19,1},{4,22},{6,... | collective-permute-start | bytes 786440 | tf_op jit(solution)/shard_map/ppermute | solution.py:64
  112.0 7.0 %collective-permute-start.17 = (bf16[4,4,2,64,256]{4,3,2,1,0:T(8,128)(2,1)}, bf16[4,4,2,64,256]{4,3,2,1,0:T(8,128)(2,1)}, u32[]{:S(2)}, u32[]{:S(2)}) collective-permute-start(bf16[4,4,2,64,256]{4,3,2,1,0:T(8,128)(2,1)} %pad_maximum_fusion.5), channel_id=1, source_target_pairs={{0,1},{1,0},{2,3},{3,2},{4,5},{5,4},{6,7},{7,6},{8,9},{9,8},{10,11... | collective-permute-start | bytes 3145736 | tf_op jit(solution)/shard_map/ppermute | solution.py:38
  138.7 188.7 %reduce-scatter.5.cloned.1.call-start = ((), (), s32[]{:S(2)}) async-start(), calls=%async_computation.12 | async-start | bytes 5242880 | tf_op jit(solution)/shard_map/reduce_scatter | solution.py:144
  139.3 27.8 %collective-permute-start.28 = (bf16[128,2048]{1,0:T(8,128)(2,1)S(1)}, bf16[128,2048]{1,0:T(8,128)(2,1)S(1)}, u32[]{:S(2)}, u32[]{:S(2)}) collective-permute-start(bf16[128,2048]{1,0:T(8,128)(2,1)S(1)} %bitcast.196), channel_id=1, source_target_pairs={{0,4},{4,0},{8,12},{12,8},{1,5},{5,1},{9,13},{13,9},{2,6},{6,2},{1... | collective-permute-start | bytes 1572872 | tf_op jit(solution)/shard_map/ppermute | solution.py:164
  139.7 25.8 %collective-permute-start.29 = (bf16[128,2048]{1,0:T(8,128)(2,1)S(1)}, bf16[128,2048]{1,0:T(8,128)(2,1)}, u32[]{:S(2)}, u32[]{:S(2)}) collective-permute-start(bf16[128,2048]{1,0:T(8,128)(2,1)S(1)} %bitcast.197), channel_id=1, source_target_pairs={{0,8},{8,0},{4,12},{12,4},{1,9},{9,1},{5,13},{13,5},{2,10},{10,2},... | collective-permute-start | bytes 1572872 | tf_op jit(solution)/shard_map/ppermute | solution.py:164
  145.8 24.6 %collective-permute-start.20 = (bf16[128,2048]{1,0:T(8,128)(2,1)S(1)}, bf16[128,2048]{1,0:T(8,128)(2,1)S(1)}, u32[]{:S(2)}, u32[]{:S(2)}) collective-permute-start(bf16[128,2048]{1,0:T(8,128)(2,1)S(1)} %get-tuple-element.104), channel_id=1, source_target_pairs={{0,2},{2,0},{16,18},{18,16},{1,3},{3,1},{17,19},{19,17},{4,6},{6,4... | collective-permute-start | bytes 1572872 | tf_op jit(solution)/shard_map/ppermute | solution.py:64
  147.4 25.0 %collective-permute-start.21 = (bf16[128,2048]{1,0:T(8,128)(2,1)S(1)}, bf16[128,2048]{1,0:T(8,128)(2,1)S(1)}, u32[]{:S(2)}, u32[]{:S(2)}) collective-permute-start(bf16[128,2048]{1,0:T(8,128)(2,1)S(1)} %get-tuple-element.106), channel_id=1, source_target_pairs={{0,16},{2,18},{16,0},{18,2},{1,17},{3,19},{17,1},{19,3},{4,20},{6,... | collective-permute-start | bytes 1572872 | tf_op jit(solution)/shard_map/ppermute | solution.py:64
  149.6 34.8 %collective-permute-start.22 = (bf16[128,2048]{1,0:T(8,128)(2,1)S(1)}, bf16[128,2048]{1,0:T(8,128)(2,1)S(1)}, u32[]{:S(2)}, u32[]{:S(2)}) collective-permute-start(bf16[128,2048]{1,0:T(8,128)(2,1)S(1)} %get-tuple-element.105), channel_id=1, source_target_pairs={{0,18},{2,16},{16,2},{18,0},{1,19},{3,17},{17,3},{19,1},{4,22},{6,... | collective-permute-start | bytes 1572872 | tf_op jit(solution)/shard_map/ppermute | solution.py:64
  165.6 24.8 %collective-permute-start.30 = (bf16[128,2048]{1,0:T(8,128)(2,1)S(1)}, bf16[128,2048]{1,0:T(8,128)(2,1)}, u32[]{:S(2)}, u32[]{:S(2)}) collective-permute-start(bf16[128,2048]{1,0:T(8,128)(2,1)S(1)} %bitcast.199), channel_id=1, source_target_pairs={{4,8},{8,4},{5,9},{9,5},{6,10},{10,6},{7,11},{11,7},{20,24},{24,20... | collective-permute-start | bytes 1572872 | tf_op jit(solution)/shard_map/ppermute | solution.py:164
  167.1 23.3 %collective-permute-start.31 = (bf16[128,2048]{1,0:T(8,128)(2,1)}, bf16[128,2048]{1,0:T(8,128)(2,1)}, u32[]{:S(2)}, u32[]{:S(2)}) collective-permute-start(bf16[128,2048]{1,0:T(8,128)(2,1)} %collective-permute-done.29), channel_id=1, source_target_pairs={{4,0},{8,12},{5,1},{9,13},{6,2},{10,14},{7,3},{11,15},{20,16},{24,... | collective-permute-start | bytes 1572872 | tf_op jit(solution)/shard_map/ppermute | solution.py:164
  188.3 25.7 %collective-permute-start.24 = (bf16[128,2048]{1,0:T(8,128)(2,1)}, bf16[128,2048]{1,0:T(8,128)(2,1)S(1)}, u32[]{:S(2)}, u32[]{:S(2)}) collective-permute-start(bf16[128,2048]{1,0:T(8,128)(2,1)} %pick_blocks.2), channel_id=1, source_target_pairs={{0,8},{8,0},{4,12},{12,4},{1,9},{9,1},{5,13},{13,5},{2,10},{10,2},... | collective-permute-start | bytes 1572872 | tf_op jit(solution)/shard_map/ppermute | solution.py:164
  189.3 26.7 %collective-permute-start.23 = (bf16[128,2048]{1,0:T(8,128)(2,1)}, bf16[128,2048]{1,0:T(8,128)(2,1)S(1)}, u32[]{:S(2)}, u32[]{:S(2)}) collective-permute-start(bf16[128,2048]{1,0:T(8,128)(2,1)} %pick_blocks.2), channel_id=1, source_target_pairs={{0,4},{4,0},{8,12},{12,8},{1,5},{5,1},{9,13},{13,9},{2,6},{6,2},{1... | collective-permute-start | bytes 1572872 | tf_op jit(solution)/shard_map/ppermute | solution.py:164
  195.2 40.4 %collective-permute-start.32 = (bf16[512,2048]{1,0:T(8,128)(2,1)}, bf16[512,2048]{1,0:T(8,128)(2,1)}, u32[]{:S(2)}, u32[]{:S(2)}) collective-permute-start(bf16[512,2048]{1,0:T(8,128)(2,1)} %pad_maximum_fusion.3.grad_near_ref), channel_id=1, source_target_pairs={{0,1},{1,0},{2,3},{3,2},{4,5},{5,4},{6,7},{7,6},{8,9},{9,8},{10,11... | collective-permute-start | bytes 6291464 | tf_op jit(solution)/shard_map/ppermute | solution.py:38
  214.6 15.7 %collective-permute-start.26 = (bf16[128,2048]{1,0:T(8,128)(2,1)S(1)}, bf16[128,2048]{1,0:T(8,128)(2,1)S(1)}, u32[]{:S(2)}, u32[]{:S(2)}) collective-permute-start(bf16[128,2048]{1,0:T(8,128)(2,1)S(1)} %collective-permute-done.24), channel_id=1, source_target_pairs={{4,0},{8,12},{5,1},{9,13},{6,2},{10,14},{7,3},{11,15},{20,16},{24,... | collective-permute-start | bytes 1572872 | tf_op jit(solution)/shard_map/ppermute | solution.py:164
  275.4 135.9 %reduce-scatter.7.cloned.1.call-start = ((), (), s32[]{:S(2)}) async-start(), calls=%async_computation.13 | async-start | bytes 5242880 | tf_op jit(solution)/shard_map/reduce_scatter | solution.py:144
  284.6 45.9 %collective-permute-start.34 = (bf16[512,2048]{1,0:T(8,128)(2,1)}, bf16[512,2048]{1,0:T(8,128)(2,1)}, u32[]{:S(2)}, u32[]{:S(2)}) collective-permute-start(bf16[512,2048]{1,0:T(8,128)(2,1)} %slice.199), channel_id=1, source_target_pairs={{0,1},{1,0},{2,3},{3,2},{4,5},{5,4},{6,7},{7,6},{8,9},{9,8},{10,11... | collective-permute-start | bytes 6291464 | tf_op jit(solution)/shard_map/ppermute | solution.py:38
  289.1 38.4 %collective-permute-start.35 = (bf16[128,2048]{1,0:T(8,128)(2,1)}, bf16[128,2048]{1,0:T(8,128)(2,1)}, u32[]{:S(2)}, u32[]{:S(2)}) collective-permute-start(bf16[128,2048]{1,0:T(8,128)(2,1)} %get-tuple-element.101), channel_id=1, source_target_pairs={{0,4},{4,0},{8,12},{12,8},{1,5},{5,1},{9,13},{13,9},{2,6},{6,2},{1... | collective-permute-start | bytes 1572872 | tf_op jit(solution)/shard_map/ppermute | solution.py:164
  289.1 38.5 %collective-permute-start.36 = (bf16[128,2048]{1,0:T(8,128)(2,1)}, bf16[128,2048]{1,0:T(8,128)(2,1)}, u32[]{:S(2)}, u32[]{:S(2)}) collective-permute-start(bf16[128,2048]{1,0:T(8,128)(2,1)} %get-tuple-element.103), channel_id=1, source_target_pairs={{0,8},{8,0},{4,12},{12,4},{1,9},{9,1},{5,13},{13,5},{2,10},{10,2},... | collective-permute-start | bytes 1572872 | tf_op jit(solution)/shard_map/ppermute | solution.py:164
  290.8 36.8 %collective-permute-start.37 = (bf16[128,2048]{1,0:T(8,128)(2,1)}, bf16[128,2048]{1,0:T(8,128)(2,1)}, u32[]{:S(2)}, u32[]{:S(2)}) collective-permute-start(bf16[128,2048]{1,0:T(8,128)(2,1)} %get-tuple-element.102), channel_id=1, source_target_pairs={{0,12},{12,0},{4,8},{8,4},{1,13},{13,1},{5,9},{9,5},{2,14},{14,2},... | collective-permute-start | bytes 1572872 | tf_op jit(solution)/shard_map/ppermute | solution.py:164
  341.8 25.7 %collective-permute-start.42 = (bf16[128,2048]{1,0:T(8,128)(2,1)S(1)}, bf16[128,2048]{1,0:T(8,128)(2,1)S(1)}, u32[]{:S(2)}, u32[]{:S(2)}) collective-permute-start(bf16[128,2048]{1,0:T(8,128)(2,1)S(1)} %get-tuple-element.87), channel_id=1, source_target_pairs={{0,2},{2,0},{16,18},{18,16},{1,3},{3,1},{17,19},{19,17},{4,6},{6,4... | collective-permute-start | bytes 1572872 | tf_op jit(solution)/shard_map/ppermute | solution.py:64
  343.4 26.0 %collective-permute-start.43 = (bf16[128,2048]{1,0:T(8,128)(2,1)S(1)}, bf16[128,2048]{1,0:T(8,128)(2,1)S(1)}, u32[]{:S(2)}, u32[]{:S(2)}) collective-permute-start(bf16[128,2048]{1,0:T(8,128)(2,1)S(1)} %get-tuple-element.87), channel_id=1, source_target_pairs={{0,16},{2,18},{16,0},{18,2},{1,17},{3,19},{17,1},{19,3},{4,20},{6,... | collective-permute-start | bytes 1572872 | tf_op jit(solution)/shard_map/ppermute | solution.py:64
  344.4 40.5 %collective-permute-start.44 = (bf16[128,2048]{1,0:T(8,128)(2,1)S(1)}, bf16[128,2048]{1,0:T(8,128)(2,1)S(1)}, u32[]{:S(2)}, u32[]{:S(2)}) collective-permute-start(bf16[128,2048]{1,0:T(8,128)(2,1)S(1)} %get-tuple-element.87), channel_id=1, source_target_pairs={{0,18},{2,16},{16,2},{18,0},{1,19},{3,17},{17,3},{19,1},{4,22},{6,... | collective-permute-start | bytes 1572872 | tf_op jit(solution)/shard_map/ppermute | solution.py:64
  346.3 38.9 %collective-permute-start.38 = (bf16[128,2048]{1,0:T(8,128)(2,1)S(1)}, bf16[128,2048]{1,0:T(8,128)(2,1)S(1)}, u32[]{:S(2)}, u32[]{:S(2)}) collective-permute-start(bf16[128,2048]{1,0:T(8,128)(2,1)S(1)} %get-tuple-element.100), channel_id=1, source_target_pairs={{0,4},{12,8},{1,5},{13,9},{2,6},{14,10},{3,7},{15,11},{16,20},{28,... | collective-permute-start | bytes 1572872 | tf_op jit(solution)/shard_map/ppermute | solution.py:164
  359.9 26.3 %collective-permute-start.40 = (bf16[128,2048]{1,0:T(8,128)(2,1)S(1)}, bf16[128,2048]{1,0:T(8,128)(2,1)S(1)}, u32[]{:S(2)}, u32[]{:S(2)}) collective-permute-start(bf16[128,2048]{1,0:T(8,128)(2,1)S(1)} %get-tuple-element.100), channel_id=1, source_target_pairs={{4,8},{8,4},{5,9},{9,5},{6,10},{10,6},{7,11},{11,7},{20,24},{24,20... | collective-permute-start | bytes 1572872 | tf_op jit(solution)/shard_map/ppermute | solution.py:164
  417.4 14.7 %collective-permute-start.47 = (bf16[512,2048]{1,0:T(8,128)(2,1)}, bf16[512,2048]{1,0:T(8,128)(2,1)}, u32[]{:S(2)}, u32[]{:S(2)}) collective-permute-start(bf16[512,2048]{1,0:T(8,128)(2,1)} %slice.164), channel_id=1, source_target_pairs={{0,1},{1,0},{2,3},{3,2},{4,5},{5,4},{6,7},{7,6},{8,9},{9,8},{10,11... | collective-permute-start | bytes 6291464 | tf_op jit(solution)/shard_map/ppermute | solution.py:38
  417.7 43.0 %all-to-all-start.2 = ((bf16[8,64,1024]{2,1,0:T(8,128)(2,1)}), bf16[8,64,1024]{2,1,0:T(8,128)(2,1)}, u32[]{:S(2)}, u32[]{:S(2)}) async-start(bf16[8,64,1024]{2,1,0:T(8,128)(2,1)} %bitcast.216), calls=%async_computation.4 | async-start | bytes 2097152 | tf_op jit(solution)/shard_map/all_to_all | solution.py:52
  422.3 87.2 %reduce-scatter.9.cloned.1.call-start = ((), (), s32[]{:S(2)}) async-start(), calls=%async_computation.14 | async-start | bytes 1310720 | tf_op jit(solution)/shard_map/reduce_scatter | solution.py:623
  424.1 49.6 %collective-permute-start.41 = (bf16[128,2048]{1,0:T(8,128)(2,1)}, bf16[128,2048]{1,0:T(8,128)(2,1)}, u32[]{:S(2)}, u32[]{:S(2)}) collective-permute-start(bf16[128,2048]{1,0:T(8,128)(2,1)} %add_convert_fusion.5), channel_id=1, source_target_pairs={{0,8},{8,0},{4,12},{12,4},{1,9},{9,1},{5,13},{13,5},{2,10},{10,2},... | collective-permute-start | bytes 1572872 | tf_op jit(solution)/shard_map/ppermute | solution.py:164
  427.0 46.8 %collective-permute-start.39 = (bf16[128,2048]{1,0:T(8,128)(2,1)}, bf16[128,2048]{1,0:T(8,128)(2,1)}, u32[]{:S(2)}, u32[]{:S(2)}) collective-permute-start(bf16[128,2048]{1,0:T(8,128)(2,1)} %get-tuple-element.57), channel_id=1, source_target_pairs={{0,4},{4,0},{8,12},{12,8},{1,5},{5,1},{9,13},{13,9},{2,6},{6,2},{1... | collective-permute-start | bytes 1572872 | tf_op jit(solution)/shard_map/ppermute | solution.py:164
  430.9 9.1 %collective-permute-start.51 = (bf16[4,2,64,256]{3,2,1,0:T(8,128)(2,1)S(1)}, bf16[4,2,64,256]{3,2,1,0:T(8,128)(2,1)S(1)}, u32[]{:S(2)}, u32[]{:S(2)}) collective-permute-start(bf16[4,2,64,256]{3,2,1,0:T(8,128)(2,1)S(1)} %get-tuple-element.113), channel_id=1, source_target_pairs={{0,2},{2,0},{16,18},{18,16},{1,3},{3,1},{17,19},{19,17},{4,6},{6,4... | collective-permute-start | bytes 786440 | tf_op jit(solution)/shard_map/ppermute | solution.py:64
  431.5 9.2 %collective-permute-start.52 = (bf16[4,2,64,256]{3,2,1,0:T(8,128)(2,1)S(1)}, bf16[4,2,64,256]{3,2,1,0:T(8,128)(2,1)S(1)}, u32[]{:S(2)}, u32[]{:S(2)}) collective-permute-start(bf16[4,2,64,256]{3,2,1,0:T(8,128)(2,1)S(1)} %get-tuple-element.115), channel_id=1, source_target_pairs={{0,16},{2,18},{16,0},{18,2},{1,17},{3,19},{17,1},{19,3},{4,20},{6,... | collective-permute-start | bytes 786440 | tf_op jit(solution)/shard_map/ppermute | solution.py:64
  432.1 15.2 %collective-permute-start.53 = (bf16[4,2,64,256]{3,2,1,0:T(8,128)(2,1)S(1)}, bf16[4,2,64,256]{3,2,1,0:T(8,128)(2,1)S(1)}, u32[]{:S(2)}, u32[]{:S(2)}) collective-permute-start(bf16[4,2,64,256]{3,2,1,0:T(8,128)(2,1)S(1)} %get-tuple-element.114), channel_id=1, source_target_pairs={{0,18},{2,16},{16,2},{18,0},{1,19},{3,17},{17,3},{19,1},{4,22},{6,... | collective-permute-start | bytes 786440 | tf_op jit(solution)/shard_map/ppermute | solution.py:64
  440.0 25.4 %collective-permute-start.48 = (bf16[128,2048]{1,0:T(8,128)(2,1)}, bf16[128,2048]{1,0:T(8,128)(2,1)}, u32[]{:S(2)}, u32[]{:S(2)}) collective-permute-start(bf16[128,2048]{1,0:T(8,128)(2,1)} %get-tuple-element.96), channel_id=1, source_target_pairs={{0,2},{2,0},{16,18},{18,16},{1,3},{3,1},{17,19},{19,17},{4,6},{6,4... | collective-permute-start | bytes 1572872 | tf_op jit(solution)/shard_map/ppermute | solution.py:64
  440.8 24.6 %collective-permute-start.49 = (bf16[128,2048]{1,0:T(8,128)(2,1)}, bf16[128,2048]{1,0:T(8,128)(2,1)}, u32[]{:S(2)}, u32[]{:S(2)}) collective-permute-start(bf16[128,2048]{1,0:T(8,128)(2,1)} %get-tuple-element.98), channel_id=1, source_target_pairs={{0,16},{2,18},{16,0},{18,2},{1,17},{3,19},{17,1},{19,3},{4,20},{6,... | collective-permute-start | bytes 1572872 | tf_op jit(solution)/shard_map/ppermute | solution.py:64
  447.3 20.9 %collective-permute-start.50 = (bf16[128,2048]{1,0:T(8,128)(2,1)}, bf16[128,2048]{1,0:T(8,128)(2,1)}, u32[]{:S(2)}, u32[]{:S(2)}) collective-permute-start(bf16[128,2048]{1,0:T(8,128)(2,1)} %get-tuple-element.97), channel_id=1, source_target_pairs={{0,18},{2,16},{16,2},{18,0},{1,19},{3,17},{17,3},{19,1},{4,22},{6,... | collective-permute-start | bytes 1572872 | tf_op jit(solution)/shard_map/ppermute | solution.py:64
  473.8 7.8 %collective-permute-start.54 = (bf16[2,64,256]{2,1,0:T(8,128)(2,1)S(1)}, bf16[2,64,256]{2,1,0:T(8,128)(2,1)S(1)}, u32[]{:S(2)}, u32[]{:S(2)}) collective-permute-start(bf16[2,64,256]{2,1,0:T(8,128)(2,1)S(1)} %get-tuple-element.120), channel_id=1, source_target_pairs={{0,12},{4,0},{8,4},{12,8},{1,13},{5,1},{9,5},{13,9},{2,14},{6,2},{... | collective-permute-start | bytes 196616 | tf_op jit(solution)/shard_map/ppermute | solution.py:160
  474.3 15.6 %collective-permute-start.55 = (bf16[2,64,256]{2,1,0:T(8,128)(2,1)S(1)}, bf16[2,64,256]{2,1,0:T(8,128)(2,1)S(1)}, u32[]{:S(2)}, u32[]{:S(2)}) collective-permute-start(bf16[2,64,256]{2,1,0:T(8,128)(2,1)S(1)} %get-tuple-element.122), channel_id=1, source_target_pairs={{0,8},{4,12},{8,0},{12,4},{1,9},{5,13},{9,1},{13,5},{2,10},{6,14},... | collective-permute-start | bytes 196616 | tf_op jit(solution)/shard_map/ppermute | solution.py:160
  476.0 14.0 %collective-permute-start.56 = (bf16[2,64,256]{2,1,0:T(8,128)(2,1)S(1)}, bf16[2,64,256]{2,1,0:T(8,128)(2,1)S(1)}, u32[]{:S(2)}, u32[]{:S(2)}) collective-permute-start(bf16[2,64,256]{2,1,0:T(8,128)(2,1)S(1)} %get-tuple-element.121), channel_id=1, source_target_pairs={{0,4},{4,8},{8,12},{12,0},{1,5},{5,9},{9,13},{13,1},{2,6},{6,10},{... | collective-permute-start | bytes 196616 | tf_op jit(solution)/shard_map/ppermute | solution.py:160
  477.5 21.4 %collective-permute-start.57 = (bf16[2,64,2048]{2,1,0:T(8,128)(2,1)}, bf16[2,64,2048]{2,1,0:T(8,128)(2,1)}, u32[]{:S(2)}, u32[]{:S(2)}) collective-permute-start(bf16[2,64,2048]{2,1,0:T(8,128)(2,1)} %dynamic-slice_bitcast_fusion), channel_id=1, source_target_pairs={{0,1},{1,0},{2,3},{3,2},{4,5},{5,4},{6,7},{7,6},{8,9},{9,8},{10,11... | collective-permute-start | bytes 1572872 | tf_op jit(solution)/shard_map/ppermute | solution.py:38
  495.4 53.0 %all-to-all-start.3 = ((bf16[32,80,256]{2,1,0:T(8,128)(2,1)}), bf16[32,80,256]{2,1,0:T(8,128)(2,1)}, u32[]{:S(2)}, u32[]{:S(2)}) async-start(bf16[32,80,256]{2,1,0:T(8,128)(2,1)} %fusion.6), calls=%async_computation.5 | async-start | bytes 2621440 | tf_op jit(solution)/shard_map/all_to_all | solution.py:52
  498.8 56.8 %reduce-scatter.11.cloned.1.call-start = ((), (), s32[]{:S(2)}) async-start(), calls=%async_computation.15 | async-start | bytes 1310720 | tf_op jit(solution)/shard_map/reduce_scatter | solution.py:636
  548.4 9.4 %all-to-all-start.4 = ((bf16[8,64,256]{2,1,0:T(8,128)(2,1)}), bf16[8,64,256]{2,1,0:T(8,128)(2,1)S(1)}, u32[]{:S(2)}, u32[]{:S(2)}) async-start(bf16[8,64,256]{2,1,0:T(8,128)(2,1)} %bitcast.233), calls=%async_computation.7 | async-start | bytes 524288 | tf_op jit(solution)/shard_map/all_to_all | solution.py:52
  (58 other events, 502.2 us)
Sparse Core Ops, SparseCore 0:
  9.6 39.6 all-gather.3
  51.1 74.7 all-gather.7
  138.9 72.6 all-gather.5
  275.5 51.8 reduce-scatter.4
  330.5 72.2 reduce-scatter.6
  465.5 27.9 reduce-scatter.8
  502.0 41.5 reduce-scatter.10

commit v3 on v2

--- a/solution.py
+++ b/solution.py
@@ -674,11 +674,16 @@
     lines = [jnp.pad(share, ((0, 0), (0, lanes - share.shape[1]))) for share in shares]
     flat = jnp.pad(jnp.stack(lines, axis=1), ((0, 0), (0, 16 - len(lines)), (0, 0))).astype(LOW)
     flat = jnp.concatenate([grad_pair_w.reshape(devices, rows, 2 * HD), flat], axis=1)
-    flat = exchange(flat, EVERY)
-    grad_query_w = exchange(after(grad_query_w.reshape(8, rows, 2 * HD), flat), PLANE)
-    grad_query_w = collect_heads(grad_query_w, planes)
+    grad_up_w = collect_units(grad_up_w, planes)
+    deep = flat.shape[1]
+    flat = flat.reshape(2, planes, 2, 2, deep, lanes).transpose(0, 2, 3, 1, 4, 5)
+    flat = flat.reshape(8, planes * deep, lanes)
+    flat = jnp.concatenate([flat, grad_query_w.reshape(8, rows, 2 * HD)], axis=1)
+    flat = exchange(flat, PLANE)
+    grad_query_w = collect_heads(flat[:, planes * deep :], planes)
+    flat = jnp.sum(flat[:, : planes * deep].astype(F32), axis=0).astype(LOW)
+    flat = exchange(flat.reshape(planes, deep, lanes), "z")
     flat = jnp.sum(flat.astype(F32), axis=0)
-    grad_up_w = collect_units(grad_up_w, planes)
     grad_pair_w = flat[:rows]
     sums = [flat[rows + i, : share.shape[1]] for i, share in enumerate(shares)]
     return (

time: 578 us -> 559 us (0.967)
  waiting for transfers between devices: 233 us -> 205 us
    all_to_all x5, waiting for transfers between devices: 53.7 us -> 25.3 us  [exchange(): return lax.all_to_all(value, axes, 0, 0, tiled=True)]
    unnamed x121 -> x134, local copies, waits for them, and re-layouts: 12 us -> 12.2 us
  transfers between devices with their start and end apart: 70 -> 70, of which waited for: 30 -> 29; matrix products, arithmetic and copies ran while one was open for 24% -> 26% of each run, Pallas kernels for 7% -> 8%
where the time goes in v3:
time: 559 us; the launch traced here: 549 us
  waiting for transfers between devices  205 us (37%)
  starting transfers between devices  93.3 us (17%)
  other arithmetic  69.6 us (12%)
  Pallas kernels  58.9 us (11%)
  local copies, waits for them, and re-layouts  54.2 us (10%)
  matrix products  52.3 us (9%)
  between operations  15.9 us (3%)
    ppermute x21, waiting for transfers between devices, hop(): return lax.ppermute(value, CHIPS, [(i, i ^ mask) for i in range(4)])  80.7 us
    dot_general x13, matrix products, dot(): lax.dot_general(left, right, (dims, ((), ())), preferred_element_type=F32)  52.3 us
    ppermute x15, waiting for transfers between devices, line(): return lax.ppermute(value, 'z', pairs)  49 us
    ppermute x15, starting transfers between devices, line(): return lax.ppermute(value, 'z', pairs)  32.6 us
    reduce_scatter x2, waiting for transfers between devices, scatter_sum(): return lax.psum_scatter(value, axes, scatter_dimension=0, tiled=True)  27.7 us
    all_to_all x5, waiting for transfers between devices, exchange(): return lax.all_to_all(value, axes, 0, 0, tiled=True)  25.3 us
    ppermute x21, starting transfers between devices, hop(): return lax.ppermute(value, CHIPS, [(i, i ^ mask) for i in range(4)])  24.3 us
    all_to_all x5, starting transfers between devices, exchange(): return lax.all_to_all(value, axes, 0, 0, tiled=True)  19.3 us
  transfers between devices with their start and end apart: 70, of which 29 were waited for; matrix products, arithmetic and copies ran while one was open for 26% of the time, Pallas kernels for 8%

profile of v3, /device:TPU:0, one launch (start us, length us, event | category | flops | bytes accessed | tf_op | source)
XLA Modules:
  0.0 548.7 jit_solution(8546995738993320530)
XLA Ops:
  11.7 4.1 collective-permute-start.1
  20.8 2.3 spread_units.1
  23.1 4.4 all-to-all-start
  29.8 2.4 collective-permute-start.5
  32.5 2.9 collective-permute-done.3
  36.8 4.0 collective-permute-done.5
  46.6 4.8 collective-permute-done.12
  51.4 2.7 pad_maximum_fusion.near_ref
  61.1 2.4 collective-permute-start.8
  66.5 2.6 all-to-all-start.1
  77.9 8.1 %normed_rows.1 = bf16[1024,2048]{1,0:T(8,128)(2,1)} custom-call(bf16[512,2048]{1,0:T(8,128)(2,1)} %pad_maximum_fusion.near_ref, bf16[512,2048]{1,0:T(8,128)(2,1)} %collective-permute-done.13.far_ref, f32[1,2048]{1,0:T(1,128)} %unstack.27.gain_ref, f32[1,2048]{1,0:T(1,128)} %unstack.28.shift_ref), custom_call_target="tpu_custom_call" | custom-call | tf_op jit(solution)/shard_map/normed_rows/pallas_call | solution.py:316
  90.3 7.5 %collective-permute-done.14 = bf16[4,2,64,256]{3,2,1,0:T(8,128)(2,1)S(1)} collective-permute-done((bf16[4,2,64,256]{3,2,1,0:T(8,128)(2,1)S(1)}, bf16[4,2,64,256]{3,2,1,0:T(8,128)(2,1)S(1)}, u32[]{:S(2)}, u32[]{:S(2)}) %collective-permute-start.14) | collective-permute-done | bytes 262176 | tf_op jit(solution)/shard_map/ppermute | solution.py:64
  97.7 3.1 collective-permute-done.15
  100.8 10.6 %collective-permute-done.16 = bf16[4,2,64,256]{3,2,1,0:T(8,128)(2,1)S(1)} collective-permute-done((bf16[4,2,64,256]{3,2,1,0:T(8,128)(2,1)S(1)}, bf16[4,2,64,256]{3,2,1,0:T(8,128)(2,1)S(1)}, u32[]{:S(2)}, u32[]{:S(2)}) %collective-permute-start.16) | collective-permute-done | bytes 262176 | tf_op jit(solution)/shard_map/ppermute | solution.py:64
  114.9 4.6 fusion.5
  119.5 3.1 pad_maximum_fusion.1.kv_ref
  122.6 9.8 %attention.1 = (bf16[2,2,2,2,64,256]{5,4,3,2,1,0:T(8,128)(2,1)}, f32[4,2,1,256]{3,2,1,0:T(1,128)}) custom-call(bf16[2,2,2,2,64,256]{5,4,3,2,1,0:T(8,128)(2,1)} %bitcast.237, bf16[2,2,2,4,2,64,256]{6,5,4,3,2,1,0:T(8,128)(2,1)} %pad_maximum_fusion.1.kv_ref, s32[1024,1]{1,0:T(8,128)} %add.499.key_pos_ref, s32[1,256]{1,0:T(1,128)} %add.452.query_pos_ref, ...), custom_call_target="tpu_custom_call" | custom-call | flops 1073741824 | bytes 3145728 | tf_op jit(solution)/shard_map/attention/pallas_call | solution.py:407
  132.3 2.6 convolution_convert_fusion.1
  143.1 3.0 add_convert_fusion.3
  147.8 2.3 collective-permute-start.21
  150.3 15.9 %collective-permute-done.29 = bf16[128,2048]{1,0:T(8,128)(2,1)} collective-permute-done((bf16[128,2048]{1,0:T(8,128)(2,1)S(1)}, bf16[128,2048]{1,0:T(8,128)(2,1)}, u32[]{:S(2)}, u32[]{:S(2)}) %collective-permute-start.29) | collective-permute-done | bytes 524320 | tf_op jit(solution)/shard_map/ppermute | solution.py:164
  170.8 2.3 collective-permute-done.21
  173.0 11.9 %collective-permute-done.22 = bf16[128,2048]{1,0:T(8,128)(2,1)S(1)} collective-permute-done((bf16[128,2048]{1,0:T(8,128)(2,1)S(1)}, bf16[128,2048]{1,0:T(8,128)(2,1)S(1)}, u32[]{:S(2)}, u32[]{:S(2)}) %collective-permute-start.22) | collective-permute-done | bytes 524320 | tf_op jit(solution)/shard_map/ppermute | solution.py:64
  193.2 2.7 pad_maximum_fusion.3.grad_near_ref
  195.9 18.7 %collective-permute-done.24 = bf16[128,2048]{1,0:T(8,128)(2,1)S(1)} collective-permute-done((bf16[128,2048]{1,0:T(8,128)(2,1)}, bf16[128,2048]{1,0:T(8,128)(2,1)S(1)}, u32[]{:S(2)}, u32[]{:S(2)}) %collective-permute-start.24) | collective-permute-done | bytes 524320 | tf_op jit(solution)/shard_map/ppermute | solution.py:164
  216.7 14.2 %collective-permute-done.26 = bf16[128,2048]{1,0:T(8,128)(2,1)S(1)} collective-permute-done((bf16[128,2048]{1,0:T(8,128)(2,1)S(1)}, bf16[128,2048]{1,0:T(8,128)(2,1)S(1)}, u32[]{:S(2)}, u32[]{:S(2)}) %collective-permute-start.26) | collective-permute-done | bytes 524320 | tf_op jit(solution)/shard_map/ppermute | solution.py:164
  236.3 2.8 collective-permute-done.27.far_ref
  239.1 16.8 %hidden_units.1 = (bf16[1024,1024]{1,0:T(8,128)(2,1)}, bf16[1024,1024]{1,0:T(8,128)(2,1)}, f32[1,1024]{1,0:T(1,128)}) custom-call(bf16[512,2048]{1,0:T(8,128)(2,1)} %pad_maximum_fusion.2.near_ref, bf16[512,2048]{1,0:T(8,128)(2,1)} %collective-permute-done.27.far_ref, bf16[512,2048]{1,0:T(8,128)(2,1)} %pad_maximum_fusion.3.grad_near_ref, ...), custom_call_target="tpu_custom_call" | custom-call | flops 8589934592 | bytes 20971520 | tf_op jit(solution)/shard_map/hidden_units/pallas_call | solution.py:362
  256.0 7.4 %convolution_convert_fusion.5 = bf16[1024,2048]{1,0:T(8,128)(2,1)S(1)} fusion(bf16[1024,1024]{1,0:T(8,128)(2,1)} %get-tuple-element.52, bf16[2048,1024]{1,0:T(8,128)(2,1)} %all-gather.6.cloned.1.call-done.up_ref), kind=kOutput, calls=%fused_computation.9 | convolution fusion | flops 4297064448 | bytes 10485760 | tf_op jit(solution)/shard_map/dot_general | solution.py:34
  269.8 6.2 %convolution_convert_fusion.4 = bf16[2048,1024]{1,0:T(8,128)(2,1)} fusion(bf16[1024,2048]{1,0:T(8,128)(2,1)S(1)} %constant_dynamic-update-slice_fusion, bf16[1024,1024]{1,0:T(8,128)(2,1)S(1)} %copy-done.58), kind=kOutput, calls=%fused_computation.8 | convolution fusion | flops 4297064448 | bytes 10485760 | tf_op jit(solution)/shard_map/dot_general | solution.py:34
  276.2 7.5 %convolution_convert_fusion.3 = bf16[1024,2048]{1,0:T(8,128)(2,1)S(1)} fusion(bf16[1024,1024]{1,0:T(8,128)(2,1)} %get-tuple-element.53, bf16[1024,2048]{1,0:T(8,128)(2,1)} %all-gather.8.cloned.1.call-done.down_ref), kind=kOutput, calls=%fused_computation.7 | convolution fusion | flops 4297064448 | bytes 10485760 | tf_op jit(solution)/shard_map/dot_general | solution.py:34
  285.3 3.2 constant_dynamic-update-slice_fusion.5
  291.4 2.7 collective-permute-start.37
  294.1 6.3 %convolution_convert_fusion.2 = bf16[1024,2048]{1,0:T(8,128)(2,1)} fusion(bf16[1024,1024]{1,0:T(8,128)(2,1)S(1)} %copy-done.57, bf16[1024,2048]{1,0:T(8,128)(2,1)S(1)} %constant_dynamic-update-slice_fusion.5), kind=kOutput, calls=%fused_computation.6 | convolution fusion | flops 4297064448 | bytes 10485760 | tf_op jit(solution)/shard_map/dot_general | solution.py:34
  300.4 27.7 %reduce-scatter.5.cloned.1.call-done = bf16[512,1024]{1,0:T(8,128)(2,1)} async-done(((bf16[2048,1024]{1,0:T(8,128)(2,1)}), bf16[512,1024]{1,0:T(8,128)(2,1)}) %reduce-scatter.5.cloned.1.call-update) | async-done | bytes 1048592 | tf_op jit(solution)/shard_map/reduce_scatter | solution.py:144
  328.2 2.8 convert_add_fusion.3.in_ref
  331.1 4.4 add_convert_fusion.1
  335.5 2.3 pick_blocks.3
  346.9 13.6 %collective-permute-start.38 = (bf16[128,2048]{1,0:T(8,128)(2,1)S(1)}, bf16[128,2048]{1,0:T(8,128)(2,1)S(1)}, u32[]{:S(2)}, u32[]{:S(2)}) collective-permute-start(bf16[128,2048]{1,0:T(8,128)(2,1)S(1)} %get-tuple-element.98), channel_id=1, source_target_pairs={{0,4},{12,8},{1,5},{13,9},{2,6},{14,10},{3,7},{15,11},{16,20},{28,... | collective-permute-start | bytes 1572872 | tf_op jit(solution)/shard_map/ppermute | solution.py:164
  361.4 6.8 %collective-permute-done.42 = bf16[128,2048]{1,0:T(8,128)(2,1)S(1)} collective-permute-done((bf16[128,2048]{1,0:T(8,128)(2,1)S(1)}, bf16[128,2048]{1,0:T(8,128)(2,1)S(1)}, u32[]{:S(2)}, u32[]{:S(2)}) %collective-permute-start.42) | collective-permute-done | bytes 524320 | tf_op jit(solution)/shard_map/ppermute | solution.py:64
  370.0 15.5 %collective-permute-done.44 = bf16[128,2048]{1,0:T(8,128)(2,1)S(1)} collective-permute-done((bf16[128,2048]{1,0:T(8,128)(2,1)S(1)}, bf16[128,2048]{1,0:T(8,128)(2,1)S(1)}, u32[]{:S(2)}, u32[]{:S(2)}) %collective-permute-start.44) | collective-permute-done | bytes 524320 | tf_op jit(solution)/shard_map/ppermute | solution.py:64
  386.9 4.0 collective-permute-done.45
  393.4 10.9 %attention_grad.1 = (bf16[2,2,2,2,64,256]{5,4,3,2,1,0:T(8,128)(2,1)}, bf16[2,2,2,4,2,64,256]{6,5,4,3,2,1,0:T(8,128)(2,1)}) custom-call(bf16[2,2,2,2,64,256]{5,4,3,2,1,0:T(8,128)(2,1)} %bitcast.238, bf16[2,2,2,2,64,256]{5,4,3,2,1,0:T(8,128)(2,1)} %bitcast.240, bf16[2,2,2,4,2,64,256]{6,5,4,3,2,1,0:T(8,128)(2,1)} %pad_maximum_fusion.1.kv_ref, ...), custom_call_target="tpu_custom_call" | custom-call | flops 2097152 | bytes 262144 | tf_op jit(solution)/shard_map/attention_grad/pallas_call | solution.py:429
  405.8 4.8 convolution_convert_fusion
  411.9 2.8 convert_element_type.325
  414.7 3.3 slice.170
  418.4 4.6 all-to-all-start.2
  424.7 2.9 collective-permute-start.41
  432.7 2.4 collective-permute-start.53
  435.1 3.0 add_convert_fusion
  442.0 6.0 %collective-permute-done.53 = bf16[4,2,64,256]{3,2,1,0:T(8,128)(2,1)S(1)} collective-permute-done((bf16[4,2,64,256]{3,2,1,0:T(8,128)(2,1)S(1)}, bf16[4,2,64,256]{3,2,1,0:T(8,128)(2,1)S(1)}, u32[]{:S(2)}, u32[]{:S(2)}) %collective-permute-start.53) | collective-permute-done | bytes 262176 | tf_op jit(solution)/shard_map/ppermute | solution.py:64
  449.6 11.8 %all-to-all-done.2.in_ref = bf16[8,64,1024]{2,1,0:T(8,128)(2,1)} async-done(((bf16[8,64,1024]{2,1,0:T(8,128)(2,1)}), bf16[8,64,1024]{2,1,0:T(8,128)(2,1)}, u32[]{:S(2)}, u32[]{:S(2)}) %all-to-all-start.2) | async-done | bytes 1048608 | tf_op jit(solution)/shard_map/all_to_all | solution.py:52
  461.4 4.6 convolution_convert_fusion.7
  466.1 2.8 collective-permute-done.50
  470.7 3.6 convolution_convert_fusion.6
  478.1 4.0 collective-permute-done.54
  482.1 8.4 %collective-permute-done.55 = bf16[2,64,256]{2,1,0:T(8,128)(2,1)S(1)} collective-permute-done((bf16[2,64,256]{2,1,0:T(8,128)(2,1)S(1)}, bf16[2,64,256]{2,1,0:T(8,128)(2,1)S(1)}, u32[]{:S(2)}, u32[]{:S(2)}) %collective-permute-start.55) | collective-permute-done | bytes 65568 | tf_op jit(solution)/shard_map/ppermute | solution.py:160
  498.3 2.7 pad_maximum_fusion.5
  501.1 4.3 all-to-all-start.3
  507.8 2.8 add_convert_fusion.4
  510.6 2.8 collect_units.1
  513.3 12.1 %all-to-all-done.3 = bf16[8,384,256]{2,1,0:T(8,128)(2,1)} async-done(((bf16[8,384,256]{2,1,0:T(8,128)(2,1)}), bf16[8,384,256]{2,1,0:T(8,128)(2,1)}, u32[]{:S(2)}, u32[]{:S(2)}) %all-to-all-start.3) | async-done | bytes 1572896 | tf_op jit(solution)/shard_map/all_to_all | solution.py:52
  525.4 2.2 slice_reduce_fusion
  527.7 3.3 all-to-all-start.4
  (395 shorter events, 143.9 us)
Async XLA Ops:
  7.2 67.0 %all-gather.4.cloned.1.call-start = ((), (), s32[]{:S(2)}) async-start(), calls=%async_computation.9 | async-start | bytes 1310720 | tf_op jit(solution)/shard_map/all_gather | solution.py:509
  11.7 16.9 %collective-permute-start.1 = (bf16[80,256]{1,0:T(8,128)(2,1)S(1)}, bf16[80,256]{1,0:T(8,128)(2,1)S(1)}, u32[]{:S(2)}, u32[]{:S(2)}) collective-permute-start(bf16[80,256]{1,0:T(8,128)(2,1)S(1)} %concatenate.63), channel_id=1, source_target_pairs={{0,8},{4,12},{8,0},{12,4},{1,9},{5,13},{9,1},{13,5},{2,10},{6,14},... | collective-permute-start | bytes 122888 | tf_op jit(solution)/shard_map/ppermute | solution.py:160
  15.8 12.8 %collective-permute-start.2 = (bf16[80,256]{1,0:T(8,128)(2,1)S(1)}, bf16[80,256]{1,0:T(8,128)(2,1)S(1)}, u32[]{:S(2)}, u32[]{:S(2)}) collective-permute-start(bf16[80,256]{1,0:T(8,128)(2,1)S(1)} %concatenate.63), channel_id=1, source_target_pairs={{0,12},{4,0},{8,4},{12,8},{1,13},{5,1},{9,5},{13,9},{2,14},{6,2},{... | collective-permute-start | bytes 122888 | tf_op jit(solution)/shard_map/ppermute | solution.py:160
  17.1 11.4 %collective-permute-start = (bf16[80,256]{1,0:T(8,128)(2,1)S(1)}, bf16[80,256]{1,0:T(8,128)(2,1)S(1)}, u32[]{:S(2)}, u32[]{:S(2)}) collective-permute-start(bf16[80,256]{1,0:T(8,128)(2,1)S(1)} %concatenate.63), channel_id=1, source_target_pairs={{0,4},{4,8},{8,12},{12,0},{1,5},{5,9},{9,13},{13,1},{2,6},{6,10},{... | collective-permute-start | bytes 122888 | tf_op jit(solution)/shard_map/ppermute | solution.py:160
  17.8 28.7 %collective-permute-start.10 = (bf16[128,2048]{1,0:T(8,128)(2,1)}, bf16[128,2048]{1,0:T(8,128)(2,1)S(1)}, u32[]{:S(2)}, u32[]{:S(2)}) collective-permute-start(bf16[128,2048]{1,0:T(8,128)(2,1)} %bitcast.198), channel_id=1, source_target_pairs={{0,2},{2,0},{16,18},{18,16},{1,3},{3,1},{17,19},{19,17},{4,6},{6,4... | collective-permute-start | bytes 1572872 | tf_op jit(solution)/shard_map/ppermute | solution.py:64
  19.3 27.2 %collective-permute-start.11 = (bf16[128,2048]{1,0:T(8,128)(2,1)}, bf16[128,2048]{1,0:T(8,128)(2,1)}, u32[]{:S(2)}, u32[]{:S(2)}) collective-permute-start(bf16[128,2048]{1,0:T(8,128)(2,1)} %bitcast.199), channel_id=1, source_target_pairs={{0,16},{2,18},{16,0},{18,2},{1,17},{3,19},{17,1},{19,3},{4,20},{6,... | collective-permute-start | bytes 1572872 | tf_op jit(solution)/shard_map/ppermute | solution.py:64
  23.1 42.4 %all-to-all-start = ((bf16[8,64,1024]{2,1,0:T(8,128)(2,1)}), bf16[8,64,1024]{2,1,0:T(8,128)(2,1)S(1)}, u32[]{:S(2)}, u32[]{:S(2)}) async-start(bf16[8,64,1024]{2,1,0:T(8,128)(2,1)} %spread_units.1), calls=%async_computation | async-start | bytes 2097152 | tf_op jit(solution)/shard_map/all_to_all | solution.py:52
  27.6 208.7 %all-gather.8.cloned.1.call-start = ((), (), s32[]{:S(2)}) async-start(), calls=%async_computation.11 | async-start | bytes 5242880 | tf_op jit(solution)/shard_map/all_gather | solution.py:521
  28.7 6.7 %collective-permute-start.3 = (bf16[4,80,256]{2,1,0:T(8,128)(2,1)S(1)}, bf16[4,80,256]{2,1,0:T(8,128)(2,1)S(1)}, u32[]{:S(2)}, u32[]{:S(2)}) collective-permute-start(bf16[4,80,256]{2,1,0:T(8,128)(2,1)S(1)} %get-tuple-element.122), channel_id=1, source_target_pairs={{0,2},{2,0},{16,18},{18,16},{1,3},{3,1},{17,19},{19,17},{4,6},{6,4... | collective-permute-start | bytes 491528 | tf_op jit(solution)/shard_map/ppermute | solution.py:64
  29.3 7.5 %collective-permute-start.4 = (bf16[4,80,256]{2,1,0:T(8,128)(2,1)S(1)}, bf16[4,80,256]{2,1,0:T(8,128)(2,1)S(1)}, u32[]{:S(2)}, u32[]{:S(2)}) collective-permute-start(bf16[4,80,256]{2,1,0:T(8,128)(2,1)S(1)} %get-tuple-element.122), channel_id=1, source_target_pairs={{0,16},{2,18},{16,0},{18,2},{1,17},{3,19},{17,1},{19,3},{4,20},{6,... | collective-permute-start | bytes 491528 | tf_op jit(solution)/shard_map/ppermute | solution.py:64
  29.8 10.9 %collective-permute-start.5 = (bf16[4,80,256]{2,1,0:T(8,128)(2,1)S(1)}, bf16[4,80,256]{2,1,0:T(8,128)(2,1)S(1)}, u32[]{:S(2)}, u32[]{:S(2)}) collective-permute-start(bf16[4,80,256]{2,1,0:T(8,128)(2,1)S(1)} %get-tuple-element.122), channel_id=1, source_target_pairs={{0,18},{2,16},{16,2},{18,0},{1,19},{3,17},{17,3},{19,1},{4,22},{6,... | collective-permute-start | bytes 491528 | tf_op jit(solution)/shard_map/ppermute | solution.py:64
  35.4 16.0 %collective-permute-start.12 = (bf16[128,2048]{1,0:T(8,128)(2,1)S(1)}, bf16[128,2048]{1,0:T(8,128)(2,1)}, u32[]{:S(2)}, u32[]{:S(2)}) collective-permute-start(bf16[128,2048]{1,0:T(8,128)(2,1)S(1)} %bitcast.200), channel_id=1, source_target_pairs={{0,18},{2,16},{16,2},{18,0},{1,19},{3,17},{17,3},{19,1},{4,22},{6,... | collective-permute-start | bytes 1572872 | tf_op jit(solution)/shard_map/ppermute | solution.py:64
  41.0 13.1 %collective-permute-start.6 = (bf16[4,4,80,256]{3,2,1,0:T(8,128)(2,1)S(1)}, bf16[4,4,80,256]{3,2,1,0:T(8,128)(2,1)}, u32[]{:S(2)}, u32[]{:S(2)}) collective-permute-start(bf16[4,4,80,256]{3,2,1,0:T(8,128)(2,1)S(1)} %pad_maximum_fusion.11), channel_id=1, source_target_pairs={{0,1},{1,0},{2,3},{3,2},{4,5},{5,4},{6,7},{7,6},{8,9},{9,8},{10,11... | collective-permute-start | bytes 1966088 | tf_op jit(solution)/shard_map/ppermute | solution.py:38
  54.1 23.8 %collective-permute-start.13 = (bf16[512,2048]{1,0:T(8,128)(2,1)}, bf16[512,2048]{1,0:T(8,128)(2,1)}, u32[]{:S(2)}, u32[]{:S(2)}) collective-permute-start(bf16[512,2048]{1,0:T(8,128)(2,1)} %pad_maximum_fusion.near_ref), channel_id=1, source_target_pairs={{0,1},{1,0},{2,3},{3,2},{4,5},{5,4},{6,7},{7,6},{8,9},{9,8},{10,11... | collective-permute-start | bytes 6291464 | tf_op jit(solution)/shard_map/ppermute | solution.py:38
  59.4 16.8 %collective-permute-start.7 = (bf16[2,64,256]{2,1,0:T(8,128)(2,1)S(1)}, bf16[2,64,256]{2,1,0:T(8,128)(2,1)S(1)}, u32[]{:S(2)}, u32[]{:S(2)}) collective-permute-start(bf16[2,64,256]{2,1,0:T(8,128)(2,1)S(1)} %bitcast.242), channel_id=1, source_target_pairs={{0,4},{4,8},{8,12},{12,0},{1,5},{5,9},{9,13},{13,1},{2,6},{6,10},{... | collective-permute-start | bytes 196616 | tf_op jit(solution)/shard_map/ppermute | solution.py:160
  61.1 15.1 %collective-permute-start.8 = (bf16[2,64,256]{2,1,0:T(8,128)(2,1)S(1)}, bf16[2,64,256]{2,1,0:T(8,128)(2,1)S(1)}, u32[]{:S(2)}, u32[]{:S(2)}) collective-permute-start(bf16[2,64,256]{2,1,0:T(8,128)(2,1)S(1)} %bitcast.243), channel_id=1, source_target_pairs={{0,8},{4,12},{8,0},{12,4},{1,9},{5,13},{9,1},{13,5},{2,10},{6,14},... | collective-permute-start | bytes 196616 | tf_op jit(solution)/shard_map/ppermute | solution.py:160
  63.5 12.7 %collective-permute-start.9 = (bf16[2,64,256]{2,1,0:T(8,128)(2,1)S(1)}, bf16[2,64,256]{2,1,0:T(8,128)(2,1)S(1)}, u32[]{:S(2)}, u32[]{:S(2)}) collective-permute-start(bf16[2,64,256]{2,1,0:T(8,128)(2,1)S(1)} %bitcast.244), channel_id=1, source_target_pairs={{0,12},{4,0},{8,4},{12,8},{1,13},{5,1},{9,5},{13,9},{2,14},{6,2},{... | collective-permute-start | bytes 196616 | tf_op jit(solution)/shard_map/ppermute | solution.py:160
  66.5 48.4 %all-to-all-start.1 = ((bf16[32,64,256]{2,1,0:T(8,128)(2,1)}), bf16[32,64,256]{2,1,0:T(8,128)(2,1)S(1)}, u32[]{:S(2)}, u32[]{:S(2)}) async-start(bf16[32,64,256]{2,1,0:T(8,128)(2,1)} %spread_heads.1), calls=%async_computation.1 | async-start | bytes 2097152 | tf_op jit(solution)/shard_map/all_to_all | solution.py:52
  69.2 167.1 %all-gather.6.cloned.1.call-start = ((), (), s32[]{:S(2)}) async-start(), calls=%async_computation.10 | async-start | bytes 5242880 | tf_op jit(solution)/shard_map/all_gather | solution.py:520
  76.1 36.4 %collective-permute-start.18 = (bf16[2,64,2048]{2,1,0:T(8,128)(2,1)}, bf16[2,64,2048]{2,1,0:T(8,128)(2,1)}, u32[]{:S(2)}, u32[]{:S(2)}) collective-permute-start(bf16[2,64,2048]{2,1,0:T(8,128)(2,1)} %dynamic-slice_bitcast_fusion.1), channel_id=1, source_target_pairs={{0,1},{1,0},{2,3},{3,2},{4,5},{5,4},{6,7},{7,6},{8,9},{9,8},{10,11... | collective-permute-start | bytes 1572872 | tf_op jit(solution)/shard_map/ppermute | solution.py:38
  86.0 11.7 %collective-permute-start.14 = (bf16[4,2,64,256]{3,2,1,0:T(8,128)(2,1)S(1)}, bf16[4,2,64,256]{3,2,1,0:T(8,128)(2,1)S(1)}, u32[]{:S(2)}, u32[]{:S(2)}) collective-permute-start(bf16[4,2,64,256]{3,2,1,0:T(8,128)(2,1)S(1)} %pad_maximum_fusion.12), channel_id=1, source_target_pairs={{0,2},{2,0},{16,18},{18,16},{1,3},{3,1},{17,19},{19,17},{4,6},{6,4... | collective-permute-start | bytes 786440 | tf_op jit(solution)/shard_map/ppermute | solution.py:64
  87.7 13.1 %collective-permute-start.15 = (bf16[4,2,64,256]{3,2,1,0:T(8,128)(2,1)S(1)}, bf16[4,2,64,256]{3,2,1,0:T(8,128)(2,1)S(1)}, u32[]{:S(2)}, u32[]{:S(2)}) collective-permute-start(bf16[4,2,64,256]{3,2,1,0:T(8,128)(2,1)S(1)} %pad_maximum_fusion.12), channel_id=1, source_target_pairs={{0,16},{2,18},{16,0},{18,2},{1,17},{3,19},{17,1},{19,3},{4,20},{6,... | collective-permute-start | bytes 786440 | tf_op jit(solution)/shard_map/ppermute | solution.py:64
  89.2 22.2 %collective-permute-start.16 = (bf16[4,2,64,256]{3,2,1,0:T(8,128)(2,1)S(1)}, bf16[4,2,64,256]{3,2,1,0:T(8,128)(2,1)S(1)}, u32[]{:S(2)}, u32[]{:S(2)}) collective-permute-start(bf16[4,2,64,256]{3,2,1,0:T(8,128)(2,1)S(1)} %pad_maximum_fusion.12), channel_id=1, source_target_pairs={{0,18},{2,16},{16,2},{18,0},{1,19},{3,17},{17,3},{19,1},{4,22},{6,... | collective-permute-start | bytes 786440 | tf_op jit(solution)/shard_map/ppermute | solution.py:64
  112.5 7.0 %collective-permute-start.17 = (bf16[4,4,2,64,256]{4,3,2,1,0:T(8,128)(2,1)}, bf16[4,4,2,64,256]{4,3,2,1,0:T(8,128)(2,1)}, u32[]{:S(2)}, u32[]{:S(2)}) collective-permute-start(bf16[4,4,2,64,256]{4,3,2,1,0:T(8,128)(2,1)} %pad_maximum_fusion.7), channel_id=1, source_target_pairs={{0,1},{1,0},{2,3},{3,2},{4,5},{5,4},{6,7},{7,6},{8,9},{9,8},{10,11... | collective-permute-start | bytes 3145736 | tf_op jit(solution)/shard_map/ppermute | solution.py:38
  139.3 188.8 %reduce-scatter.5.cloned.1.call-start = ((), (), s32[]{:S(2)}) async-start(), calls=%async_computation.12 | async-start | bytes 5242880 | tf_op jit(solution)/shard_map/reduce_scatter | solution.py:144
  139.8 28.0 %collective-permute-start.28 = (bf16[128,2048]{1,0:T(8,128)(2,1)S(1)}, bf16[128,2048]{1,0:T(8,128)(2,1)S(1)}, u32[]{:S(2)}, u32[]{:S(2)}) collective-permute-start(bf16[128,2048]{1,0:T(8,128)(2,1)S(1)} %bitcast.202), channel_id=1, source_target_pairs={{0,4},{4,0},{8,12},{12,8},{1,5},{5,1},{9,13},{13,9},{2,6},{6,2},{1... | collective-permute-start | bytes 1572872 | tf_op jit(solution)/shard_map/ppermute | solution.py:164
  140.4 25.8 %collective-permute-start.29 = (bf16[128,2048]{1,0:T(8,128)(2,1)S(1)}, bf16[128,2048]{1,0:T(8,128)(2,1)}, u32[]{:S(2)}, u32[]{:S(2)}) collective-permute-start(bf16[128,2048]{1,0:T(8,128)(2,1)S(1)} %bitcast.203), channel_id=1, source_target_pairs={{0,8},{8,0},{4,12},{12,4},{1,9},{9,1},{5,13},{13,5},{2,10},{10,2},... | collective-permute-start | bytes 1572872 | tf_op jit(solution)/shard_map/ppermute | solution.py:164
  146.3 24.5 %collective-permute-start.20 = (bf16[128,2048]{1,0:T(8,128)(2,1)S(1)}, bf16[128,2048]{1,0:T(8,128)(2,1)S(1)}, u32[]{:S(2)}, u32[]{:S(2)}) collective-permute-start(bf16[128,2048]{1,0:T(8,128)(2,1)S(1)} %get-tuple-element.102), channel_id=1, source_target_pairs={{0,2},{2,0},{16,18},{18,16},{1,3},{3,1},{17,19},{19,17},{4,6},{6,4... | collective-permute-start | bytes 1572872 | tf_op jit(solution)/shard_map/ppermute | solution.py:64
  147.8 25.2 %collective-permute-start.21 = (bf16[128,2048]{1,0:T(8,128)(2,1)S(1)}, bf16[128,2048]{1,0:T(8,128)(2,1)S(1)}, u32[]{:S(2)}, u32[]{:S(2)}) collective-permute-start(bf16[128,2048]{1,0:T(8,128)(2,1)S(1)} %get-tuple-element.104), channel_id=1, source_target_pairs={{0,16},{2,18},{16,0},{18,2},{1,17},{3,19},{17,1},{19,3},{4,20},{6,... | collective-permute-start | bytes 1572872 | tf_op jit(solution)/shard_map/ppermute | solution.py:64
  150.1 34.8 %collective-permute-start.22 = (bf16[128,2048]{1,0:T(8,128)(2,1)S(1)}, bf16[128,2048]{1,0:T(8,128)(2,1)S(1)}, u32[]{:S(2)}, u32[]{:S(2)}) collective-permute-start(bf16[128,2048]{1,0:T(8,128)(2,1)S(1)} %get-tuple-element.103), channel_id=1, source_target_pairs={{0,18},{2,16},{16,2},{18,0},{1,19},{3,17},{17,3},{19,1},{4,22},{6,... | collective-permute-start | bytes 1572872 | tf_op jit(solution)/shard_map/ppermute | solution.py:64
  166.2 24.7 %collective-permute-start.30 = (bf16[128,2048]{1,0:T(8,128)(2,1)S(1)}, bf16[128,2048]{1,0:T(8,128)(2,1)}, u32[]{:S(2)}, u32[]{:S(2)}) collective-permute-start(bf16[128,2048]{1,0:T(8,128)(2,1)S(1)} %bitcast.205), channel_id=1, source_target_pairs={{4,8},{8,4},{5,9},{9,5},{6,10},{10,6},{7,11},{11,7},{20,24},{24,20... | collective-permute-start | bytes 1572872 | tf_op jit(solution)/shard_map/ppermute | solution.py:164
  167.7 23.2 %collective-permute-start.31 = (bf16[128,2048]{1,0:T(8,128)(2,1)}, bf16[128,2048]{1,0:T(8,128)(2,1)}, u32[]{:S(2)}, u32[]{:S(2)}) collective-permute-start(bf16[128,2048]{1,0:T(8,128)(2,1)} %collective-permute-done.29), channel_id=1, source_target_pairs={{4,0},{8,12},{5,1},{9,13},{6,2},{10,14},{7,3},{11,15},{20,16},{24,... | collective-permute-start | bytes 1572872 | tf_op jit(solution)/shard_map/ppermute | solution.py:164
  188.9 25.7 %collective-permute-start.24 = (bf16[128,2048]{1,0:T(8,128)(2,1)}, bf16[128,2048]{1,0:T(8,128)(2,1)S(1)}, u32[]{:S(2)}, u32[]{:S(2)}) collective-permute-start(bf16[128,2048]{1,0:T(8,128)(2,1)} %pick_blocks.2), channel_id=1, source_target_pairs={{0,8},{8,0},{4,12},{12,4},{1,9},{9,1},{5,13},{13,5},{2,10},{10,2},... | collective-permute-start | bytes 1572872 | tf_op jit(solution)/shard_map/ppermute | solution.py:164
  189.9 26.7 %collective-permute-start.23 = (bf16[128,2048]{1,0:T(8,128)(2,1)}, bf16[128,2048]{1,0:T(8,128)(2,1)S(1)}, u32[]{:S(2)}, u32[]{:S(2)}) collective-permute-start(bf16[128,2048]{1,0:T(8,128)(2,1)} %pick_blocks.2), channel_id=1, source_target_pairs={{0,4},{4,0},{8,12},{12,8},{1,5},{5,1},{9,13},{13,9},{2,6},{6,2},{1... | collective-permute-start | bytes 1572872 | tf_op jit(solution)/shard_map/ppermute | solution.py:164
  195.9 40.4 %collective-permute-start.32 = (bf16[512,2048]{1,0:T(8,128)(2,1)}, bf16[512,2048]{1,0:T(8,128)(2,1)}, u32[]{:S(2)}, u32[]{:S(2)}) collective-permute-start(bf16[512,2048]{1,0:T(8,128)(2,1)} %pad_maximum_fusion.3.grad_near_ref), channel_id=1, source_target_pairs={{0,1},{1,0},{2,3},{3,2},{4,5},{5,4},{6,7},{7,6},{8,9},{9,8},{10,11... | collective-permute-start | bytes 6291464 | tf_op jit(solution)/shard_map/ppermute | solution.py:38
  215.3 15.7 %collective-permute-start.26 = (bf16[128,2048]{1,0:T(8,128)(2,1)S(1)}, bf16[128,2048]{1,0:T(8,128)(2,1)S(1)}, u32[]{:S(2)}, u32[]{:S(2)}) collective-permute-start(bf16[128,2048]{1,0:T(8,128)(2,1)S(1)} %collective-permute-done.24), channel_id=1, source_target_pairs={{4,0},{8,12},{5,1},{9,13},{6,2},{10,14},{7,3},{11,15},{20,16},{24,... | collective-permute-start | bytes 1572872 | tf_op jit(solution)/shard_map/ppermute | solution.py:164
  276.0 135.9 %reduce-scatter.7.cloned.1.call-start = ((), (), s32[]{:S(2)}) async-start(), calls=%async_computation.13 | async-start | bytes 5242880 | tf_op jit(solution)/shard_map/reduce_scatter | solution.py:144
  285.2 45.9 %collective-permute-start.34 = (bf16[512,2048]{1,0:T(8,128)(2,1)}, bf16[512,2048]{1,0:T(8,128)(2,1)}, u32[]{:S(2)}, u32[]{:S(2)}) collective-permute-start(bf16[512,2048]{1,0:T(8,128)(2,1)} %slice.207), channel_id=1, source_target_pairs={{0,1},{1,0},{2,3},{3,2},{4,5},{5,4},{6,7},{7,6},{8,9},{9,8},{10,11... | collective-permute-start | bytes 6291464 | tf_op jit(solution)/shard_map/ppermute | solution.py:38
  289.7 38.4 %collective-permute-start.35 = (bf16[128,2048]{1,0:T(8,128)(2,1)}, bf16[128,2048]{1,0:T(8,128)(2,1)}, u32[]{:S(2)}, u32[]{:S(2)}) collective-permute-start(bf16[128,2048]{1,0:T(8,128)(2,1)} %get-tuple-element.99), channel_id=1, source_target_pairs={{0,4},{4,0},{8,12},{12,8},{1,5},{5,1},{9,13},{13,9},{2,6},{6,2},{1... | collective-permute-start | bytes 1572872 | tf_op jit(solution)/shard_map/ppermute | solution.py:164
  289.7 38.5 %collective-permute-start.36 = (bf16[128,2048]{1,0:T(8,128)(2,1)}, bf16[128,2048]{1,0:T(8,128)(2,1)}, u32[]{:S(2)}, u32[]{:S(2)}) collective-permute-start(bf16[128,2048]{1,0:T(8,128)(2,1)} %get-tuple-element.101), channel_id=1, source_target_pairs={{0,8},{8,0},{4,12},{12,4},{1,9},{9,1},{5,13},{13,5},{2,10},{10,2},... | collective-permute-start | bytes 1572872 | tf_op jit(solution)/shard_map/ppermute | solution.py:164
  291.4 36.8 %collective-permute-start.37 = (bf16[128,2048]{1,0:T(8,128)(2,1)}, bf16[128,2048]{1,0:T(8,128)(2,1)}, u32[]{:S(2)}, u32[]{:S(2)}) collective-permute-start(bf16[128,2048]{1,0:T(8,128)(2,1)} %get-tuple-element.100), channel_id=1, source_target_pairs={{0,12},{12,0},{4,8},{8,4},{1,13},{13,1},{5,9},{9,5},{2,14},{14,2},... | collective-permute-start | bytes 1572872 | tf_op jit(solution)/shard_map/ppermute | solution.py:164
  342.5 25.7 %collective-permute-start.42 = (bf16[128,2048]{1,0:T(8,128)(2,1)S(1)}, bf16[128,2048]{1,0:T(8,128)(2,1)S(1)}, u32[]{:S(2)}, u32[]{:S(2)}) collective-permute-start(bf16[128,2048]{1,0:T(8,128)(2,1)S(1)} %get-tuple-element.85), channel_id=1, source_target_pairs={{0,2},{2,0},{16,18},{18,16},{1,3},{3,1},{17,19},{19,17},{4,6},{6,4... | collective-permute-start | bytes 1572872 | tf_op jit(solution)/shard_map/ppermute | solution.py:64
  344.0 26.0 %collective-permute-start.43 = (bf16[128,2048]{1,0:T(8,128)(2,1)S(1)}, bf16[128,2048]{1,0:T(8,128)(2,1)S(1)}, u32[]{:S(2)}, u32[]{:S(2)}) collective-permute-start(bf16[128,2048]{1,0:T(8,128)(2,1)S(1)} %get-tuple-element.85), channel_id=1, source_target_pairs={{0,16},{2,18},{16,0},{18,2},{1,17},{3,19},{17,1},{19,3},{4,20},{6,... | collective-permute-start | bytes 1572872 | tf_op jit(solution)/shard_map/ppermute | solution.py:64
  345.1 40.4 %collective-permute-start.44 = (bf16[128,2048]{1,0:T(8,128)(2,1)S(1)}, bf16[128,2048]{1,0:T(8,128)(2,1)S(1)}, u32[]{:S(2)}, u32[]{:S(2)}) collective-permute-start(bf16[128,2048]{1,0:T(8,128)(2,1)S(1)} %get-tuple-element.85), channel_id=1, source_target_pairs={{0,18},{2,16},{16,2},{18,0},{1,19},{3,17},{17,3},{19,1},{4,22},{6,... | collective-permute-start | bytes 1572872 | tf_op jit(solution)/shard_map/ppermute | solution.py:64
  346.9 38.9 %collective-permute-start.38 = (bf16[128,2048]{1,0:T(8,128)(2,1)S(1)}, bf16[128,2048]{1,0:T(8,128)(2,1)S(1)}, u32[]{:S(2)}, u32[]{:S(2)}) collective-permute-start(bf16[128,2048]{1,0:T(8,128)(2,1)S(1)} %get-tuple-element.98), channel_id=1, source_target_pairs={{0,4},{12,8},{1,5},{13,9},{2,6},{14,10},{3,7},{15,11},{16,20},{28,... | collective-permute-start | bytes 1572872 | tf_op jit(solution)/shard_map/ppermute | solution.py:164
  360.5 26.2 %collective-permute-start.40 = (bf16[128,2048]{1,0:T(8,128)(2,1)S(1)}, bf16[128,2048]{1,0:T(8,128)(2,1)S(1)}, u32[]{:S(2)}, u32[]{:S(2)}) collective-permute-start(bf16[128,2048]{1,0:T(8,128)(2,1)S(1)} %get-tuple-element.98), channel_id=1, source_target_pairs={{4,8},{8,4},{5,9},{9,5},{6,10},{10,6},{7,11},{11,7},{20,24},{24,20... | collective-permute-start | bytes 1572872 | tf_op jit(solution)/shard_map/ppermute | solution.py:164
  418.0 14.7 %collective-permute-start.47 = (bf16[512,2048]{1,0:T(8,128)(2,1)}, bf16[512,2048]{1,0:T(8,128)(2,1)}, u32[]{:S(2)}, u32[]{:S(2)}) collective-permute-start(bf16[512,2048]{1,0:T(8,128)(2,1)} %slice.170), channel_id=1, source_target_pairs={{0,1},{1,0},{2,3},{3,2},{4,5},{5,4},{6,7},{7,6},{8,9},{9,8},{10,11... | collective-permute-start | bytes 6291464 | tf_op jit(solution)/shard_map/ppermute | solution.py:38
  418.4 43.0 %all-to-all-start.2 = ((bf16[8,64,1024]{2,1,0:T(8,128)(2,1)}), bf16[8,64,1024]{2,1,0:T(8,128)(2,1)}, u32[]{:S(2)}, u32[]{:S(2)}) async-start(bf16[8,64,1024]{2,1,0:T(8,128)(2,1)} %bitcast.224), calls=%async_computation.4 | async-start | bytes 2097152 | tf_op jit(solution)/shard_map/all_to_all | solution.py:52
  423.0 75.3 %reduce-scatter.9.cloned.1.call-start = ((), (), s32[]{:S(2)}) async-start(), calls=%async_computation.14 | async-start | bytes 1310720 | tf_op jit(solution)/shard_map/reduce_scatter | solution.py:623
  424.7 49.6 %collective-permute-start.41 = (bf16[128,2048]{1,0:T(8,128)(2,1)}, bf16[128,2048]{1,0:T(8,128)(2,1)}, u32[]{:S(2)}, u32[]{:S(2)}) collective-permute-start(bf16[128,2048]{1,0:T(8,128)(2,1)} %add_convert_fusion.5), channel_id=1, source_target_pairs={{0,8},{8,0},{4,12},{12,4},{1,9},{9,1},{5,13},{13,5},{2,10},{10,2},... | collective-permute-start | bytes 1572872 | tf_op jit(solution)/shard_map/ppermute | solution.py:164
  427.6 46.8 %collective-permute-start.39 = (bf16[128,2048]{1,0:T(8,128)(2,1)}, bf16[128,2048]{1,0:T(8,128)(2,1)}, u32[]{:S(2)}, u32[]{:S(2)}) collective-permute-start(bf16[128,2048]{1,0:T(8,128)(2,1)} %get-tuple-element.56), channel_id=1, source_target_pairs={{0,4},{4,0},{8,12},{12,8},{1,5},{5,1},{9,13},{13,9},{2,6},{6,2},{1... | collective-permute-start | bytes 1572872 | tf_op jit(solution)/shard_map/ppermute | solution.py:164
  431.6 9.1 %collective-permute-start.51 = (bf16[4,2,64,256]{3,2,1,0:T(8,128)(2,1)S(1)}, bf16[4,2,64,256]{3,2,1,0:T(8,128)(2,1)S(1)}, u32[]{:S(2)}, u32[]{:S(2)}) collective-permute-start(bf16[4,2,64,256]{3,2,1,0:T(8,128)(2,1)S(1)} %get-tuple-element.111), channel_id=1, source_target_pairs={{0,2},{2,0},{16,18},{18,16},{1,3},{3,1},{17,19},{19,17},{4,6},{6,4... | collective-permute-start | bytes 786440 | tf_op jit(solution)/shard_map/ppermute | solution.py:64
  432.2 9.2 %collective-permute-start.52 = (bf16[4,2,64,256]{3,2,1,0:T(8,128)(2,1)S(1)}, bf16[4,2,64,256]{3,2,1,0:T(8,128)(2,1)S(1)}, u32[]{:S(2)}, u32[]{:S(2)}) collective-permute-start(bf16[4,2,64,256]{3,2,1,0:T(8,128)(2,1)S(1)} %get-tuple-element.113), channel_id=1, source_target_pairs={{0,16},{2,18},{16,0},{18,2},{1,17},{3,19},{17,1},{19,3},{4,20},{6,... | collective-permute-start | bytes 786440 | tf_op jit(solution)/shard_map/ppermute | solution.py:64
  432.7 15.2 %collective-permute-start.53 = (bf16[4,2,64,256]{3,2,1,0:T(8,128)(2,1)S(1)}, bf16[4,2,64,256]{3,2,1,0:T(8,128)(2,1)S(1)}, u32[]{:S(2)}, u32[]{:S(2)}) collective-permute-start(bf16[4,2,64,256]{3,2,1,0:T(8,128)(2,1)S(1)} %get-tuple-element.112), channel_id=1, source_target_pairs={{0,18},{2,16},{16,2},{18,0},{1,19},{3,17},{17,3},{19,1},{4,22},{6,... | collective-permute-start | bytes 786440 | tf_op jit(solution)/shard_map/ppermute | solution.py:64
  440.6 25.4 %collective-permute-start.48 = (bf16[128,2048]{1,0:T(8,128)(2,1)}, bf16[128,2048]{1,0:T(8,128)(2,1)}, u32[]{:S(2)}, u32[]{:S(2)}) collective-permute-start(bf16[128,2048]{1,0:T(8,128)(2,1)} %get-tuple-element.94), channel_id=1, source_target_pairs={{0,2},{2,0},{16,18},{18,16},{1,3},{3,1},{17,19},{19,17},{4,6},{6,4... | collective-permute-start | bytes 1572872 | tf_op jit(solution)/shard_map/ppermute | solution.py:64
  441.4 24.7 %collective-permute-start.49 = (bf16[128,2048]{1,0:T(8,128)(2,1)}, bf16[128,2048]{1,0:T(8,128)(2,1)}, u32[]{:S(2)}, u32[]{:S(2)}) collective-permute-start(bf16[128,2048]{1,0:T(8,128)(2,1)} %get-tuple-element.96), channel_id=1, source_target_pairs={{0,16},{2,18},{16,0},{18,2},{1,17},{3,19},{17,1},{19,3},{4,20},{6,... | collective-permute-start | bytes 1572872 | tf_op jit(solution)/shard_map/ppermute | solution.py:64
  448.0 20.9 %collective-permute-start.50 = (bf16[128,2048]{1,0:T(8,128)(2,1)}, bf16[128,2048]{1,0:T(8,128)(2,1)}, u32[]{:S(2)}, u32[]{:S(2)}) collective-permute-start(bf16[128,2048]{1,0:T(8,128)(2,1)} %get-tuple-element.95), channel_id=1, source_target_pairs={{0,18},{2,16},{16,2},{18,0},{1,19},{3,17},{17,3},{19,1},{4,22},{6,... | collective-permute-start | bytes 1572872 | tf_op jit(solution)/shard_map/ppermute | solution.py:64
  474.4 7.7 %collective-permute-start.54 = (bf16[2,64,256]{2,1,0:T(8,128)(2,1)S(1)}, bf16[2,64,256]{2,1,0:T(8,128)(2,1)S(1)}, u32[]{:S(2)}, u32[]{:S(2)}) collective-permute-start(bf16[2,64,256]{2,1,0:T(8,128)(2,1)S(1)} %get-tuple-element.118), channel_id=1, source_target_pairs={{0,12},{4,0},{8,4},{12,8},{1,13},{5,1},{9,5},{13,9},{2,14},{6,2},{... | collective-permute-start | bytes 196616 | tf_op jit(solution)/shard_map/ppermute | solution.py:160
  475.0 15.6 %collective-permute-start.55 = (bf16[2,64,256]{2,1,0:T(8,128)(2,1)S(1)}, bf16[2,64,256]{2,1,0:T(8,128)(2,1)S(1)}, u32[]{:S(2)}, u32[]{:S(2)}) collective-permute-start(bf16[2,64,256]{2,1,0:T(8,128)(2,1)S(1)} %get-tuple-element.120), channel_id=1, source_target_pairs={{0,8},{4,12},{8,0},{12,4},{1,9},{5,13},{9,1},{13,5},{2,10},{6,14},... | collective-permute-start | bytes 196616 | tf_op jit(solution)/shard_map/ppermute | solution.py:160
  476.6 13.9 %collective-permute-start.56 = (bf16[2,64,256]{2,1,0:T(8,128)(2,1)S(1)}, bf16[2,64,256]{2,1,0:T(8,128)(2,1)S(1)}, u32[]{:S(2)}, u32[]{:S(2)}) collective-permute-start(bf16[2,64,256]{2,1,0:T(8,128)(2,1)S(1)} %get-tuple-element.119), channel_id=1, source_target_pairs={{0,4},{4,8},{8,12},{12,0},{1,5},{5,9},{9,13},{13,1},{2,6},{6,10},{... | collective-permute-start | bytes 196616 | tf_op jit(solution)/shard_map/ppermute | solution.py:160
  478.1 27.3 %collective-permute-start.57 = (bf16[2,64,2048]{2,1,0:T(8,128)(2,1)}, bf16[2,64,2048]{2,1,0:T(8,128)(2,1)}, u32[]{:S(2)}, u32[]{:S(2)}) collective-permute-start(bf16[2,64,2048]{2,1,0:T(8,128)(2,1)} %dynamic-slice_bitcast_fusion), channel_id=1, source_target_pairs={{0,1},{1,0},{2,3},{3,2},{4,5},{5,4},{6,7},{7,6},{8,9},{9,8},{10,11... | collective-permute-start | bytes 1572872 | tf_op jit(solution)/shard_map/ppermute | solution.py:38
  501.1 24.4 %all-to-all-start.3 = ((bf16[8,384,256]{2,1,0:T(8,128)(2,1)}), bf16[8,384,256]{2,1,0:T(8,128)(2,1)}, u32[]{:S(2)}, u32[]{:S(2)}) async-start(bf16[8,384,256]{2,1,0:T(8,128)(2,1)} %pad_maximum_fusion.5), calls=%async_computation.6 | async-start | bytes 3145728 | tf_op jit(solution)/shard_map/all_to_all | solution.py:52
  505.4 34.3 %reduce-scatter.11.cloned.1.call-start = ((), (), s32[]{:S(2)}) async-start(), calls=%async_computation.15 | async-start | bytes 1310720 | tf_op jit(solution)/shard_map/reduce_scatter | solution.py:636
  527.7 9.8 %all-to-all-start.4 = ((bf16[4,80,256]{2,1,0:T(8,128)(2,1)}), bf16[4,80,256]{2,1,0:T(8,128)(2,1)S(1)}, u32[]{:S(2)}, u32[]{:S(2)}) async-start(bf16[4,80,256]{2,1,0:T(8,128)(2,1)} %bitcast.81), calls=%async_computation.7 | async-start | bytes 327680 | tf_op jit(solution)/shard_map/all_to_all | solution.py:52
  (65 other events, 633.0 us)
Sparse Core Ops, SparseCore 0:
  9.6 39.6 all-gather.3
  51.1 74.9 all-gather.7
  139.4 72.7 all-gather.5
  276.1 51.8 reduce-scatter.4
  331.1 72.2 reduce-scatter.6
  466.2 27.9 reduce-scatter.8
  508.6 25.6 reduce-scatter.10
